TPU v7x, 128 devices: a whole 4x4x4 slice. The times are simulated.
128 devices in a mesh: layer: 4 (over z_hi, core), row: 4 (over x), col: 8 (over y, z_lo).
Axes of the slice: x: 4, y: 4, z: 4 (z_hi: 2, z_lo: 2; z = z_hi * 2 + z_lo), core: 2. Of those that a mesh axis runs over, the one named last changes fastest.
Arguments:
- traces_rows: bfloat16 [64, 2048, 4096], P(None, 'row', ('layer', 'col')), may hold values from -6 to 6
- traces_cols: bfloat16 [64, 2048, 4096], P(None, 'col', ('layer', 'row')), may hold values from -6 to 6
- offsets_rows: int32 [2048], P('row'), may hold values from 0 to 16
- offsets_cols: int32 [2048], P('col'), may hold values from 0 to 16
- bins: int32 [8], replicated, may hold values from 1 to 511
Outputs:
- c3: float32 [8, 2, 2048, 2048], P('layer', None, 'row', 'col')
Inputs may be any that keep to these rules, and one draw needn't show every extreme that they name: `bins`: bin indices, not necessarily distinct.
All inputs are finite; a program needn't handle non-finite values.
Results may differ from a plain program's by a relative error of at most 0.0054.
Values may be sent and summed in bfloat16 or wider, within the bound.
No kernel may reach another device: no remote copies, remote signals or barrier semaphores. Data moves between devices by JAX's collectives and lax.ppermute only.
A program may use at most 192 MiB of HBM per device.

v0:
```python
import math

import jax
import jax.numpy as jnp
from jax import lax
from jax.sharding import PartitionSpec as P

NFFT = 1024
SAMPLES = 64
WINDOW = 48
K_AUX = 4096


def make_basis(offsets, bins):
    tick = jnp.arange(SAMPLES, dtype=jnp.int32)
    lag = tick[:, None] - offsets[None, :]
    inside = (lag >= 0) & (lag < WINDOW)
    lagf = lag.astype(jnp.float32)
    taper = 0.5 - 0.5 * jnp.cos(2.0 * math.pi * (lagf + 0.5) / WINDOW)
    clipped = jnp.clip(lag, 0, WINDOW - 1)
    phase_int = bins[None, :, None] * clipped[:, None, :] % NFFT
    angle = 2.0 * math.pi * phase_int.astype(jnp.float32) / NFFT
    weight = jnp.where(inside, taper, 0.0)[:, None, :]
    real = weight * jnp.cos(angle)
    imag = -weight * jnp.sin(angle)
    return jnp.stack([real, imag], axis=2).astype(jnp.bfloat16)


def spectra(traces, offsets, bins):
    basis = make_basis(offsets, bins)
    result = jnp.einsum("tnk,tfpn->fnpk", traces, basis, preferred_element_type=jnp.float32)
    return result.astype(jnp.bfloat16)


def paired(piece):
    real = piece[..., 0, :]
    imag = piece[..., 1, :]
    second = jnp.stack([imag, -real], axis=-2)
    return jnp.stack([piece, second], axis=-4)


def local(traces_rows, traces_cols, offsets_rows, offsets_cols, bins):
    spec_rows = spectra(traces_rows, offsets_rows, bins)
    spec_cols = spectra(traces_cols, offsets_cols, bins)
    panel_cols = lax.all_gather(spec_cols, "row", axis=3, tiled=True)
    partial_term = jnp.einsum(
        "fcipk,fjpk->fcij",
        paired(lax.all_gather(spec_rows, "col", axis=3, tiled=True)),
        panel_cols,
        preferred_element_type=jnp.float32,
    )
    summed = lax.psum_scatter(partial_term, "layer", scatter_dimension=0, tiled=True)
    return summed * (1.0 / K_AUX)


def solution(mesh):
    return jax.shard_map(
        local,
        mesh=mesh,
        in_specs=(
            P(None, "row", ("layer", "col")),
            P(None, "col", ("layer", "row")),
            P("row"),
            P("col"),
            P(),
        ),
        out_specs=P("layer", None, "row", "col"),
        check_vma=False,
    )
```

profile of v0, /device:TPU:1, one launch (start us, length us, event | category | flops | bytes accessed | tf_op | source)
XLA Modules:
  0.0 573.1 jit_solution(11625470212043997421)
XLA Ops:
  6.5 0.0 all-gather.3.cloned.1.call-start
  6.5 1.7 subtract_select_fusion
  8.2 0.8 fusion.26
  9.0 0.0 copy-start
  9.1 0.0 copy-start.1
  9.1 9.8 %multiply_convert_fusion.1 = (bf16[64,8,1,512]{0,1,2,3:T(8,128)(2,1)S(1)}, bf16[64,8,1,512]{0,1,2,3:T(8,128)(2,1)S(1)}) fusion(s32[64,512]{0,1:T(8,128)S(1)} %fusion.26, s32[8]{0:T(128)} %param.9, f32[64,512]{0,1:T(8,128)S(1)} %get-tuple-element.11, f32[64,512]{0,1:T(8,128)S(1)} %get-tuple-element.12), kind=kLoop, calls=%fused_computation.26 | loop fusion | flops 4718592 | bytes 1441824 | tf_op jit(solution)/shard_map/convert.2
  18.9 10.7 %convert_bitcast_fusion = bf16[8,512,2,128]{3,0,2,1:T(8,128)(2,1)} fusion(bf16[64,512,128,1]{2,1,0,3:T(8,128)(2,1)} %bitcast.22, bf16[64,8,1,512]{0,1,2,3:T(8,128)(2,1)S(1)} %get-tuple-element.8, bf16[64,8,1,512]{0,1,2,3:T(8,128)(2,1)S(1)} %get-tuple-element.7), kind=kOutput, calls=%fused_computation.24 | convolution fusion | flops 135790592 | bytes 11534336 | tf_op jit(solution)/shard_map/tnk,tfpn->fnpk/dot_general | solution.py:31
  29.7 0.0 all-gather.3.cloned.1.call-update
  29.7 0.2 all-gather.5.cloned.1.call-start
  29.9 0.0 copy-done
  29.9 0.3 subtract_select_fusion.1
  30.2 0.0 copy-done.1
  30.2 2.5 multiply_convert_fusion.3
  32.8 1.3 copy.11
  34.0 8.0 %fusion.5 = bf16[256,8,2,256]{3,1,2,0:T(8,128)(2,1)S(1)} fusion(bf16[64,8,2,256]{0,1,2,3:T(8,128)(2,1)S(1)} %copy.11, bf16[64,256,256,1]{2,1,0,3:T(8,128)(2,1)} %bitcast.23), kind=kOutput, calls=%fused_computation.8 | convolution fusion | flops 134217728 | bytes 11010048 | tf_op jit(solution)/shard_map/tnk,tfpn->fnpk/dot_general | solution.py:31
  42.1 2.1 copy.31
  44.1 0.0 all-gather.5.cloned.1.call-update
  44.2 0.3 reduce-scatter.2.cloned.1.call-start
  44.4 314.3 %all-gather.3.cloned.1.call-done = bf16[8,512,2,1024]{3,0,2,1:T(8,128)(2,1)} async-done(((bf16[8,512,2,128]{3,0,2,1:T(8,128)(2,1)}), bf16[8,512,2,1024]{3,0,2,1:T(8,128)(2,1)}) %all-gather.3.cloned.1.call-update) | async-done | bytes 16777232 | tf_op jit(solution)/shard_map/all_gather | solution.py:48
  358.7 6.5 %fusion.37 = (bf16[8,512,1,1024]{3,0,2,1:T(8,128)(2,1)S(1)}, bf16[8,512,1,1024]{3,0,2,1:T(8,128)(2,1)S(1)}) fusion(bf16[8,512,2,1024]{3,0,2,1:T(8,128)(2,1)} %all-gather.3.cloned.1.call-done), kind=kLoop, calls=%fused_computation.54 | loop fusion | flops 4194304 | bytes 33554432 | tf_op jit(solution)/shard_map/slice | solution.py:37
  365.2 6.8 %maximum_bitcast_fusion = bf16[8,1,512,2,1024]{4,0,3,2,1:T(8,128)(2,1)} fusion(bf16[8,512,1,1024]{3,0,2,1:T(8,128)(2,1)S(1)} %get-tuple-element.6, bf16[8,512,1,1024]{3,0,2,1:T(8,128)(2,1)S(1)} %get-tuple-element.5), kind=kLoop, calls=%fused_computation.3 | loop fusion | flops 8388608 | bytes 33554432 | tf_op jit(solution)/shard_map/stack | solution.py:39
  372.0 23.6 %pad_maximum_fusion = bf16[8,2,512,2,1024]{4,0,3,2,1:T(8,128)(2,1)} fusion(bf16[8,1,512,2,1024]{4,0,3,2,1:T(8,128)(2,1)} %maximum_bitcast_fusion, bf16[8,1,512,2,1024]{4,0,3,2,1:T(8,128)(2,1)} %bitcast.21), kind=kLoop, calls=%fused_computation | loop fusion | flops 16777216 | bytes 67108864 | tf_op jit(solution)/shard_map/stack | solution.py:39
  395.7 53.8 %all-gather.5.cloned.1.call-done = bf16[8,256,2,1024]{3,1,2,0:T(8,128)(2,1)} async-done(((bf16[8,256,2,256]{3,1,2,0:T(8,128)(2,1)}), bf16[8,256,2,1024]{3,1,2,0:T(8,128)(2,1)}) %all-gather.5.cloned.1.call-update) | async-done | bytes 8388624 | tf_op jit(solution)/shard_map/all_gather | solution.py:45
  449.5 33.7 %fusion.7 = f32[8,2,512,256]{3,2,1,0:T(8,128)} fusion(bf16[8,256,2,1024]{3,1,2,0:T(8,128)(2,1)} %all-gather.5.cloned.1.call-done, bf16[8,2,512,2,1024]{4,0,3,2,1:T(8,128)(2,1)} %pad_maximum_fusion), kind=kOutput, calls=%fused_computation.14 | convolution fusion | flops 8589934592 | bytes 50331648 | tf_op jit(solution)/shard_map/fcipk,fjpk->fcij/dot_general | solution.py:46
  483.2 0.0 reduce-scatter.2.cloned.1.call-update
  483.2 80.2 %reduce-scatter.2.cloned.1.call-done = f32[2,2,512,256]{3,2,1,0:T(8,128)} async-done(((f32[8,2,512,256]{3,2,1,0:T(8,128)}), f32[2,2,512,256]{3,2,1,0:T(8,128)}) %reduce-scatter.2.cloned.1.call-update) | async-done | bytes 2097168 | tf_op jit(solution)/shard_map/reduce_scatter | solution.py:52
  563.5 3.1 broadcast_multiply_fusion
  (2 shorter events, 0.1 us)
Async XLA Ops:
  6.5 352.2 %all-gather.3.cloned.1.call-start = ((), (), s32[]{:S(2)}) async-start(), calls=%async_computation.1 | async-start | bytes 18874368 | tf_op jit(solution)/shard_map/all_gather | solution.py:48
  9.0 20.9 %copy-start = (s32[256]{0:T(256)S(1)}, s32[256]{0:T(256)}, u32[]{:S(2)}) copy-start(s32[256]{0:T(256)} %param.8) | copy-start | bytes 3076
  9.1 21.1 %copy-start.1 = (s32[8]{0:T(128)S(1)}, s32[8]{0:T(128)}, u32[]{:S(2)}) copy-start(s32[8]{0:T(128)} %param.9) | copy-start | bytes 100
  29.7 419.8 %all-gather.5.cloned.1.call-start = ((), (), s32[]{:S(2)}) async-start(), calls=%async_computation.2 | async-start | bytes 10485760 | tf_op jit(solution)/shard_map/all_gather | solution.py:45
  44.2 519.3 %reduce-scatter.2.cloned.1.call-start = ((), (), s32[]{:S(2)}) async-start(), calls=%async_computation.3 | async-start | bytes 10485760 | tf_op jit(solution)/shard_map/reduce_scatter | solution.py:52
Sparse Core Ops, SparseCore 0:
  29.8 328.8 all-gather.2
  360.3 89.0 all-gather.4
  483.4 80.0 reduce-scatter.1
where the time goes:
time: 573 us
  waiting for transfers between devices  448 us (78%)
  other arithmetic  55.1 us (10%)
  matrix products  52.5 us (9%)
  between operations  13.2 us (2%)
    all_gather x1, waiting for transfers between devices, local(): lax.all_gather(spec_rows, 'col', axis=3, tiled=True)  314 us
    reduce_scatter x1, waiting for transfers between devices, local(): lax.psum_scatter(partial_term, 'layer', scatter_dimension=0, tiled=True)  80.2 us
    all_gather x1, waiting for transfers between devices, local(): panel_cols = lax.all_gather(spec_cols, 'row', axis=3, tiled=True)  53.8 us
    dot_general x1, matrix products, local(): jnp.einsum('fcipk,fjpk->fcij', paired(lax.all_gather(spec_rows, 'col', ax...  33.7 us
    another operation x2, other arithmetic, paired(): return jnp.stack([piece, second], axis=-4)  30.5 us
    dot_general x2, matrix products, spectra(): jnp.einsum('tnk,tfpn->fnpk', traces, basis, preferred_element_type=jnp.fl...  18.8 us
    another operation x2, other arithmetic  12.3 us
  transfers between devices with their start and end apart: 3, of which 3 were waited for; matrix products, arithmetic and copies ran while one was open for 9% of the time, Pallas kernels for 0%

commit v1 on v0

v1 whole, which is shorter than its diff:
```python
import functools
import math

import jax
import jax.numpy as jnp
from jax import lax
from jax.experimental import pallas as pl
from jax.experimental.pallas import tpu as pltpu
from jax.sharding import PartitionSpec as P

NFFT = 1024
SAMPLES = 64
WINDOW = 48
K_AUX = 4096
AXES = ("layer", "row", "col")
GROUP = 16
STEP = 64
BF16 = jnp.bfloat16
F32 = jnp.float32


def permutation(dest):
    pairs = []
    for layer in range(4):
        for row in range(4):
            for col in range(8):
                z, core = 2 * (layer // 2) + col % 2, layer % 2
                x, y, z, core2 = dest(row, col // 2, z, core)
                to = ((z // 2) * 2 + core2) * 32 + x * 8 + y * 2 + z % 2
                pairs.append(((layer * 4 + row) * 8 + col, to))
    return pairs


def near(core):
    return 3 if core else 1


def far(core):
    return 1 if core else 3


Y_A = permutation(lambda x, y, z, c: (x, y ^ near(c), z, c))
Y_B = permutation(lambda x, y, z, c: (x, y ^ far(c), z, c))
X_A = permutation(lambda x, y, z, c: (x ^ near(c), y, z, c))
X_B = permutation(lambda x, y, z, c: (x ^ far(c), y, z, c))
SLOTS = [
    permutation(lambda x, y, z, c: (x, y, z, 1 - c)),
    permutation(lambda x, y, z, c: (x, y, z ^ near(c), c)),
    permutation(lambda x, y, z, c: (x, y, z ^ far(c), 1 - c)),
    permutation(lambda x, y, z, c: (x, y, z ^ far(c), c)),
    permutation(lambda x, y, z, c: (x, y, z ^ near(c), 1 - c)),
    permutation(lambda x, y, z, c: (x, y, z ^ 2, c)),
    permutation(lambda x, y, z, c: (x, y, z ^ 2, 1 - c)),
]
HALVES = permutation(lambda x, y, z, c: (x, y, z ^ 1, c))


def send(value, pairs):
    return lax.ppermute(value, AXES, pairs)


def after(value, *others):
    return lax.optimization_barrier((value,) + others)[0]


def basis_table(bins):
    lag = jnp.arange(SAMPLES, dtype=jnp.int32)
    taper = 0.5 - 0.5 * jnp.cos(2.0 * math.pi * (lag.astype(F32) + 0.5) / WINDOW)
    clipped = jnp.clip(lag, 0, WINDOW - 1)
    phase = bins[:, None] * clipped[None, :] % NFFT
    angle = 2.0 * math.pi * phase.astype(F32) / NFFT
    weight = jnp.where(lag < WINDOW, taper, 0.0)[None, :]
    both = jnp.stack([weight * jnp.cos(angle), -weight * jnp.sin(angle)], axis=1)
    return both.astype(BF16).reshape(16, SAMPLES)


def lag_rows(offsets):
    tick = jnp.arange(SAMPLES, dtype=jnp.int32)
    lag = tick[None, :, None] - offsets.reshape(-1, 1, GROUP)
    return lag.reshape(-1, 1, SAMPLES * GROUP)


def spectra_kernel(steps_rows, place, table, lags, rows, cols, *refs):
    outs, weights, result = refs[:8], refs[8], refs[9]
    step = pl.program_id(0)
    zl = place[0]

    def stations(traces, group, width, store):
        lag = lags[pl.ds(step * (STEP // GROUP) + group, 1)].reshape(1, SAMPLES * GROUP)
        tick = lax.broadcasted_iota(jnp.int32, (SAMPLES, SAMPLES * GROUP), 0)
        onehot = jnp.where(tick == lag, 1.0, 0.0).astype(BF16)
        basis = jnp.dot(table[...], onehot, preferred_element_type=F32).astype(BF16)
        lane = lax.broadcasted_iota(jnp.int32, (16, SAMPLES * GROUP), 1) % GROUP
        for n in range(GROUP):
            mask = jnp.where(lane == n, 1.0, 0.0).astype(BF16)
            weights[pl.ds(n * 16, 16), :] = basis * mask
        block = traces[:, pl.ds(group * GROUP, GROUP), :]
        spectrum = jnp.dot(
            weights[...],
            block.reshape(SAMPLES * GROUP, width),
            preferred_element_type=F32,
        )
        for half in range(width // 128):
            result[half] = spectrum[:, half * 128:half * 128 + 128]
        for slot in range(8):
            for part in range(2):
                store(slot, part, pl.ds(slot * 2 + part, GROUP, 16))

    @pl.when(step < steps_rows)
    def _():
        for group in range(STEP // GROUP):
            first = step * STEP + group * GROUP

            def store(slot, part, picked):
                at = pl.multiple_of(part * 512 + first, GROUP)
                outs[slot][pl.ds(at, GROUP), :] = result[0, picked, :].astype(BF16)

            stations(rows, group, 128, store)

    @pl.when(step >= steps_rows)
    def _():
        for group in range(STEP // GROUP):
            first = (step - steps_rows) * STEP + group * GROUP

            def store(slot, part, picked):
                for half in range(2):
                    at = 1024 + (half ^ zl) * 512 + part * 256 + first
                    outs[slot][pl.ds(pl.multiple_of(at, GROUP), GROUP), :] = result[half, picked, :].astype(BF16)

            stations(cols, group, 256, store)


def spectra(place, table, lags, rows, cols):
    steps_rows, steps_cols = rows.shape[1] // STEP, cols.shape[1] // STEP
    whole = lambda *shape: pl.BlockSpec(shape, lambda s, _: (0,) * len(shape))
    return pl.pallas_call(
        functools.partial(spectra_kernel, steps_rows),
        grid_spec=pltpu.PrefetchScalarGridSpec(
            num_scalar_prefetch=1,
            grid=(steps_rows + steps_cols,),
            in_specs=[
                whole(16, SAMPLES),
                whole(*lags.shape),
                pl.BlockSpec((SAMPLES, STEP, 128), lambda s, _: (0, jnp.minimum(s, steps_rows - 1), 0)),
                pl.BlockSpec((SAMPLES, STEP, 256), lambda s, _: (0, jnp.maximum(s - steps_rows, 0), 0)),
            ],
            out_specs=[whole(2048, 128)] * 8,
            scratch_shapes=[
                pltpu.VMEM((256, SAMPLES * GROUP), BF16),
                pltpu.VMEM((2, 256, 128), F32),
            ],
        ),
        out_shape=[jax.ShapeDtypeStruct((2048, 128), BF16)] * 8,
        compiler_params=pltpu.CompilerParams(vmem_limit_bytes=48 << 20),
        cost_estimate=pl.CostEstimate(flops=4 << 30, bytes_accessed=20 << 20, transcendentals=0),
        name="spectra",
    )(place, table, lags, rows, cols)


def correlate_kernel(halves, swap, keep, has_start, place, *refs):
    count = 24
    pieces, refs = refs[:count], refs[count:]
    starts, refs = refs[: len(halves) * has_start], refs[len(halves) * has_start:]
    outs, refs = refs[: len(halves)], refs[len(halves):]
    a_all, b_all, sems = refs[:3]
    core = place[1]
    first = core == (1 if swap else 0)
    a_in = [pieces[0:4], pieces[4:8], pieces[8:12]]
    b_in = [pieces[12:16], pieces[16:20], pieces[20:24]]

    def copies(chunk, slot):
        got = []
        for n in range(4):
            got.append(pltpu.make_async_copy(a_in[chunk][n], a_all.at[place[2 + n], slot], sems.at[slot * 8 + n]))
            got.append(pltpu.make_async_copy(b_in[chunk][n], b_all.at[place[6 + n], slot], sems.at[slot * 8 + 4 + n]))
        return got

    for copy in copies(0, 0):
        copy.start()

    @pl.when(first)
    def _():
        for copy in copies(1, 1):
            copy.start()

    @pl.when(jnp.logical_not(first))
    def _():
        for copy in copies(2, 1):
            copy.start()

    for copy in copies(0, 0) + copies(1, 1):
        copy.wait()

    scale = 1.0 / K_AUX
    for at, half in enumerate(halves):
        out = outs[at]
        for part in range(2):

            def body(block, _):
                rows = pl.ds(pl.multiple_of(block * 256, 256), 256)
                total = starts[at][part, rows, :] if has_start else None
                for q in range(4):
                    left, right = [], []
                    for other in range(2):
                        for z in range(2):
                            for p in range(2):
                                left.append(a_all[q, z, other, p, rows, :])
                                b = b_all[q, half, other, z ^ half, p ^ part]
                                right.append(-b if part == 1 and p == 0 else b)
                    term = lax.dot_general(
                        jnp.concatenate(left, axis=1),
                        jnp.concatenate(right, axis=1),
                        (((1,), (1,)), ((), ())),
                        preferred_element_type=F32,
                    )
                    total = term if total is None else total + term
                if keep is None:
                    out[part, rows, :] = total
                elif keep:
                    out[0, part, rows, :] = total * scale
                else:
                    out[part, rows, :] = (total * scale).astype(BF16)
                return 0

            lax.fori_loop(0, 2, body, 0)


def correlate(place, a_chunks, b_chunks, halves, swap=False, keep=None, starts=()):
    pieces = [piece for chunk in a_chunks + b_chunks for piece in chunk]
    whole = lambda *shape: pl.BlockSpec(shape, lambda s, _: (0,) * len(shape))
    if keep is None:
        outs = [jax.ShapeDtypeStruct((2, 512, 256), F32)] * len(halves)
        out_specs = [whole(2, 512, 256)] * len(halves)
    elif keep:
        outs = [jax.ShapeDtypeStruct((2, 2, 512, 256), F32)]
        out_specs = [pl.BlockSpec((1, 2, 512, 256), lambda s, place: (place[0], 0, 0, 0))]
    else:
        outs = [jax.ShapeDtypeStruct((2, 512, 256), BF16)]
        out_specs = [whole(2, 512, 256)]
    return pl.pallas_call(
        functools.partial(correlate_kernel, halves, swap, keep, len(starts) > 0),
        grid_spec=pltpu.PrefetchScalarGridSpec(
            num_scalar_prefetch=1,
            grid=(1,),
            in_specs=[pl.BlockSpec(memory_space=pl.ANY)] * 24 + [whole(2, 512, 256)] * len(starts),
            out_specs=out_specs,
            scratch_shapes=[
                pltpu.VMEM((4, 2, 2, 2, 512, 128), BF16),
                pltpu.VMEM((4, 2, 2, 2, 2, 256, 128), BF16),
                pltpu.SemaphoreType.DMA((16,)),
            ],
        ),
        out_shape=outs,
        compiler_params=pltpu.CompilerParams(vmem_limit_bytes=48 << 20),
        cost_estimate=pl.CostEstimate(flops=(2 << 30) * len(halves), bytes_accessed=10 << 20, transcendentals=0),
        name="correlate",
    )(place, *pieces, *starts)


def finish_kernel(place, got, whole, out):
    del place, whole
    out[0] = got[...].astype(F32)


def finish(place, got, whole):
    return pl.pallas_call(
        finish_kernel,
        grid_spec=pltpu.PrefetchScalarGridSpec(
            num_scalar_prefetch=1,
            grid=(2,),
            in_specs=[
                pl.BlockSpec((1, 512, 256), lambda s, _: (s, 0, 0)),
                pl.BlockSpec(memory_space=pl.ANY),
            ],
            out_specs=pl.BlockSpec((1, 1, 512, 256), lambda s, place: (1 - place[0], s, 0, 0)),
        ),
        out_shape=jax.ShapeDtypeStruct((2, 2, 512, 256), F32),
        input_output_aliases={2: 0},
        name="finish",
    )(place, got, whole)


def local(traces_rows, traces_cols, offsets_rows, offsets_cols, bins):
    layer, x, col = (lax.axis_index(axis) for axis in AXES)
    y, zl, zh, core = col // 2, col % 2, layer // 2, layer % 2
    z = 2 * zh + zl
    one, three = 1 + 2 * core, 3 - 2 * core
    place = jnp.stack(
        [zl, core, y, y ^ one, y ^ three, y ^ 2, x, x ^ one, x ^ three, x ^ 2]
    ).astype(jnp.int32)

    dests = [
        (z, core), (z, 1 - core), (z ^ one, core), (z ^ three, 1 - core),
        (z ^ three, core), (z ^ one, 1 - core), (z ^ 2, core), (z ^ 2, 1 - core),
    ]
    order = jnp.stack([4 * (a // 2) + 2 * b + a % 2 for a, b in dests])
    picked = jnp.sum(jnp.where(order[:, None] == jnp.arange(8)[None, :], bins[None, :], 0), axis=1)
    lags = jnp.concatenate([lag_rows(offsets_rows), lag_rows(offsets_cols)], axis=0)
    own, *away = spectra(place, basis_table(picked), lags, traces_rows, traces_cols)

    got = [send(slab, pairs) for slab, pairs in zip(away, SLOTS)]
    pairs = [(own, got[0]), (got[1], got[2]), (got[3], got[4]), (got[5], got[6])]
    a_chunks, b_chunks = [], []
    for first, second in pairs:
        a = jnp.stack([first[:1024], second[:1024]]).reshape(2, 2, 512, 128)
        b = jnp.stack([first[1024:], second[1024:]]).reshape(2, 2, 2, 256, 128)
        for chunk, chunks, one_way, other_way in ((a, a_chunks, Y_A, Y_B), (b, b_chunks, X_A, X_B)):
            near_by, far_by = send(chunk, one_way), send(chunk, other_way)
            chunks.append((chunk, near_by, far_by, send(far_by, one_way)))

    pa, qa, ra, sa = a_chunks
    pb, qb, rb, sb = b_chunks
    keep0, send0 = correlate(place, [pa, qa, ra], [pb, qb, rb], (0, 1))
    (leaves,) = correlate(place, [sa, qa, ra], [sb, qb, rb], (1,), swap=True, keep=False, starts=(send0,))
    arrived = send(leaves, HALVES)
    (stays,) = correlate(place, [sa, qa, ra], [sb, qb, rb], (0,), swap=True, keep=True, starts=(keep0,))
    return finish(place, arrived, stays)


def solution(mesh):
    return jax.shard_map(
        local,
        mesh=mesh,
        in_specs=(
            P(None, "row", ("layer", "col")),
            P(None, "col", ("layer", "row")),
            P("row"),
            P("col"),
            P(),
        ),
        out_specs=P("layer", None, "row", "col"),
        check_vma=False,
    )
```

time: 573 us -> 182 us (0.32)
  waiting for transfers between devices: 448 us -> 67 us
  starting transfers between devices: 0.49 us -> 61.1 us
  other arithmetic: 55.1 us -> 1.59 us
  matrix products: 52.5 us -> 0 us
  Pallas kernels: 0 us -> 46.9 us
  between operations: 13.2 us -> 0.58 us
    all_gather x2 -> x0, waiting for transfers between devices: 368 us -> none  [the longest x1 314 us: local(): lax.all_gather(spec_rows, 'col', axis=3, tiled=True)]
    reduce_scatter x1 -> x0, waiting for transfers between devices: 80.2 us -> none  [local(): lax.psum_scatter(partial_term, 'layer', scatter_dimension=0, tiled=True)]
    ppermute x0 -> x32, waiting for transfers between devices: none -> 67 us  [send(): return lax.ppermute(value, AXES, pairs)]
    ppermute x0 -> x32, starting transfers between devices: none -> 61.1 us  [send(): return lax.ppermute(value, AXES, pairs)]
    dot_general x3 -> x0, matrix products: 52.5 us -> none  [the longest x1 33.7 us: local(): jnp.einsum('fcipk,fjpk->fcij', paired(lax.all_gather(spec_rows, 'col', ax...]
    pallas_call x0 -> x5, Pallas kernels: none -> 46.9 us  [the longest x3 25.2 us: correlate(): pl.pallas_call(functools.partial(correlate_kernel, halves, swap, keep, le...]
    another operation x5 -> x10, other arithmetic: 42.8 us -> 0.54 us  [the longest x4 0.21 us: local(): a = jnp.stack([first[:1024], second[:1024]]).reshape(2, 2, 512, 128)]
    slice x1 -> x0, other arithmetic: 6.48 us -> none  [paired(): imag = piece[..., 1, :]]
  transfers between devices with their start and end apart: 3 -> 32, of which waited for: 3 -> 13; matrix products, arithmetic and copies ran while one was open for 9% -> 0% of each run, Pallas kernels for 0% -> 10%
where the time goes in v1:
time: 182 us
  waiting for transfers between devices  67 us (37%)
  starting transfers between devices  61.1 us (34%)
  Pallas kernels  46.9 us (26%)
  local copies, waits for them, and re-layouts  4.5 us (2%)
    ppermute x32, waiting for transfers between devices, send(): return lax.ppermute(value, AXES, pairs)  67 us
    ppermute x32, starting transfers between devices, send(): return lax.ppermute(value, AXES, pairs)  61.1 us
    pallas_call x3, Pallas kernels, correlate(): pl.pallas_call(functools.partial(correlate_kernel, halves, swap, keep, le...  25.2 us
    pallas_call x1, Pallas kernels, spectra(): pl.pallas_call(functools.partial(spectra_kernel, steps_rows), grid_spec=p...  19 us
  transfers between devices with their start and end apart: 32, of which 13 were waited for; matrix products, arithmetic and copies ran while one was open for 0% of the time, Pallas kernels for 10%

profile of v1, /device:TPU:1, one launch (start us, length us, event | category | flops | bytes accessed | tf_op | source)
XLA Modules:
  0.0 181.7 jit_solution(6062618772276747060)
XLA Ops:
  3.7 19.0 %spectra.1 = (bf16[2048,128]{1,0:T(8,128)(2,1)S(1)}, bf16[2048,128]{1,0:T(8,128)(2,1)S(1)}, bf16[2048,128]{1,0:T(8,128)(2,1)S(1)}, bf16[2048,128]{1,0:T(8,128)(2...) custom-call(s32[10]{0:T(128)S(1)} %stack.148.place, ...), custom_call_target="tpu_custom_call" | custom-call | flops 4294967296 | bytes 20971520 | tf_op jit(solution)/shard_map/spectra/pallas_call | solution.py:136
  22.7 2.5 %collective-permute-start.10 = (bf16[2048,128]{1,0:T(8,128)(2,1)S(1)}, bf16[2048,128]{1,0:T(8,128)(2,1)S(1)}, u32[]{:S(2)}, u32[]{:S(2)}) collective-permute-start(bf16[2048,128]{1,0:T(8,128)(2,1)S(1)} %get-tuple-element.19), channel_id=1, source_target_pairs={{0,65},{1,64},{2,67},{3,66},{4,69},{5,68},{6,71},{7,70},{8,73},{9,... | collective-permute-start | bytes 1572872 | tf_op jit(solution)/shard_map/ppermute | solution.py:59
  25.3 2.8 %collective-permute-start.11 = (bf16[2048,128]{1,0:T(8,128)(2,1)S(1)}, bf16[2048,128]{1,0:T(8,128)(2,1)S(1)}, u32[]{:S(2)}, u32[]{:S(2)}) collective-permute-start(bf16[2048,128]{1,0:T(8,128)(2,1)S(1)} %get-tuple-element.20), channel_id=1, source_target_pairs={{0,33},{1,32},{2,35},{3,34},{4,37},{5,36},{6,39},{7,38},{8,41},{9,... | collective-permute-start | bytes 1572872 | tf_op jit(solution)/shard_map/ppermute | solution.py:59
  28.1 2.9 %collective-permute-start.5 = (bf16[2048,128]{1,0:T(8,128)(2,1)S(1)}, bf16[2048,128]{1,0:T(8,128)(2,1)S(1)}, u32[]{:S(2)}, u32[]{:S(2)}) collective-permute-start(bf16[2048,128]{1,0:T(8,128)(2,1)S(1)} %get-tuple-element.17), channel_id=1, source_target_pairs={{0,1},{1,0},{2,3},{3,2},{4,5},{5,4},{6,7},{7,6},{8,9},{9,8},{10,11... | collective-permute-start | bytes 1572872 | tf_op jit(solution)/shard_map/ppermute | solution.py:59
  31.4 3.5 %collective-permute-done.10 = bf16[2048,128]{1,0:T(8,128)(2,1)S(1)} collective-permute-done((bf16[2048,128]{1,0:T(8,128)(2,1)S(1)}, bf16[2048,128]{1,0:T(8,128)(2,1)S(1)}, u32[]{:S(2)}, u32[]{:S(2)}) %collective-permute-start.10) | collective-permute-done | bytes 524320 | tf_op jit(solution)/shard_map/ppermute | solution.py:59
  34.9 4.7 %collective-permute-start = (bf16[2048,128]{1,0:T(8,128)(2,1)S(1)}, bf16[2048,128]{1,0:T(8,128)(2,1)S(1)}, u32[]{:S(2)}, u32[]{:S(2)}) collective-permute-start(bf16[2048,128]{1,0:T(8,128)(2,1)S(1)} %get-tuple-element.15), channel_id=1, source_target_pairs={{0,64},{1,65},{2,66},{3,67},{4,68},{5,69},{6,70},{7,71},{8,72},{9,... | collective-permute-start | bytes 1572872 | tf_op jit(solution)/shard_map/ppermute | solution.py:59
  40.6 3.3 %collective-permute-start.1 = (bf16[2048,128]{1,0:T(8,128)(2,1)S(1)}, bf16[2048,128]{1,0:T(8,128)(2,1)S(1)}, u32[]{:S(2)}, u32[]{:S(2)}) collective-permute-start(bf16[2048,128]{1,0:T(8,128)(2,1)S(1)} %get-tuple-element.16), channel_id=1, source_target_pairs={{0,96},{1,97},{2,98},{3,99},{4,100},{5,101},{6,102},{7,103},{8,104... | collective-permute-start | bytes 1572872 | tf_op jit(solution)/shard_map/ppermute | solution.py:59
  44.0 29.1 %collective-permute-done.5 = bf16[2048,128]{1,0:T(8,128)(2,1)S(1)} collective-permute-done((bf16[2048,128]{1,0:T(8,128)(2,1)S(1)}, bf16[2048,128]{1,0:T(8,128)(2,1)S(1)}, u32[]{:S(2)}, u32[]{:S(2)}) %collective-permute-start.5) | collective-permute-done | bytes 524320 | tf_op jit(solution)/shard_map/ppermute | solution.py:59
  74.4 2.0 %collective-permute-start.12 = (bf16[2,2,512,128]{3,2,1,0:T(8,128)(2,1)S(1)}, bf16[2,2,512,128]{3,2,1,0:T(8,128)(2,1)S(1)}, u32[]{:S(2)}, u32[]{:S(2)}) collective-permute-start(bf16[2,2,512,128]{3,2,1,0:T(8,128)(2,1)S(1)} %pad_maximum_fusion.2.refs_8_), channel_id=1, source_target_pairs={{0,2},{1,3},{2,0},{3,1},{4,6},{5,7},{6,4},{7,5},{8,10},{9,11},{10,... | collective-permute-start | bytes 1572872 | tf_op jit(solution)/shard_map/ppermute | solution.py:59
  77.9 1.8 %collective-permute-start.18 = (bf16[2,2,2,256,128]{4,3,2,1,0:T(8,128)(2,1)S(1)}, bf16[2,2,2,256,128]{4,3,2,1,0:T(8,128)(2,1)S(1)}, u32[]{:S(2)}, u32[]{:S(2)}) collective-permute-start(bf16[2,2,2,256,128]{4,3,2,1,0:T(8,128)(2,1)S(1)} %pad_maximum_fusion.4.refs_16_), channel_id=1, source_target_pairs={{0,8},{1,9},{2,10},{3,11},{4,12},{5,13},{6,14},{7,15},{8,0},{9,1},... | collective-permute-start | bytes 1572872 | tf_op jit(solution)/shard_map/ppermute | solution.py:59
  80.2 5.5 %collective-permute-done.13.refs_10_ = bf16[2,2,512,128]{3,2,1,0:T(8,128)(2,1)S(1)} collective-permute-done((bf16[2,2,512,128]{3,2,1,0:T(8,128)(2,1)S(1)}, bf16[2,2,512,128]{3,2,1,0:T(8,128)(2,1)S(1)}, u32[]{:S(2)}, u32[]{:S(2)}) %collective-permute-start.13) | collective-permute-done | bytes 524320 | tf_op jit(solution)/shard_map/ppermute | solution.py:59
  85.7 2.5 %collective-permute-start.21 = (bf16[2,2,2,256,128]{4,3,2,1,0:T(8,128)(2,1)S(1)}, bf16[2,2,2,256,128]{4,3,2,1,0:T(8,128)(2,1)S(1)}, u32[]{:S(2)}, u32[]{:S(2)}) collective-permute-start(bf16[2,2,2,256,128]{4,3,2,1,0:T(8,128)(2,1)S(1)} %pad_maximum_fusion.5.refs_20_), channel_id=1, source_target_pairs={{0,8},{1,9},{2,10},{3,11},{4,12},{5,13},{6,14},{7,15},{8,0},{9,1},... | collective-permute-start | bytes 1572872 | tf_op jit(solution)/shard_map/ppermute | solution.py:59
  89.5 10.4 %collective-permute-done.22.refs_22_ = bf16[2,2,2,256,128]{4,3,2,1,0:T(8,128)(2,1)S(1)} collective-permute-done((bf16[2,2,2,256,128]{4,3,2,1,0:T(8,128)(2,1)S(1)}, bf16[2,2,2,256,128]{4,3,2,1,0:T(8,128)(2,1)S(1)}, u32[]{:S(2)}, u32[]{:S(2)}) %collective-permute-start.22) | collective-permute-done | bytes 524320 | tf_op jit(solution)/shard_map/ppermute | solution.py:59
  99.9 2.3 %collective-permute-start.29 = (bf16[2,2,2,256,128]{4,3,2,1,0:T(8,128)(2,1)S(1)}, bf16[2,2,2,256,128]{4,3,2,1,0:T(8,128)(2,1)S(1)}, u32[]{:S(2)}, u32[]{:S(2)}) collective-permute-start(bf16[2,2,2,256,128]{4,3,2,1,0:T(8,128)(2,1)S(1)} %pad_maximum_fusion.7.refs_12_), channel_id=1, source_target_pairs={{0,24},{1,25},{2,26},{3,27},{4,28},{5,29},{6,30},{7,31},{8,16},{9,... | collective-permute-start | bytes 1572872 | tf_op jit(solution)/shard_map/ppermute | solution.py:59
  102.1 2.8 %collective-permute-start.28 = (bf16[2,2,2,256,128]{4,3,2,1,0:T(8,128)(2,1)S(1)}, bf16[2,2,2,256,128]{4,3,2,1,0:T(8,128)(2,1)S(1)}, u32[]{:S(2)}, u32[]{:S(2)}) collective-permute-start(bf16[2,2,2,256,128]{4,3,2,1,0:T(8,128)(2,1)S(1)} %pad_maximum_fusion.7.refs_12_), channel_id=1, source_target_pairs={{0,8},{1,9},{2,10},{3,11},{4,12},{5,13},{6,14},{7,15},{8,0},{9,1},... | collective-permute-start | bytes 1572872 | tf_op jit(solution)/shard_map/ppermute | solution.py:59
  105.4 2.6 %collective-permute-start.7 = (bf16[2,2,512,128]{3,2,1,0:T(8,128)(2,1)S(1)}, bf16[2,2,512,128]{3,2,1,0:T(8,128)(2,1)S(1)}, u32[]{:S(2)}, u32[]{:S(2)}) collective-permute-start(bf16[2,2,512,128]{3,2,1,0:T(8,128)(2,1)S(1)} %pad_maximum_fusion.1.refs_4_), channel_id=1, source_target_pairs={{0,2},{1,3},{2,0},{3,1},{4,6},{5,7},{6,4},{7,5},{8,10},{9,11},{10,... | collective-permute-start | bytes 1572872 | tf_op jit(solution)/shard_map/ppermute | solution.py:59
  107.9 2.9 %collective-permute-done.29.refs_14_ = bf16[2,2,2,256,128]{4,3,2,1,0:T(8,128)(2,1)S(1)} collective-permute-done((bf16[2,2,2,256,128]{4,3,2,1,0:T(8,128)(2,1)S(1)}, bf16[2,2,2,256,128]{4,3,2,1,0:T(8,128)(2,1)S(1)}, u32[]{:S(2)}, u32[]{:S(2)}) %collective-permute-start.29) | collective-permute-done | bytes 524320 | tf_op jit(solution)/shard_map/ppermute | solution.py:59
  110.9 2.2 %collective-permute-start.16 = (bf16[2,2,2,256,128]{4,3,2,1,0:T(8,128)(2,1)S(1)}, bf16[2,2,2,256,128]{4,3,2,1,0:T(8,128)(2,1)S(1)}, u32[]{:S(2)}, u32[]{:S(2)}) collective-permute-start(bf16[2,2,2,256,128]{4,3,2,1,0:T(8,128)(2,1)S(1)} %pad_maximum_fusion.3.refs_12_), channel_id=1, source_target_pairs={{0,24},{1,25},{2,26},{3,27},{4,28},{5,29},{6,30},{7,31},{8,16},{9,... | collective-permute-start | bytes 1572872 | tf_op jit(solution)/shard_map/ppermute | solution.py:59
  113.1 4.2 %collective-permute-done.28.refs_13_ = bf16[2,2,2,256,128]{4,3,2,1,0:T(8,128)(2,1)S(1)} collective-permute-done((bf16[2,2,2,256,128]{4,3,2,1,0:T(8,128)(2,1)S(1)}, bf16[2,2,2,256,128]{4,3,2,1,0:T(8,128)(2,1)S(1)}, u32[]{:S(2)}, u32[]{:S(2)}) %collective-permute-start.28) | collective-permute-done | bytes 524320 | tf_op jit(solution)/shard_map/ppermute | solution.py:59
  119.3 2.7 %collective-permute-start.20 = (bf16[2,2,2,256,128]{4,3,2,1,0:T(8,128)(2,1)S(1)}, bf16[2,2,2,256,128]{4,3,2,1,0:T(8,128)(2,1)S(1)}, u32[]{:S(2)}, u32[]{:S(2)}) collective-permute-start(bf16[2,2,2,256,128]{4,3,2,1,0:T(8,128)(2,1)S(1)} %collective-permute-done.19.refs_18_), channel_id=1, source_target_pairs={{0,8},{1,9},{2,10},{3,11},{4,12},{5,13},{6,14},{7,15},{8,0},{9,1},... | collective-permute-start | bytes 1572872 | tf_op jit(solution)/shard_map/ppermute | solution.py:59
  122.0 3.2 %collective-permute-start.23 = (bf16[2,2,2,256,128]{4,3,2,1,0:T(8,128)(2,1)S(1)}, bf16[2,2,2,256,128]{4,3,2,1,0:T(8,128)(2,1)S(1)}, u32[]{:S(2)}, u32[]{:S(2)}) collective-permute-start(bf16[2,2,2,256,128]{4,3,2,1,0:T(8,128)(2,1)S(1)} %collective-permute-done.22.refs_22_), channel_id=1, source_target_pairs={{0,8},{1,9},{2,10},{3,11},{4,12},{5,13},{6,14},{7,15},{8,0},{9,1},... | collective-permute-start | bytes 1572872 | tf_op jit(solution)/shard_map/ppermute | solution.py:59
  126.9 6.0 %collective-permute-start.30 = (bf16[2,2,2,256,128]{4,3,2,1,0:T(8,128)(2,1)S(1)}, bf16[2,2,2,256,128]{4,3,2,1,0:T(8,128)(2,1)}, u32[]{:S(2)}, u32[]{:S(2)}) collective-permute-start(bf16[2,2,2,256,128]{4,3,2,1,0:T(8,128)(2,1)S(1)} %collective-permute-done.29.refs_14_), channel_id=1, source_target_pairs={{0,8},{1,9},{2,10},{3,11},{4,12},{5,13},{6,14},{7,15},{8,0},{9,1},... | collective-permute-start | bytes 1572872 | tf_op jit(solution)/shard_map/ppermute | solution.py:59
  133.8 2.7 %collective-permute-start.15 = (bf16[2,2,2,256,128]{4,3,2,1,0:T(8,128)(2,1)S(1)}, bf16[2,2,2,256,128]{4,3,2,1,0:T(8,128)(2,1)S(1)}, u32[]{:S(2)}, u32[]{:S(2)}) collective-permute-start(bf16[2,2,2,256,128]{4,3,2,1,0:T(8,128)(2,1)S(1)} %pad_maximum_fusion.3.refs_12_), channel_id=1, source_target_pairs={{0,8},{1,9},{2,10},{3,11},{4,12},{5,13},{6,14},{7,15},{8,0},{9,1},... | collective-permute-start | bytes 1572872 | tf_op jit(solution)/shard_map/ppermute | solution.py:59
  136.5 1.9 %collective-permute-done.23.refs_23_ = bf16[2,2,2,256,128]{4,3,2,1,0:T(8,128)(2,1)S(1)} collective-permute-done((bf16[2,2,2,256,128]{4,3,2,1,0:T(8,128)(2,1)S(1)}, bf16[2,2,2,256,128]{4,3,2,1,0:T(8,128)(2,1)S(1)}, u32[]{:S(2)}, u32[]{:S(2)}) %collective-permute-start.23) | collective-permute-done | bytes 524320 | tf_op jit(solution)/shard_map/ppermute | solution.py:59
  138.5 2.9 %collective-permute-start.2 = (bf16[2,2,512,128]{3,2,1,0:T(8,128)(2,1)S(1)}, bf16[2,2,512,128]{3,2,1,0:T(8,128)(2,1)S(1)}, u32[]{:S(2)}, u32[]{:S(2)}) collective-permute-start(bf16[2,2,512,128]{3,2,1,0:T(8,128)(2,1)S(1)} %pad_maximum_fusion.refs_0_), channel_id=1, source_target_pairs={{0,2},{1,3},{2,0},{3,1},{4,6},{5,7},{6,4},{7,5},{8,10},{9,11},{10,... | collective-permute-start | bytes 1572872 | tf_op jit(solution)/shard_map/ppermute | solution.py:59
  141.3 1.8 collective-permute-start.17
  144.2 2.9 %collective-permute-start.4 = (bf16[2,2,512,128]{3,2,1,0:T(8,128)(2,1)S(1)}, bf16[2,2,512,128]{3,2,1,0:T(8,128)(2,1)S(1)}, u32[]{:S(2)}, u32[]{:S(2)}) collective-permute-start(bf16[2,2,512,128]{3,2,1,0:T(8,128)(2,1)S(1)} %collective-permute-done.3.refs_2_), channel_id=1, source_target_pairs={{0,2},{1,3},{2,0},{3,1},{4,6},{5,7},{6,4},{7,5},{8,10},{9,11},{10,... | collective-permute-start | bytes 1572872 | tf_op jit(solution)/shard_map/ppermute | solution.py:59
  147.2 10.0 %correlate.3 = (f32[2,512,256]{2,1,0:T(8,128)}, f32[2,512,256]{2,1,0:T(8,128)}) custom-call(s32[10]{0:T(128)S(1)} %stack.148.place, bf16[2,2,512,128]{3,2,1,0:T(8,128)(2,1)S(1)} %pad_maximum_fusion.6.refs_0_, bf16[2,2,512,128]{3,2,1,0:T(8,128)(2,1)S(1)} %collective-permute-done.25.refs_1_, bf16[2,2,512,128]{3,2,1,0:T(8,128)(2,1)S(1)} %collective-permute-done.26.refs_2_, ...), custom_call_target="tpu_custom_call" | custom-call | flops 4294967296 | bytes 10485760 | tf_op jit(solution)/shard_map/correlate/pallas_call | solution.py:240
  158.3 7.1 %correlate.4 = bf16[2,512,256]{2,1,0:T(8,128)(2,1)S(1)} custom-call(s32[10]{0:T(128)S(1)} %stack.148.place, bf16[2,2,512,128]{3,2,1,0:T(8,128)(2,1)S(1)} %pad_maximum_fusion.refs_0_, bf16[2,2,512,128]{3,2,1,0:T(8,128)(2,1)S(1)} %collective-permute-done.2.refs_1_, bf16[2,2,512,128]{3,2,1,0:T(8,128)(2,1)S(1)} %collective-permute-done.3.refs_2_, ...), custom_call_target="tpu_custom_call" | custom-call | flops 2147483648 | bytes 10485760 | tf_op jit(solution)/shard_map/correlate/pallas_call | solution.py:240
  165.5 8.1 %correlate.5.whole = f32[2,2,512,256]{3,2,1,0:T(8,128)} custom-call(s32[10]{0:T(128)S(1)} %stack.148.place, bf16[2,2,512,128]{3,2,1,0:T(8,128)(2,1)S(1)} %pad_maximum_fusion.refs_0_, bf16[2,2,512,128]{3,2,1,0:T(8,128)(2,1)S(1)} %collective-permute-done.2.refs_1_, bf16[2,2,512,128]{3,2,1,0:T(8,128)(2,1)S(1)} %collective-permute-done.3.refs_2_, ...), custom_call_target="tpu_custom_call" | custom-call | flops 2147483648 | bytes 10485760 | tf_op jit(solution)/shard_map/correlate/pallas_call | solution.py:240
  173.6 4.6 %collective-permute-done.31.got = bf16[2,512,256]{2,1,0:T(8,128)(2,1)S(1)} collective-permute-done((bf16[2,512,256]{2,1,0:T(8,128)(2,1)S(1)}, bf16[2,512,256]{2,1,0:T(8,128)(2,1)S(1)}, u32[]{:S(2)}, u32[]{:S(2)}) %collective-permute-start.31) | collective-permute-done | bytes 524320 | tf_op jit(solution)/shard_map/ppermute | solution.py:59
  179.0 2.6 %finish.1 = f32[2,2,512,256]{3,2,1,0:T(8,128)} custom-call(s32[10]{0:T(128)} %copy-done.2, bf16[2,512,256]{2,1,0:T(8,128)(2,1)} %copy-done.16, f32[2,2,512,256]{3,2,1,0:T(8,128)} %correlate.5.whole), custom_call_target="tpu_custom_call", output_to_operand_aliasing={{}: (2, {})} | custom-call | tf_op jit(solution)/shard_map/finish/pallas_call | solution.py:266
  (113 shorter events, 17.6 us)
Async XLA Ops:
  22.7 12.2 %collective-permute-start.10 = (bf16[2048,128]{1,0:T(8,128)(2,1)S(1)}, bf16[2048,128]{1,0:T(8,128)(2,1)S(1)}, u32[]{:S(2)}, u32[]{:S(2)}) collective-permute-start(bf16[2048,128]{1,0:T(8,128)(2,1)S(1)} %get-tuple-element.19), channel_id=1, source_target_pairs={{0,65},{1,64},{2,67},{3,66},{4,69},{5,68},{6,71},{7,70},{8,73},{9,... | collective-permute-start | bytes 1572872 | tf_op jit(solution)/shard_map/ppermute | solution.py:59
  25.3 15.3 %collective-permute-start.11 = (bf16[2048,128]{1,0:T(8,128)(2,1)S(1)}, bf16[2048,128]{1,0:T(8,128)(2,1)S(1)}, u32[]{:S(2)}, u32[]{:S(2)}) collective-permute-start(bf16[2048,128]{1,0:T(8,128)(2,1)S(1)} %get-tuple-element.20), channel_id=1, source_target_pairs={{0,33},{1,32},{2,35},{3,34},{4,37},{5,36},{6,39},{7,38},{8,41},{9,... | collective-permute-start | bytes 1572872 | tf_op jit(solution)/shard_map/ppermute | solution.py:59
  28.1 45.0 %collective-permute-start.5 = (bf16[2048,128]{1,0:T(8,128)(2,1)S(1)}, bf16[2048,128]{1,0:T(8,128)(2,1)S(1)}, u32[]{:S(2)}, u32[]{:S(2)}) collective-permute-start(bf16[2048,128]{1,0:T(8,128)(2,1)S(1)} %get-tuple-element.17), channel_id=1, source_target_pairs={{0,1},{1,0},{2,3},{3,2},{4,5},{5,4},{6,7},{7,6},{8,9},{9,8},{10,11... | collective-permute-start | bytes 1572872 | tf_op jit(solution)/shard_map/ppermute | solution.py:59
  30.9 43.5 %collective-permute-start.6 = (bf16[2048,128]{1,0:T(8,128)(2,1)S(1)}, bf16[2048,128]{1,0:T(8,128)(2,1)S(1)}, u32[]{:S(2)}, u32[]{:S(2)}) collective-permute-start(bf16[2048,128]{1,0:T(8,128)(2,1)S(1)} %get-tuple-element.18), channel_id=1, source_target_pairs={{0,97},{1,96},{2,99},{3,98},{4,101},{5,100},{6,103},{7,102},{8,105... | collective-permute-start | bytes 1572872 | tf_op jit(solution)/shard_map/ppermute | solution.py:59
  30.9 45.6 %collective-permute-start.24 = (bf16[2048,128]{1,0:T(8,128)(2,1)S(1)}, bf16[2048,128]{1,0:T(8,128)(2,1)S(1)}, u32[]{:S(2)}, u32[]{:S(2)}) collective-permute-start(bf16[2048,128]{1,0:T(8,128)(2,1)S(1)} %get-tuple-element.22), channel_id=1, source_target_pairs={{0,32},{1,33},{2,34},{3,35},{4,36},{5,37},{6,38},{7,39},{8,40},{9,... | collective-permute-start | bytes 1572872 | tf_op jit(solution)/shard_map/ppermute | solution.py:59
  34.9 42.9 %collective-permute-start = (bf16[2048,128]{1,0:T(8,128)(2,1)S(1)}, bf16[2048,128]{1,0:T(8,128)(2,1)S(1)}, u32[]{:S(2)}, u32[]{:S(2)}) collective-permute-start(bf16[2048,128]{1,0:T(8,128)(2,1)S(1)} %get-tuple-element.15), channel_id=1, source_target_pairs={{0,64},{1,65},{2,66},{3,67},{4,68},{5,69},{6,70},{7,71},{8,72},{9,... | collective-permute-start | bytes 1572872 | tf_op jit(solution)/shard_map/ppermute | solution.py:59
  40.6 39.1 %collective-permute-start.1 = (bf16[2048,128]{1,0:T(8,128)(2,1)S(1)}, bf16[2048,128]{1,0:T(8,128)(2,1)S(1)}, u32[]{:S(2)}, u32[]{:S(2)}) collective-permute-start(bf16[2048,128]{1,0:T(8,128)(2,1)S(1)} %get-tuple-element.16), channel_id=1, source_target_pairs={{0,96},{1,97},{2,98},{3,99},{4,100},{5,101},{6,102},{7,103},{8,104... | collective-permute-start | bytes 1572872 | tf_op jit(solution)/shard_map/ppermute | solution.py:59
  73.1 12.6 %collective-permute-start.13 = (bf16[2,2,512,128]{3,2,1,0:T(8,128)(2,1)S(1)}, bf16[2,2,512,128]{3,2,1,0:T(8,128)(2,1)S(1)}, u32[]{:S(2)}, u32[]{:S(2)}) collective-permute-start(bf16[2,2,512,128]{3,2,1,0:T(8,128)(2,1)S(1)} %pad_maximum_fusion.2.refs_8_), channel_id=1, source_target_pairs={{0,6},{1,7},{2,4},{3,5},{4,2},{5,3},{6,0},{7,1},{8,14},{9,15},{10,... | collective-permute-start | bytes 1572872 | tf_op jit(solution)/shard_map/ppermute | solution.py:59
  74.4 25.4 %collective-permute-start.12 = (bf16[2,2,512,128]{3,2,1,0:T(8,128)(2,1)S(1)}, bf16[2,2,512,128]{3,2,1,0:T(8,128)(2,1)S(1)}, u32[]{:S(2)}, u32[]{:S(2)}) collective-permute-start(bf16[2,2,512,128]{3,2,1,0:T(8,128)(2,1)S(1)} %pad_maximum_fusion.2.refs_8_), channel_id=1, source_target_pairs={{0,2},{1,3},{2,0},{3,1},{4,6},{5,7},{6,4},{7,5},{8,10},{9,11},{10,... | collective-permute-start | bytes 1572872 | tf_op jit(solution)/shard_map/ppermute | solution.py:59
  76.6 12.0 %collective-permute-start.19 = (bf16[2,2,2,256,128]{4,3,2,1,0:T(8,128)(2,1)S(1)}, bf16[2,2,2,256,128]{4,3,2,1,0:T(8,128)(2,1)S(1)}, u32[]{:S(2)}, u32[]{:S(2)}) collective-permute-start(bf16[2,2,2,256,128]{4,3,2,1,0:T(8,128)(2,1)S(1)} %pad_maximum_fusion.4.refs_16_), channel_id=1, source_target_pairs={{0,24},{1,25},{2,26},{3,27},{4,28},{5,29},{6,30},{7,31},{8,16},{9,... | collective-permute-start | bytes 1572872 | tf_op jit(solution)/shard_map/ppermute | solution.py:59
  77.9 24.2 %collective-permute-start.18 = (bf16[2,2,2,256,128]{4,3,2,1,0:T(8,128)(2,1)S(1)}, bf16[2,2,2,256,128]{4,3,2,1,0:T(8,128)(2,1)S(1)}, u32[]{:S(2)}, u32[]{:S(2)}) collective-permute-start(bf16[2,2,2,256,128]{4,3,2,1,0:T(8,128)(2,1)S(1)} %pad_maximum_fusion.4.refs_16_), channel_id=1, source_target_pairs={{0,8},{1,9},{2,10},{3,11},{4,12},{5,13},{6,14},{7,15},{8,0},{9,1},... | collective-permute-start | bytes 1572872 | tf_op jit(solution)/shard_map/ppermute | solution.py:59
  79.7 20.1 %collective-permute-start.22 = (bf16[2,2,2,256,128]{4,3,2,1,0:T(8,128)(2,1)S(1)}, bf16[2,2,2,256,128]{4,3,2,1,0:T(8,128)(2,1)S(1)}, u32[]{:S(2)}, u32[]{:S(2)}) collective-permute-start(bf16[2,2,2,256,128]{4,3,2,1,0:T(8,128)(2,1)S(1)} %pad_maximum_fusion.5.refs_20_), channel_id=1, source_target_pairs={{0,24},{1,25},{2,26},{3,27},{4,28},{5,29},{6,30},{7,31},{8,16},{9,... | collective-permute-start | bytes 1572872 | tf_op jit(solution)/shard_map/ppermute | solution.py:59
  85.7 19.4 %collective-permute-start.21 = (bf16[2,2,2,256,128]{4,3,2,1,0:T(8,128)(2,1)S(1)}, bf16[2,2,2,256,128]{4,3,2,1,0:T(8,128)(2,1)S(1)}, u32[]{:S(2)}, u32[]{:S(2)}) collective-permute-start(bf16[2,2,2,256,128]{4,3,2,1,0:T(8,128)(2,1)S(1)} %pad_maximum_fusion.5.refs_20_), channel_id=1, source_target_pairs={{0,8},{1,9},{2,10},{3,11},{4,12},{5,13},{6,14},{7,15},{8,0},{9,1},... | collective-permute-start | bytes 1572872 | tf_op jit(solution)/shard_map/ppermute | solution.py:59
  88.6 16.8 %collective-permute-start.26 = (bf16[2,2,512,128]{3,2,1,0:T(8,128)(2,1)S(1)}, bf16[2,2,512,128]{3,2,1,0:T(8,128)(2,1)S(1)}, u32[]{:S(2)}, u32[]{:S(2)}) collective-permute-start(bf16[2,2,512,128]{3,2,1,0:T(8,128)(2,1)S(1)} %pad_maximum_fusion.6.refs_0_), channel_id=1, source_target_pairs={{0,6},{1,7},{2,4},{3,5},{4,2},{5,3},{6,0},{7,1},{8,14},{9,15},{10,... | collective-permute-start | bytes 1572872 | tf_op jit(solution)/shard_map/ppermute | solution.py:59
  99.8 13.2 %collective-permute-start.25 = (bf16[2,2,512,128]{3,2,1,0:T(8,128)(2,1)S(1)}, bf16[2,2,512,128]{3,2,1,0:T(8,128)(2,1)S(1)}, u32[]{:S(2)}, u32[]{:S(2)}) collective-permute-start(bf16[2,2,512,128]{3,2,1,0:T(8,128)(2,1)S(1)} %pad_maximum_fusion.6.refs_0_), channel_id=1, source_target_pairs={{0,2},{1,3},{2,0},{3,1},{4,6},{5,7},{6,4},{7,5},{8,10},{9,11},{10,... | collective-permute-start | bytes 1572872 | tf_op jit(solution)/shard_map/ppermute | solution.py:59
  99.9 11.0 %collective-permute-start.29 = (bf16[2,2,2,256,128]{4,3,2,1,0:T(8,128)(2,1)S(1)}, bf16[2,2,2,256,128]{4,3,2,1,0:T(8,128)(2,1)S(1)}, u32[]{:S(2)}, u32[]{:S(2)}) collective-permute-start(bf16[2,2,2,256,128]{4,3,2,1,0:T(8,128)(2,1)S(1)} %pad_maximum_fusion.7.refs_12_), channel_id=1, source_target_pairs={{0,24},{1,25},{2,26},{3,27},{4,28},{5,29},{6,30},{7,31},{8,16},{9,... | collective-permute-start | bytes 1572872 | tf_op jit(solution)/shard_map/ppermute | solution.py:59
  102.1 15.1 %collective-permute-start.28 = (bf16[2,2,2,256,128]{4,3,2,1,0:T(8,128)(2,1)S(1)}, bf16[2,2,2,256,128]{4,3,2,1,0:T(8,128)(2,1)S(1)}, u32[]{:S(2)}, u32[]{:S(2)}) collective-permute-start(bf16[2,2,2,256,128]{4,3,2,1,0:T(8,128)(2,1)S(1)} %pad_maximum_fusion.7.refs_12_), channel_id=1, source_target_pairs={{0,8},{1,9},{2,10},{3,11},{4,12},{5,13},{6,14},{7,15},{8,0},{9,1},... | collective-permute-start | bytes 1572872 | tf_op jit(solution)/shard_map/ppermute | solution.py:59
  105.2 14.1 %collective-permute-start.8 = (bf16[2,2,512,128]{3,2,1,0:T(8,128)(2,1)S(1)}, bf16[2,2,512,128]{3,2,1,0:T(8,128)(2,1)S(1)}, u32[]{:S(2)}, u32[]{:S(2)}) collective-permute-start(bf16[2,2,512,128]{3,2,1,0:T(8,128)(2,1)S(1)} %pad_maximum_fusion.1.refs_4_), channel_id=1, source_target_pairs={{0,6},{1,7},{2,4},{3,5},{4,2},{5,3},{6,0},{7,1},{8,14},{9,15},{10,... | collective-permute-start | bytes 1572872 | tf_op jit(solution)/shard_map/ppermute | solution.py:59
  105.4 16.6 %collective-permute-start.7 = (bf16[2,2,512,128]{3,2,1,0:T(8,128)(2,1)S(1)}, bf16[2,2,512,128]{3,2,1,0:T(8,128)(2,1)S(1)}, u32[]{:S(2)}, u32[]{:S(2)}) collective-permute-start(bf16[2,2,512,128]{3,2,1,0:T(8,128)(2,1)S(1)} %pad_maximum_fusion.1.refs_4_), channel_id=1, source_target_pairs={{0,2},{1,3},{2,0},{3,1},{4,6},{5,7},{6,4},{7,5},{8,10},{9,11},{10,... | collective-permute-start | bytes 1572872 | tf_op jit(solution)/shard_map/ppermute | solution.py:59
  110.9 14.3 %collective-permute-start.16 = (bf16[2,2,2,256,128]{4,3,2,1,0:T(8,128)(2,1)S(1)}, bf16[2,2,2,256,128]{4,3,2,1,0:T(8,128)(2,1)S(1)}, u32[]{:S(2)}, u32[]{:S(2)}) collective-permute-start(bf16[2,2,2,256,128]{4,3,2,1,0:T(8,128)(2,1)S(1)} %pad_maximum_fusion.3.refs_12_), channel_id=1, source_target_pairs={{0,24},{1,25},{2,26},{3,27},{4,28},{5,29},{6,30},{7,31},{8,16},{9,... | collective-permute-start | bytes 1572872 | tf_op jit(solution)/shard_map/ppermute | solution.py:59
  113.1 13.8 %collective-permute-start.3 = (bf16[2,2,512,128]{3,2,1,0:T(8,128)(2,1)S(1)}, bf16[2,2,512,128]{3,2,1,0:T(8,128)(2,1)S(1)}, u32[]{:S(2)}, u32[]{:S(2)}) collective-permute-start(bf16[2,2,512,128]{3,2,1,0:T(8,128)(2,1)S(1)} %pad_maximum_fusion.refs_0_), channel_id=1, source_target_pairs={{0,6},{1,7},{2,4},{3,5},{4,2},{5,3},{6,0},{7,1},{8,14},{9,15},{10,... | collective-permute-start | bytes 1572872 | tf_op jit(solution)/shard_map/ppermute | solution.py:59
  117.3 15.6 %collective-permute-start.14 = (bf16[2,2,512,128]{3,2,1,0:T(8,128)(2,1)S(1)}, bf16[2,2,512,128]{3,2,1,0:T(8,128)(2,1)S(1)}, u32[]{:S(2)}, u32[]{:S(2)}) collective-permute-start(bf16[2,2,512,128]{3,2,1,0:T(8,128)(2,1)S(1)} %collective-permute-done.13.refs_10_), channel_id=1, source_target_pairs={{0,2},{1,3},{2,0},{3,1},{4,6},{5,7},{6,4},{7,5},{8,10},{9,11},{10,... | collective-permute-start | bytes 1572872 | tf_op jit(solution)/shard_map/ppermute | solution.py:59
  119.3 14.5 %collective-permute-start.20 = (bf16[2,2,2,256,128]{4,3,2,1,0:T(8,128)(2,1)S(1)}, bf16[2,2,2,256,128]{4,3,2,1,0:T(8,128)(2,1)S(1)}, u32[]{:S(2)}, u32[]{:S(2)}) collective-permute-start(bf16[2,2,2,256,128]{4,3,2,1,0:T(8,128)(2,1)S(1)} %collective-permute-done.19.refs_18_), channel_id=1, source_target_pairs={{0,8},{1,9},{2,10},{3,11},{4,12},{5,13},{6,14},{7,15},{8,0},{9,1},... | collective-permute-start | bytes 1572872 | tf_op jit(solution)/shard_map/ppermute | solution.py:59
  122.0 16.5 %collective-permute-start.23 = (bf16[2,2,2,256,128]{4,3,2,1,0:T(8,128)(2,1)S(1)}, bf16[2,2,2,256,128]{4,3,2,1,0:T(8,128)(2,1)S(1)}, u32[]{:S(2)}, u32[]{:S(2)}) collective-permute-start(bf16[2,2,2,256,128]{4,3,2,1,0:T(8,128)(2,1)S(1)} %collective-permute-done.22.refs_22_), channel_id=1, source_target_pairs={{0,8},{1,9},{2,10},{3,11},{4,12},{5,13},{6,14},{7,15},{8,0},{9,1},... | collective-permute-start | bytes 1572872 | tf_op jit(solution)/shard_map/ppermute | solution.py:59
  125.2 16.2 %collective-permute-start.27 = (bf16[2,2,512,128]{3,2,1,0:T(8,128)(2,1)S(1)}, bf16[2,2,512,128]{3,2,1,0:T(8,128)(2,1)S(1)}, u32[]{:S(2)}, u32[]{:S(2)}) collective-permute-start(bf16[2,2,512,128]{3,2,1,0:T(8,128)(2,1)S(1)} %collective-permute-done.26.refs_2_), channel_id=1, source_target_pairs={{0,2},{1,3},{2,0},{3,1},{4,6},{5,7},{6,4},{7,5},{8,10},{9,11},{10,... | collective-permute-start | bytes 1572872 | tf_op jit(solution)/shard_map/ppermute | solution.py:59
  126.9 17.3 %collective-permute-start.30 = (bf16[2,2,2,256,128]{4,3,2,1,0:T(8,128)(2,1)S(1)}, bf16[2,2,2,256,128]{4,3,2,1,0:T(8,128)(2,1)}, u32[]{:S(2)}, u32[]{:S(2)}) collective-permute-start(bf16[2,2,2,256,128]{4,3,2,1,0:T(8,128)(2,1)S(1)} %collective-permute-done.29.refs_14_), channel_id=1, source_target_pairs={{0,8},{1,9},{2,10},{3,11},{4,12},{5,13},{6,14},{7,15},{8,0},{9,1},... | collective-permute-start | bytes 1572872 | tf_op jit(solution)/shard_map/ppermute | solution.py:59
  132.9 14.2 %collective-permute-start.9 = (bf16[2,2,512,128]{3,2,1,0:T(8,128)(2,1)S(1)}, bf16[2,2,512,128]{3,2,1,0:T(8,128)(2,1)S(1)}, u32[]{:S(2)}, u32[]{:S(2)}) collective-permute-start(bf16[2,2,512,128]{3,2,1,0:T(8,128)(2,1)S(1)} %collective-permute-done.8.refs_6_), channel_id=1, source_target_pairs={{0,2},{1,3},{2,0},{3,1},{4,6},{5,7},{6,4},{7,5},{8,10},{9,11},{10,... | collective-permute-start | bytes 1572872 | tf_op jit(solution)/shard_map/ppermute | solution.py:59
  133.8 23.4 %collective-permute-start.15 = (bf16[2,2,2,256,128]{4,3,2,1,0:T(8,128)(2,1)S(1)}, bf16[2,2,2,256,128]{4,3,2,1,0:T(8,128)(2,1)S(1)}, u32[]{:S(2)}, u32[]{:S(2)}) collective-permute-start(bf16[2,2,2,256,128]{4,3,2,1,0:T(8,128)(2,1)S(1)} %pad_maximum_fusion.3.refs_12_), channel_id=1, source_target_pairs={{0,8},{1,9},{2,10},{3,11},{4,12},{5,13},{6,14},{7,15},{8,0},{9,1},... | collective-permute-start | bytes 1572872 | tf_op jit(solution)/shard_map/ppermute | solution.py:59
  138.5 18.8 %collective-permute-start.2 = (bf16[2,2,512,128]{3,2,1,0:T(8,128)(2,1)S(1)}, bf16[2,2,512,128]{3,2,1,0:T(8,128)(2,1)S(1)}, u32[]{:S(2)}, u32[]{:S(2)}) collective-permute-start(bf16[2,2,512,128]{3,2,1,0:T(8,128)(2,1)S(1)} %pad_maximum_fusion.refs_0_), channel_id=1, source_target_pairs={{0,2},{1,3},{2,0},{3,1},{4,6},{5,7},{6,4},{7,5},{8,10},{9,11},{10,... | collective-permute-start | bytes 1572872 | tf_op jit(solution)/shard_map/ppermute | solution.py:59
  141.3 15.9 %collective-permute-start.17 = (bf16[2,2,2,256,128]{4,3,2,1,0:T(8,128)(2,1)S(1)}, bf16[2,2,2,256,128]{4,3,2,1,0:T(8,128)(2,1)S(1)}, u32[]{:S(2)}, u32[]{:S(2)}) collective-permute-start(bf16[2,2,2,256,128]{4,3,2,1,0:T(8,128)(2,1)S(1)} %collective-permute-done.16.refs_14_), channel_id=1, source_target_pairs={{0,8},{1,9},{2,10},{3,11},{4,12},{5,13},{6,14},{7,15},{8,0},{9,1},... | collective-permute-start | bytes 1572872 | tf_op jit(solution)/shard_map/ppermute | solution.py:59
  144.2 13.1 %collective-permute-start.4 = (bf16[2,2,512,128]{3,2,1,0:T(8,128)(2,1)S(1)}, bf16[2,2,512,128]{3,2,1,0:T(8,128)(2,1)S(1)}, u32[]{:S(2)}, u32[]{:S(2)}) collective-permute-start(bf16[2,2,512,128]{3,2,1,0:T(8,128)(2,1)S(1)} %collective-permute-done.3.refs_2_), channel_id=1, source_target_pairs={{0,2},{1,3},{2,0},{3,1},{4,6},{5,7},{6,4},{7,5},{8,10},{9,11},{10,... | collective-permute-start | bytes 1572872 | tf_op jit(solution)/shard_map/ppermute | solution.py:59
  165.4 12.8 %collective-permute-start.31 = (bf16[2,512,256]{2,1,0:T(8,128)(2,1)S(1)}, bf16[2,512,256]{2,1,0:T(8,128)(2,1)S(1)}, u32[]{:S(2)}, u32[]{:S(2)}) collective-permute-start(bf16[2,512,256]{2,1,0:T(8,128)(2,1)S(1)} %correlate.4), channel_id=1, source_target_pairs={{0,1},{1,0},{2,3},{3,2},{4,5},{5,4},{6,7},{7,6},{8,9},{9,8},{10,11... | collective-permute-start | bytes 1572872 | tf_op jit(solution)/shard_map/ppermute | solution.py:59
  (20 other events, 831.5 us)

commit v2 on v1

v2 whole, which is shorter than its diff:
```python
import functools
import math

import jax
import jax.numpy as jnp
from jax import lax
from jax.experimental import pallas as pl
from jax.experimental.pallas import tpu as pltpu
from jax.sharding import PartitionSpec as P

NFFT = 1024
SAMPLES = 64
WINDOW = 48
K_AUX = 4096
AXES = ("layer", "row", "col")
GROUP = 16
STEP = 64
BF16 = jnp.bfloat16
F32 = jnp.float32


def permutation(dest):
    pairs = []
    for layer in range(4):
        for row in range(4):
            for col in range(8):
                z, core = 2 * (layer // 2) + col % 2, layer % 2
                x, y, z, core2 = dest(row, col // 2, z, core)
                to = ((z // 2) * 2 + core2) * 32 + x * 8 + y * 2 + z % 2
                pairs.append(((layer * 4 + row) * 8 + col, to))
    return pairs


def near(core):
    return 3 if core else 1


def far(core):
    return 1 if core else 3


Y_A = permutation(lambda x, y, z, c: (x, y ^ near(c), z, c))
Y_B = permutation(lambda x, y, z, c: (x, y ^ far(c), z, c))
X_A = permutation(lambda x, y, z, c: (x ^ near(c), y, z, c))
X_B = permutation(lambda x, y, z, c: (x ^ far(c), y, z, c))
SLOTS = [
    permutation(lambda x, y, z, c: (x, y, z, 1 - c)),
    permutation(lambda x, y, z, c: (x, y, z ^ near(c), c)),
    permutation(lambda x, y, z, c: (x, y, z ^ far(c), 1 - c)),
    permutation(lambda x, y, z, c: (x, y, z ^ far(c), c)),
    permutation(lambda x, y, z, c: (x, y, z ^ near(c), 1 - c)),
    permutation(lambda x, y, z, c: (x, y, z ^ 2, c)),
    permutation(lambda x, y, z, c: (x, y, z ^ 2, 1 - c)),
]
HALVES = permutation(lambda x, y, z, c: (x, y, z ^ 1, c))


LANES = (
    ("y1b", "y1f", "y2a"),
    ("y1a", "y2b", "y2f"),
    ("Bza", "Bzb", "Az2", "Bz2"),
    ("Bzbc", "Bzac", "Az2c", "Bz2c"),
    ("xPb", "xPf", "xQa", "xSb", "xSf"),
    ("xPa", "xQb", "xQf", "xSa"),
)
SLOT_NAMES = ("cc", "za", "zbc", "zb", "zac", "z2", "z2c")


def send(value, pairs):
    return lax.ppermute(value, AXES, pairs)


def after(value, *others):
    return lax.optimization_barrier((value,) + others)[0] if others else value


def basis_table(bins):
    lag = jnp.arange(SAMPLES, dtype=jnp.int32)
    taper = 0.5 - 0.5 * jnp.cos(2.0 * math.pi * (lag.astype(F32) + 0.5) / WINDOW)
    clipped = jnp.clip(lag, 0, WINDOW - 1)
    phase = bins[:, None] * clipped[None, :] % NFFT
    angle = 2.0 * math.pi * phase.astype(F32) / NFFT
    weight = jnp.where(lag < WINDOW, taper, 0.0)[None, :]
    both = jnp.stack([weight * jnp.cos(angle), -weight * jnp.sin(angle)], axis=1)
    return both.astype(BF16).reshape(16, SAMPLES)


def lag_rows(offsets):
    tick = jnp.arange(SAMPLES, dtype=jnp.int32)
    lag = tick[None, :, None] - offsets.reshape(-1, 1, GROUP)
    return lag.reshape(-1, 1, SAMPLES * GROUP)


def spectra_kernel(halves, place, table, lags, traces, *refs):
    outs, weights, result, masks = refs[:8], refs[8], refs[9], refs[10]
    step = pl.program_id(0)
    stations = lags.shape[0] * GROUP
    lanes = SAMPLES * GROUP

    @pl.when(step == 0)
    def _():
        lane = lax.broadcasted_iota(jnp.int32, (16, 128), 1) % GROUP
        for n in range(GROUP):
            masks[n] = jnp.where(lane == n, 1.0, 0.0).astype(BF16)

    def build(group):
        lag = lags[pl.ds(step * (STEP // GROUP) + group, 1)].reshape(1, lanes)
        tick = lax.broadcasted_iota(jnp.int32, (SAMPLES, lanes), 0)
        onehot = jnp.where(tick == lag, 1.0, 0.0).astype(BF16)
        basis = jnp.dot(table[...], onehot, preferred_element_type=F32).astype(BF16)
        for n in range(GROUP):
            mask = masks[n]
            for at in range(0, lanes, 128):
                weights[group, pl.ds(n * 16, 16), pl.ds(at, 128)] = basis[:, at:at + 128] * mask

    def multiply(group):
        block = traces[:, pl.ds(group * GROUP, GROUP), :].reshape(lanes, halves * 128)
        spectrum = jnp.dot(weights[group], block, preferred_element_type=F32)
        for half in range(halves):
            result[group, half] = spectrum[:, half * 128:half * 128 + 128]

    def store(group):
        first = step * STEP + group * GROUP
        for slot in range(8):
            for part in range(2):
                picked = pl.ds(slot * 2 + part, GROUP, 16)
                for half in range(halves):
                    base = (half ^ place[0]) * 2 * stations if halves == 2 else 0
                    at = pl.multiple_of(base + part * stations + first, GROUP)
                    outs[slot][pl.ds(at, GROUP), :] = result[group, half, picked, :].astype(BF16)

    groups = STEP // GROUP
    build(0)
    for group in range(groups):
        if group + 1 < groups:
            build(group + 1)
        multiply(group)
        if group:
            store(group - 1)
    store(groups - 1)


def spectra(place, table, lags, traces):
    stations, width = traces.shape[1:]
    rows = 2 * stations * (width // 128)
    whole = lambda *shape: pl.BlockSpec(shape, lambda s, _: (0,) * len(shape))
    return pl.pallas_call(
        functools.partial(spectra_kernel, width // 128),
        grid_spec=pltpu.PrefetchScalarGridSpec(
            num_scalar_prefetch=1,
            grid=(stations // STEP,),
            in_specs=[
                whole(16, SAMPLES),
                whole(*lags.shape),
                pl.BlockSpec((SAMPLES, STEP, width), lambda s, _: (0, s, 0)),
            ],
            out_specs=[whole(rows, 128)] * 8,
            scratch_shapes=[
                pltpu.VMEM((STEP // GROUP, 256, SAMPLES * GROUP), BF16),
                pltpu.VMEM((STEP // GROUP, width // 128, 256, 128), F32),
                pltpu.VMEM((GROUP, 16, 128), BF16),
            ],
        ),
        out_shape=[jax.ShapeDtypeStruct((rows, 128), BF16)] * 8,
        compiler_params=pltpu.CompilerParams(vmem_limit_bytes=48 << 20),
        cost_estimate=pl.CostEstimate(flops=8 << 30, bytes_accessed=10 << 20, transcendentals=0),
        name="spectra",
    )(place, table, lags, traces)


def correlate_kernel(pairs, picks, part_out, has_start, place, *refs):
    a_in, b_in, refs = refs[:4], refs[4:8], refs[8:]
    start, refs = (refs[0], refs[1:]) if has_start else (None, refs)
    out, a_all, b_all, total, a_sems, b_sems = refs
    core = place[1]
    entry = 0 if picks is None else 2 * jnp.where(core == 0, picks[0], picks[1])

    a_copies = [pltpu.make_async_copy(a_in[n], a_all.at[n], a_sems.at[n]) for n in range(4)]
    b_copies = [
        pltpu.make_async_copy(b_in[n].at[pl.ds(entry, 2)], b_all.at[place[6 + n]], b_sems.at[n])
        for n in range(4)
    ]
    for copy in b_copies + a_copies:
        copy.start()
    for copy in b_copies:
        copy.wait()

    scale = 1.0 / K_AUX
    for n in range(4):
        a_copies[n].wait()
        q = place[2 + n]
        for part in range(2):
            right = []
            for z, half in pairs:
                for other in range(2):
                    for p in range(2):
                        piece = b_all[q, other, half, p ^ part]
                        right.append(-piece if part == 1 and p == 0 else piece)
            right = jnp.concatenate(right, axis=1)
            for block in range(2):
                rows = pl.ds(block * 256, 256)
                left = [
                    a_all[n, 2 * z + other, p, rows, :]
                    for z, _ in pairs
                    for other in range(2)
                    for p in range(2)
                ]
                term = lax.dot_general(
                    jnp.concatenate(left, axis=1),
                    right,
                    (((1,), (1,)), ((), ())),
                    preferred_element_type=F32,
                )
                if n > 0:
                    term += total[part, rows, :]
                elif has_start:
                    term += start[part, rows, :]
                if n < 3:
                    total[part, rows, :] = term
                elif part_out == "sum":
                    out[part, rows, :] = term
                elif part_out == "send":
                    out[part, rows, :] = (term * scale).astype(BF16)
                else:
                    out[0, part, rows, :] = term * scale


def correlate(place, a_pieces, b_pieces, pairs, picks, part_out, start=None):
    whole = lambda *shape: pl.BlockSpec(shape, lambda s, _: (0,) * len(shape))
    out, out_spec = jax.ShapeDtypeStruct((2, 512, 256), F32), whole(2, 512, 256)
    if part_out == "send":
        out = jax.ShapeDtypeStruct((2, 512, 256), BF16)
    elif part_out == "keep":
        out = jax.ShapeDtypeStruct((2, 2, 512, 256), F32)
        out_spec = pl.BlockSpec((1, 2, 512, 256), lambda s, place: (place[0], 0, 0, 0))
    starts = [] if start is None else [start]
    return pl.pallas_call(
        functools.partial(correlate_kernel, pairs, picks, part_out, start is not None),
        grid_spec=pltpu.PrefetchScalarGridSpec(
            num_scalar_prefetch=1,
            grid=(1,),
            in_specs=[pl.BlockSpec(memory_space=pl.ANY)] * 8 + [whole(2, 512, 256)] * len(starts),
            out_specs=out_spec,
            scratch_shapes=[
                pltpu.VMEM((4, 4, 2, 512, 128), BF16),
                pltpu.VMEM((4, 2, 2, 2, 256, 128), BF16),
                pltpu.VMEM((2, 512, 256), F32),
                pltpu.SemaphoreType.DMA((4,)),
                pltpu.SemaphoreType.DMA((4,)),
            ],
        ),
        out_shape=out,
        compiler_params=pltpu.CompilerParams(vmem_limit_bytes=20 << 20),
        cost_estimate=pl.CostEstimate(
            flops=(32 if part_out == "send" else 2) << 30, bytes_accessed=6 << 20, transcendentals=0
        ),
        name="correlate",
    )(place, *a_pieces, *b_pieces, *starts)


KEEP = ((0, 0), (1, 1))
SEND = ((0, 1), (1, 0))


def finish_kernel(place, got, whole, out):
    del place, whole
    out[0] = got[...].astype(F32)


def finish(place, got, whole):
    return pl.pallas_call(
        finish_kernel,
        grid_spec=pltpu.PrefetchScalarGridSpec(
            num_scalar_prefetch=1,
            grid=(2,),
            in_specs=[
                pl.BlockSpec((1, 512, 256), lambda s, _: (s, 0, 0)),
                pl.BlockSpec(memory_space=pl.ANY),
            ],
            out_specs=pl.BlockSpec((1, 1, 512, 256), lambda s, place: (1 - place[0], s, 0, 0)),
        ),
        out_shape=jax.ShapeDtypeStruct((2, 2, 512, 256), F32),
        input_output_aliases={2: 0},
        name="finish",
    )(place, got, whole)


def local(traces_rows, traces_cols, offsets_rows, offsets_cols, bins):
    layer, x, col = (lax.axis_index(axis) for axis in AXES)
    y, zl, zh, core = col // 2, col % 2, layer // 2, layer % 2
    z = 2 * zh + zl
    one, three = 1 + 2 * core, 3 - 2 * core
    place = jnp.stack(
        [zl, core, y, y ^ one, y ^ three, y ^ 2, x, x ^ one, x ^ three, x ^ 2]
    ).astype(jnp.int32)

    dests = [
        (z, core), (z, 1 - core), (z ^ one, core), (z ^ three, 1 - core),
        (z ^ three, core), (z ^ one, 1 - core), (z ^ 2, core), (z ^ 2, 1 - core),
    ]
    order = jnp.stack([4 * (a // 2) + 2 * b + a % 2 for a, b in dests])
    picked = jnp.sum(jnp.where(order[:, None] == jnp.arange(8)[None, :], bins[None, :], 0), axis=1)
    table = basis_table(picked)
    a_own, *a_away = spectra(place, table, lag_rows(offsets_rows), traces_rows)
    b_own, *b_away = spectra(after(place, a_own), table, lag_rows(offsets_cols), traces_cols)

    slabs = {"A" + name: slab for name, slab in zip(SLOT_NAMES, a_away)}
    slabs.update({"B" + name: slab for name, slab in zip(SLOT_NAMES, b_away)})
    moves = {array + name: pairs for name, pairs in zip(SLOT_NAMES, SLOTS) for array in "AB"}
    moves.update(ya=Y_A, yb=Y_B, yf=Y_A, xa=X_A, xb=X_B, xf=X_A)
    before = {name: lane[n - 1] for lane in LANES for n, name in enumerate(lane) if n}
    got, chunks = {}, {}

    def build(name):
        axis, which = name
        array, own = ("A", a_own) if axis == "y" else ("B", b_own)
        slots = lambda *names: jnp.stack([arrival(array + n) for n in names])
        if axis == "y":
            q, r = slots("za", "zbc"), slots("zb", "zac")
            if which == "1":
                parts = [own[None], slots("cc"), jnp.where(core == 0, q, r)]
            else:
                parts = [slots("z2", "z2c"), jnp.where(core == 0, r, q)]
            return jnp.concatenate(parts).reshape(4, 2, 512, 128)
        if which == "P":
            parts = [own[None], slots("cc")]
        elif which == "Q":
            parts = [slots("za", "zbc", "zb", "zac")]
        else:
            parts = [slots("z2", "z2c")]
        return jnp.concatenate(parts).reshape(-1, 2, 2, 256, 128)

    def chunk(name):
        if name not in chunks:
            chunks[name] = build(name)
        return chunks[name]

    def arrival(name):
        if name not in got:
            if name in slabs:
                value, move = slabs[name], moves[name]
            else:
                which, way = name[:2], name[2]
                value = arrival(which + "b") if way == "f" else chunk(which)
                move = moves[name[0] + way]
            if name in before:
                value = after(value, arrival(before[name]))
            with jax.named_scope("send_" + name):
                got[name] = send(value, move)
        return got[name]

    pieces = {
        name: [chunk(name)] + [arrival(name + way) for way in "abf"] for name in ("y1", "y2", "xP", "xQ", "xS")
    }
    keep_early = correlate(place, pieces["y1"], pieces["xP"], KEEP, None, "sum")
    send_early = correlate(place, pieces["y1"], pieces["xQ"], SEND, (0, 1), "sum")
    leaves = correlate(place, pieces["y2"], pieces["xQ"], SEND, (1, 0), "send", send_early)
    arrived = send(leaves, HALVES)
    stays = correlate(after(place, leaves), pieces["y2"], pieces["xS"], KEEP, None, "keep", keep_early)
    return finish(place, arrived, stays)


def solution(mesh):
    return jax.shard_map(
        local,
        mesh=mesh,
        in_specs=(
            P(None, "row", ("layer", "col")),
            P(None, "col", ("layer", "row")),
            P("row"),
            P("col"),
            P(),
        ),
        out_specs=P("layer", None, "row", "col"),
        check_vma=False,
    )
```

time: 182 us -> 138 us (0.76)
  waiting for transfers between devices: 67 us -> 43.9 us
  starting transfers between devices: 61.1 us -> 48 us
  Pallas kernels: 46.9 us -> 37.7 us
  other arithmetic: 1.59 us -> 3.84 us
    ppermute x32 -> x30, waiting for transfers between devices: 67 us -> 43.9 us  [send(): return lax.ppermute(value, AXES, pairs)]
    ppermute x32 -> x30, starting transfers between devices: 61.1 us -> 48 us  [send(): return lax.ppermute(value, AXES, pairs)]
    pallas_call x4 -> x6, Pallas kernels: 44.2 us -> 35.1 us  [the longest x2 19.3 us: spectra(): pl.pallas_call(functools.partial(spectra_kernel, width // 128), grid_spec...]
  transfers between devices with their start and end apart: 32 -> 30, of which waited for: 13 -> 11; matrix products, arithmetic and copies ran while one was open for 0% -> 2% of each run, Pallas kernels for 10% -> 17%
where the time goes in v2:
time: 138 us; the launch traced here: 137 us
  starting transfers between devices  48 us (35%)
  waiting for transfers between devices  43.9 us (32%)
  Pallas kernels  37.7 us (27%)
  other arithmetic  3.84 us (3%)
  local copies, waits for them, and re-layouts  3.17 us (2%)
    ppermute x30, starting transfers between devices, send(): return lax.ppermute(value, AXES, pairs)  48 us
    ppermute x30, waiting for transfers between devices, send(): return lax.ppermute(value, AXES, pairs)  43.9 us
    pallas_call x2, Pallas kernels, spectra(): pl.pallas_call(functools.partial(spectra_kernel, width // 128), grid_spec...  19.3 us
    pallas_call x4, Pallas kernels, correlate(): pl.pallas_call(functools.partial(correlate_kernel, pairs, picks, part_out...  15.8 us
  transfers between devices with their start and end apart: 30, of which 11 were waited for; matrix products, arithmetic and copies ran while one was open for 2% of the time, Pallas kernels for 17%

profile of v2, /device:TPU:1, one launch (start us, length us, event | category | flops | bytes accessed | tf_op | source)
XLA Modules:
  0.0 136.9 jit_solution(12824204036191191768)
XLA Ops:
  2.6 11.8 %spectra.2 = (bf16[1024,128]{1,0:T(8,128)(2,1)S(1)}, bf16[1024,128]{1,0:T(8,128)(2,1)S(1)}, bf16[1024,128]{1,0:T(8,128)(2,1)S(1)}, bf16[1024,128]{1,0:T(8,128)(2...) custom-call(s32[10]{0:T(128)S(1)} %stack.128.place, ...), custom_call_target="tpu_custom_call" | custom-call | flops 8589934592 | bytes 10485760 | tf_op jit(solution)/shard_map/spectra/pallas_call | solution.py:147
  14.3 2.5 %collective-permute-start.6 = (bf16[1024,128]{1,0:T(8,128)(2,1)}, bf16[1024,128]{1,0:T(8,128)(2,1)}, u32[]{:S(2)}, u32[]{:S(2)}) collective-permute-start(bf16[1024,128]{1,0:T(8,128)(2,1)} %get-tuple-element.52), channel_id=1, source_target_pairs={{0,65},{1,64},{2,67},{3,66},{4,69},{5,68},{6,71},{7,70},{8,73},{9,... | collective-permute-start | bytes 786440 | tf_op jit(solution)/shard_map/send_Azb/ppermute | solution.py:70
  16.8 2.7 %collective-permute-start.7 = (bf16[1024,128]{1,0:T(8,128)(2,1)}, bf16[1024,128]{1,0:T(8,128)(2,1)}, u32[]{:S(2)}, u32[]{:S(2)}) collective-permute-start(bf16[1024,128]{1,0:T(8,128)(2,1)} %get-tuple-element.53), channel_id=1, source_target_pairs={{0,33},{1,32},{2,35},{3,34},{4,37},{5,36},{6,39},{7,38},{8,41},{9,... | collective-permute-start | bytes 786440 | tf_op jit(solution)/shard_map/send_Azac/ppermute | solution.py:70
  19.5 2.9 %collective-permute-start.8 = (bf16[1024,128]{1,0:T(8,128)(2,1)S(1)}, bf16[1024,128]{1,0:T(8,128)(2,1)}, u32[]{:S(2)}, u32[]{:S(2)}) collective-permute-start(bf16[1024,128]{1,0:T(8,128)(2,1)S(1)} %get-tuple-element.54), channel_id=1, source_target_pairs={{0,1},{1,0},{2,3},{3,2},{4,5},{5,4},{6,7},{7,6},{8,9},{9,8},{10,11... | collective-permute-start | bytes 786440 | tf_op jit(solution)/shard_map/send_Aza/ppermute | solution.py:70
  23.3 7.5 %spectra.3 = (bf16[1024,128]{1,0:T(8,128)(2,1)S(1)}, bf16[1024,128]{1,0:T(8,128)(2,1)S(1)}, bf16[1024,128]{1,0:T(8,128)(2,1)S(1)}, bf16[1024,128]{1,0:T(8,128)(2...) custom-call(s32[10]{0:T(128)S(1)} %stack.128.place, ...), custom_call_target="tpu_custom_call" | custom-call | flops 8589934592 | bytes 10485760 | tf_op jit(solution)/shard_map/spectra/pallas_call | solution.py:147
  31.5 2.6 %collective-permute-start = (bf16[1024,128]{1,0:T(8,128)(2,1)}, bf16[1024,128]{1,0:T(8,128)(2,1)S(1)}, u32[]{:S(2)}, u32[]{:S(2)}) collective-permute-start(bf16[1024,128]{1,0:T(8,128)(2,1)} %copy-done.1), channel_id=1, source_target_pairs={{0,1},{1,0},{2,3},{3,2},{4,5},{5,4},{6,7},{7,6},{8,9},{9,8},{10,11... | collective-permute-start | bytes 786440 | tf_op jit(solution)/shard_map/send_Bza/ppermute | solution.py:70
  36.6 1.4 collective-permute-start.11
  39.8 1.7 %collective-permute-start.1 = (bf16[1024,128]{1,0:T(8,128)(2,1)S(1)}, bf16[1024,128]{1,0:T(8,128)(2,1)S(1)}, u32[]{:S(2)}, u32[]{:S(2)}) collective-permute-start(bf16[1024,128]{1,0:T(8,128)(2,1)S(1)} %get-tuple-element.45), channel_id=1, source_target_pairs={{0,65},{1,64},{2,67},{3,66},{4,69},{5,68},{6,71},{7,70},{8,73},{9,... | collective-permute-start | bytes 786440 | tf_op jit(solution)/shard_map/send_Bzb/ppermute | solution.py:70
  41.6 1.3 collective-permute-start.18
  42.9 2.4 %collective-permute-done.3 = bf16[1024,128]{1,0:T(8,128)(2,1)S(1)} collective-permute-done((bf16[1024,128]{1,0:T(8,128)(2,1)S(1)}, bf16[1024,128]{1,0:T(8,128)(2,1)S(1)}, u32[]{:S(2)}, u32[]{:S(2)}) %collective-permute-start.3) | collective-permute-done | bytes 262176 | tf_op jit(solution)/shard_map/send_Bzbc/ppermute | solution.py:70
  45.2 2.5 %collective-permute-start.21 = (bf16[2,2,2,256,128]{4,3,2,1,0:T(8,128)(2,1)S(1)}, bf16[2,2,2,256,128]{4,3,2,1,0:T(8,128)(2,1)S(1)}, u32[]{:S(2)}, u32[]{:S(2)}) collective-permute-start(bf16[2,2,2,256,128]{4,3,2,1,0:T(8,128)(2,1)S(1)} %pad_maximum_fusion.5.refs_4_), channel_id=1, source_target_pairs={{0,8},{1,9},{2,10},{3,11},{4,12},{5,13},{6,14},{7,15},{8,0},{9,1},... | collective-permute-start | bytes 1572872 | tf_op jit(solution)/shard_map/send_xPa/ppermute | solution.py:70
  48.3 1.8 %collective-permute-start.4 = (bf16[1024,128]{1,0:T(8,128)(2,1)S(1)}, bf16[1024,128]{1,0:T(8,128)(2,1)S(1)}, u32[]{:S(2)}, u32[]{:S(2)}) collective-permute-start(bf16[1024,128]{1,0:T(8,128)(2,1)S(1)} %get-tuple-element.50), channel_id=1, source_target_pairs={{0,33},{1,32},{2,35},{3,34},{4,37},{5,36},{6,39},{7,38},{8,41},{9,... | collective-permute-start | bytes 786440 | tf_op jit(solution)/shard_map/send_Bzac/ppermute | solution.py:70
  50.1 4.3 %collective-permute-done.4 = bf16[1024,128]{1,0:T(8,128)(2,1)S(1)} collective-permute-done((bf16[1024,128]{1,0:T(8,128)(2,1)S(1)}, bf16[1024,128]{1,0:T(8,128)(2,1)S(1)}, u32[]{:S(2)}, u32[]{:S(2)}) %collective-permute-start.4) | collective-permute-done | bytes 262176 | tf_op jit(solution)/shard_map/send_Bzac/ppermute | solution.py:70
  55.7 2.9 %collective-permute-start.5 = (bf16[1024,128]{1,0:T(8,128)(2,1)S(1)}, bf16[1024,128]{1,0:T(8,128)(2,1)S(1)}, u32[]{:S(2)}, u32[]{:S(2)}) collective-permute-start(bf16[1024,128]{1,0:T(8,128)(2,1)S(1)} %get-tuple-element.51), channel_id=1, source_target_pairs={{0,96},{1,97},{2,98},{3,99},{4,100},{5,101},{6,102},{7,103},{8,104... | collective-permute-start | bytes 786440 | tf_op jit(solution)/shard_map/send_Az2c/ppermute | solution.py:70
  58.6 2.5 %collective-permute-start.19 = (bf16[2,2,2,256,128]{4,3,2,1,0:T(8,128)(2,1)S(1)}, bf16[2,2,2,256,128]{4,3,2,1,0:T(8,128)(2,1)S(1)}, u32[]{:S(2)}, u32[]{:S(2)}) collective-permute-start(bf16[2,2,2,256,128]{4,3,2,1,0:T(8,128)(2,1)S(1)} %collective-permute-done.18.refs_6_), channel_id=1, source_target_pairs={{0,8},{1,9},{2,10},{3,11},{4,12},{5,13},{6,14},{7,15},{8,0},{9,1},... | collective-permute-start | bytes 1572872 | tf_op jit(solution)/shard_map/send_xPf/ppermute | solution.py:70
  61.3 1.5 %collective-permute-done.2 = bf16[1024,128]{1,0:T(8,128)(2,1)S(1)} collective-permute-done((bf16[1024,128]{1,0:T(8,128)(2,1)S(1)}, bf16[1024,128]{1,0:T(8,128)(2,1)S(1)}, u32[]{:S(2)}, u32[]{:S(2)}) %collective-permute-start.2) | collective-permute-done | bytes 262176 | tf_op jit(solution)/shard_map/send_Az2/ppermute | solution.py:70
  63.9 5.7 %collective-permute-done.5 = bf16[1024,128]{1,0:T(8,128)(2,1)S(1)} collective-permute-done((bf16[1024,128]{1,0:T(8,128)(2,1)S(1)}, bf16[1024,128]{1,0:T(8,128)(2,1)S(1)}, u32[]{:S(2)}, u32[]{:S(2)}) %collective-permute-start.5) | collective-permute-done | bytes 262176 | tf_op jit(solution)/shard_map/send_Az2c/ppermute | solution.py:70
  69.8 2.6 %collective-permute-start.20 = (bf16[4,2,2,256,128]{4,3,2,1,0:T(8,128)(2,1)S(1)}, bf16[4,2,2,256,128]{4,3,2,1,0:T(8,128)(2,1)S(1)}, u32[]{:S(2)}, u32[]{:S(2)}) collective-permute-start(bf16[4,2,2,256,128]{4,3,2,1,0:T(8,128)(2,1)S(1)} %pad_maximum_fusion.2.refs_4_), channel_id=1, source_target_pairs={{0,8},{1,9},{2,10},{3,11},{4,12},{5,13},{6,14},{7,15},{8,0},{9,1},... | collective-permute-start | bytes 3145736 | tf_op jit(solution)/shard_map/send_xQa/ppermute | solution.py:70
  72.4 1.5 %collective-permute-start.25 = (bf16[1024,128]{1,0:T(8,128)(2,1)S(1)}, bf16[1024,128]{1,0:T(8,128)(2,1)S(1)}, u32[]{:S(2)}, u32[]{:S(2)}) collective-permute-start(bf16[1024,128]{1,0:T(8,128)(2,1)S(1)} %get-tuple-element.69), channel_id=1, source_target_pairs={{0,64},{1,65},{2,66},{3,67},{4,68},{5,69},{6,70},{7,71},{8,72},{9,... | collective-permute-start | bytes 786440 | tf_op jit(solution)/shard_map/send_Bz2/ppermute | solution.py:70
  73.9 8.3 %collective-permute-done.22.refs_6_ = bf16[4,2,2,256,128]{4,3,2,1,0:T(8,128)(2,1)S(1)} collective-permute-done((bf16[4,2,2,256,128]{4,3,2,1,0:T(8,128)(2,1)S(1)}, bf16[4,2,2,256,128]{4,3,2,1,0:T(8,128)(2,1)S(1)}, u32[]{:S(2)}, u32[]{:S(2)}) %collective-permute-start.22) | collective-permute-done | bytes 1048608 | tf_op jit(solution)/shard_map/send_xQb/ppermute | solution.py:70
  83.0 6.9 %collective-permute-start.26 = (bf16[1024,128]{1,0:T(8,128)(2,1)S(1)}, bf16[1024,128]{1,0:T(8,128)(2,1)S(1)}, u32[]{:S(2)}, u32[]{:S(2)}) collective-permute-start(bf16[1024,128]{1,0:T(8,128)(2,1)S(1)} %get-tuple-element.71), channel_id=1, source_target_pairs={{0,96},{1,97},{2,98},{3,99},{4,100},{5,101},{6,102},{7,103},{8,104... | collective-permute-start | bytes 786440 | tf_op jit(solution)/shard_map/send_Bz2c/ppermute | solution.py:70
  89.9 1.9 %collective-permute-done.15.refs_2_ = bf16[4,2,512,128]{3,2,1,0:T(8,128)(2,1)S(1)} collective-permute-done((bf16[4,2,512,128]{3,2,1,0:T(8,128)(2,1)S(1)}, bf16[4,2,512,128]{3,2,1,0:T(8,128)(2,1)S(1)}, u32[]{:S(2)}, u32[]{:S(2)}) %collective-permute-start.15) | collective-permute-done | bytes 1048608 | tf_op jit(solution)/shard_map/send_y2b/ppermute | solution.py:70
  91.8 3.3 %collective-permute-start.13 = (bf16[4,2,512,128]{3,2,1,0:T(8,128)(2,1)S(1)}, bf16[4,2,512,128]{3,2,1,0:T(8,128)(2,1)S(1)}, u32[]{:S(2)}, u32[]{:S(2)}) collective-permute-start(bf16[4,2,512,128]{3,2,1,0:T(8,128)(2,1)S(1)} %pad_maximum_fusion.refs_0_), channel_id=1, source_target_pairs={{0,2},{1,3},{2,0},{3,1},{4,6},{5,7},{6,4},{7,5},{8,10},{9,11},{10,... | collective-permute-start | bytes 3145736 | tf_op jit(solution)/shard_map/send_y2a/ppermute | solution.py:70
  95.9 10.1 %collective-permute-done.28.refs_6_ = bf16[2,2,2,256,128]{4,3,2,1,0:T(8,128)(2,1)S(1)} collective-permute-done((bf16[2,2,2,256,128]{4,3,2,1,0:T(8,128)(2,1)S(1)}, bf16[2,2,2,256,128]{4,3,2,1,0:T(8,128)(2,1)S(1)}, u32[]{:S(2)}, u32[]{:S(2)}) %collective-permute-start.28) | collective-permute-done | bytes 524320 | tf_op jit(solution)/shard_map/send_xSb/ppermute | solution.py:70
  105.9 2.5 %collective-permute-start.29 = (bf16[2,2,2,256,128]{4,3,2,1,0:T(8,128)(2,1)S(1)}, bf16[2,2,2,256,128]{4,3,2,1,0:T(8,128)(2,1)S(1)}, u32[]{:S(2)}, u32[]{:S(2)}) collective-permute-start(bf16[2,2,2,256,128]{4,3,2,1,0:T(8,128)(2,1)S(1)} %collective-permute-done.28.refs_6_), channel_id=1, source_target_pairs={{0,8},{1,9},{2,10},{3,11},{4,12},{5,13},{6,14},{7,15},{8,0},{9,1},... | collective-permute-start | bytes 1572872 | tf_op jit(solution)/shard_map/send_xSf/ppermute | solution.py:70
  108.6 3.7 %correlate.4.refs_8_ = f32[2,512,256]{2,1,0:T(8,128)S(1)} custom-call(s32[10]{0:T(128)S(1)} %stack.128.place, bf16[4,2,512,128]{3,2,1,0:T(8,128)(2,1)S(1)} %pad_maximum_fusion.1.refs_0_, bf16[4,2,512,128]{3,2,1,0:T(8,128)(2,1)S(1)} %collective-permute-done.14.refs_1_, bf16[4,2,512,128]{3,2,1,0:T(8,128)(2,1)S(1)} %collective-permute-done.11.refs_2_, ...), custom_call_target="tpu_custom_call" | custom-call | flops 2147483648 | bytes 6291456 | tf_op jit(solution)/shard_map/correlate/pallas_call | solution.py:237
  112.3 6.2 %collective-permute-done.16.refs_3_ = bf16[4,2,512,128]{3,2,1,0:T(8,128)(2,1)S(1)} collective-permute-done((bf16[4,2,512,128]{3,2,1,0:T(8,128)(2,1)S(1)}, bf16[4,2,512,128]{3,2,1,0:T(8,128)(2,1)S(1)}, u32[]{:S(2)}, u32[]{:S(2)}) %collective-permute-start.16) | collective-permute-done | bytes 1048608 | tf_op jit(solution)/shard_map/send_y2f/ppermute | solution.py:70
  118.5 3.7 %correlate.5 = bf16[2,512,256]{2,1,0:T(8,128)(2,1)S(1)} custom-call(s32[10]{0:T(128)S(1)} %stack.128.place, bf16[4,2,512,128]{3,2,1,0:T(8,128)(2,1)S(1)} %pad_maximum_fusion.refs_0_, bf16[4,2,512,128]{3,2,1,0:T(8,128)(2,1)S(1)} %collective-permute-done.13.refs_1_, bf16[4,2,512,128]{3,2,1,0:T(8,128)(2,1)S(1)} %collective-permute-done.15.refs_2_, ...), custom_call_target="tpu_custom_call" | custom-call | flops 34359738368 | bytes 6291456 | tf_op jit(solution)/shard_map/correlate/pallas_call | solution.py:237
  122.4 3.7 %correlate.6.refs_8_ = f32[2,512,256]{2,1,0:T(8,128)S(1)} custom-call(s32[10]{0:T(128)S(1)} %stack.128.place, bf16[4,2,512,128]{3,2,1,0:T(8,128)(2,1)S(1)} %pad_maximum_fusion.1.refs_0_, bf16[4,2,512,128]{3,2,1,0:T(8,128)(2,1)S(1)} %collective-permute-done.14.refs_1_, bf16[4,2,512,128]{3,2,1,0:T(8,128)(2,1)S(1)} %collective-permute-done.11.refs_2_, ...), custom_call_target="tpu_custom_call" | custom-call | flops 2147483648 | bytes 6291456 | tf_op jit(solution)/shard_map/correlate/pallas_call | solution.py:237
  126.1 4.7 %correlate.7.whole = f32[2,2,512,256]{3,2,1,0:T(8,128)} custom-call(s32[10]{0:T(128)S(1)} %stack.128.place, bf16[4,2,512,128]{3,2,1,0:T(8,128)(2,1)S(1)} %pad_maximum_fusion.refs_0_, bf16[4,2,512,128]{3,2,1,0:T(8,128)(2,1)S(1)} %collective-permute-done.13.refs_1_, bf16[4,2,512,128]{3,2,1,0:T(8,128)(2,1)S(1)} %collective-permute-done.15.refs_2_, ...), custom_call_target="tpu_custom_call" | custom-call | flops 2147483648 | bytes 6291456 | tf_op jit(solution)/shard_map/correlate/pallas_call | solution.py:237
  130.8 2.7 %collective-permute-done.24.got = bf16[2,512,256]{2,1,0:T(8,128)(2,1)S(1)} collective-permute-done((bf16[2,512,256]{2,1,0:T(8,128)(2,1)S(1)}, bf16[2,512,256]{2,1,0:T(8,128)(2,1)S(1)}, u32[]{:S(2)}, u32[]{:S(2)}) %collective-permute-start.24) | collective-permute-done | bytes 524320 | tf_op jit(solution)/shard_map/ppermute | solution.py:70
  134.3 2.6 %finish.1 = f32[2,2,512,256]{3,2,1,0:T(8,128)} custom-call(s32[10]{0:T(128)} %copy-done, bf16[2,512,256]{2,1,0:T(8,128)(2,1)} %copy-done.2, f32[2,2,512,256]{3,2,1,0:T(8,128)} %correlate.7.whole), custom_call_target="tpu_custom_call", output_to_operand_aliasing={{}: (2, {})} | custom-call | tf_op jit(solution)/shard_map/finish/pallas_call | solution.py:271
  (68 shorter events, 14.3 us)
Async XLA Ops:
  2.5 123.6 %copy-start = (s32[10]{0:T(128)}, s32[10]{0:T(128)S(1)}, u32[]{:S(2)}) copy-start(s32[10]{0:T(128)S(1)} %stack.128.place) | copy-start | bytes 124
  2.5 20.3 %copy-start.3 = (s32[256]{0:T(256)S(1)}, s32[256]{0:T(256)}, u32[]{:S(2)}) copy-start(s32[256]{0:T(256)} %param.8) | copy-start | bytes 3076
  14.3 17.2 %collective-permute-start.6 = (bf16[1024,128]{1,0:T(8,128)(2,1)}, bf16[1024,128]{1,0:T(8,128)(2,1)}, u32[]{:S(2)}, u32[]{:S(2)}) collective-permute-start(bf16[1024,128]{1,0:T(8,128)(2,1)} %get-tuple-element.52), channel_id=1, source_target_pairs={{0,65},{1,64},{2,67},{3,66},{4,69},{5,68},{6,71},{7,70},{8,73},{9,... | collective-permute-start | bytes 786440 | tf_op jit(solution)/shard_map/send_Azb/ppermute | solution.py:70
  16.8 17.4 %collective-permute-start.7 = (bf16[1024,128]{1,0:T(8,128)(2,1)}, bf16[1024,128]{1,0:T(8,128)(2,1)}, u32[]{:S(2)}, u32[]{:S(2)}) collective-permute-start(bf16[1024,128]{1,0:T(8,128)(2,1)} %get-tuple-element.53), channel_id=1, source_target_pairs={{0,33},{1,32},{2,35},{3,34},{4,37},{5,36},{6,39},{7,38},{8,41},{9,... | collective-permute-start | bytes 786440 | tf_op jit(solution)/shard_map/send_Azac/ppermute | solution.py:70
  19.5 14.7 %collective-permute-start.8 = (bf16[1024,128]{1,0:T(8,128)(2,1)S(1)}, bf16[1024,128]{1,0:T(8,128)(2,1)}, u32[]{:S(2)}, u32[]{:S(2)}) collective-permute-start(bf16[1024,128]{1,0:T(8,128)(2,1)S(1)} %get-tuple-element.54), channel_id=1, source_target_pairs={{0,1},{1,0},{2,3},{3,2},{4,5},{5,4},{6,7},{7,6},{8,9},{9,8},{10,11... | collective-permute-start | bytes 786440 | tf_op jit(solution)/shard_map/send_Aza/ppermute | solution.py:70
  22.4 11.8 %collective-permute-start.9 = (bf16[1024,128]{1,0:T(8,128)(2,1)S(1)}, bf16[1024,128]{1,0:T(8,128)(2,1)}, u32[]{:S(2)}, u32[]{:S(2)}) collective-permute-start(bf16[1024,128]{1,0:T(8,128)(2,1)S(1)} %get-tuple-element.55), channel_id=1, source_target_pairs={{0,97},{1,96},{2,99},{3,98},{4,101},{5,100},{6,103},{7,102},{8,105... | collective-permute-start | bytes 786440 | tf_op jit(solution)/shard_map/send_Azbc/ppermute | solution.py:70
  22.4 13.1 %collective-permute-start.10 = (bf16[1024,128]{1,0:T(8,128)(2,1)S(1)}, bf16[1024,128]{1,0:T(8,128)(2,1)}, u32[]{:S(2)}, u32[]{:S(2)}) collective-permute-start(bf16[1024,128]{1,0:T(8,128)(2,1)S(1)} %get-tuple-element.56), channel_id=1, source_target_pairs={{0,32},{1,33},{2,34},{3,35},{4,36},{5,37},{6,38},{7,39},{8,40},{9,... | collective-permute-start | bytes 786440 | tf_op jit(solution)/shard_map/send_Acc/ppermute | solution.py:70
  31.5 8.3 %collective-permute-start = (bf16[1024,128]{1,0:T(8,128)(2,1)}, bf16[1024,128]{1,0:T(8,128)(2,1)S(1)}, u32[]{:S(2)}, u32[]{:S(2)}) collective-permute-start(bf16[1024,128]{1,0:T(8,128)(2,1)} %copy-done.1), channel_id=1, source_target_pairs={{0,1},{1,0},{2,3},{3,2},{4,5},{5,4},{6,7},{7,6},{8,9},{9,8},{10,11... | collective-permute-start | bytes 786440 | tf_op jit(solution)/shard_map/send_Bza/ppermute | solution.py:70
  34.2 7.3 %collective-permute-start.17 = (bf16[1024,128]{1,0:T(8,128)(2,1)S(1)}, bf16[1024,128]{1,0:T(8,128)(2,1)S(1)}, u32[]{:S(2)}, u32[]{:S(2)}) collective-permute-start(bf16[1024,128]{1,0:T(8,128)(2,1)S(1)} %get-tuple-element.62), channel_id=1, source_target_pairs={{0,32},{1,33},{2,34},{3,35},{4,36},{5,37},{6,38},{7,39},{8,40},{9,... | collective-permute-start | bytes 786440 | tf_op jit(solution)/shard_map/send_Bcc/ppermute | solution.py:70
  36.6 24.6 %collective-permute-start.11 = (bf16[4,2,512,128]{3,2,1,0:T(8,128)(2,1)S(1)}, bf16[4,2,512,128]{3,2,1,0:T(8,128)(2,1)S(1)}, u32[]{:S(2)}, u32[]{:S(2)}) collective-permute-start(bf16[4,2,512,128]{3,2,1,0:T(8,128)(2,1)S(1)} %pad_maximum_fusion.1.refs_0_), channel_id=1, source_target_pairs={{0,6},{1,7},{2,4},{3,5},{4,2},{5,3},{6,0},{7,1},{8,14},{9,15},{10,... | collective-permute-start | bytes 3145736 | tf_op jit(solution)/shard_map/send_y1b/ppermute | solution.py:70
  37.9 7.3 %collective-permute-start.3 = (bf16[1024,128]{1,0:T(8,128)(2,1)S(1)}, bf16[1024,128]{1,0:T(8,128)(2,1)S(1)}, u32[]{:S(2)}, u32[]{:S(2)}) collective-permute-start(bf16[1024,128]{1,0:T(8,128)(2,1)S(1)} %get-tuple-element.49), channel_id=1, source_target_pairs={{0,97},{1,96},{2,99},{3,98},{4,101},{5,100},{6,103},{7,102},{8,105... | collective-permute-start | bytes 786440 | tf_op jit(solution)/shard_map/send_Bzbc/ppermute | solution.py:70
  38.7 31.0 %collective-permute-start.14 = (bf16[4,2,512,128]{3,2,1,0:T(8,128)(2,1)S(1)}, bf16[4,2,512,128]{3,2,1,0:T(8,128)(2,1)S(1)}, u32[]{:S(2)}, u32[]{:S(2)}) collective-permute-start(bf16[4,2,512,128]{3,2,1,0:T(8,128)(2,1)S(1)} %pad_maximum_fusion.1.refs_0_), channel_id=1, source_target_pairs={{0,2},{1,3},{2,0},{3,1},{4,6},{5,7},{6,4},{7,5},{8,10},{9,11},{10,... | collective-permute-start | bytes 3145736 | tf_op jit(solution)/shard_map/send_y1a/ppermute | solution.py:70
  39.8 8.5 %collective-permute-start.1 = (bf16[1024,128]{1,0:T(8,128)(2,1)S(1)}, bf16[1024,128]{1,0:T(8,128)(2,1)S(1)}, u32[]{:S(2)}, u32[]{:S(2)}) collective-permute-start(bf16[1024,128]{1,0:T(8,128)(2,1)S(1)} %get-tuple-element.45), channel_id=1, source_target_pairs={{0,65},{1,64},{2,67},{3,66},{4,69},{5,68},{6,71},{7,70},{8,73},{9,... | collective-permute-start | bytes 786440 | tf_op jit(solution)/shard_map/send_Bzb/ppermute | solution.py:70
  41.6 14.1 %collective-permute-start.18 = (bf16[2,2,2,256,128]{4,3,2,1,0:T(8,128)(2,1)S(1)}, bf16[2,2,2,256,128]{4,3,2,1,0:T(8,128)(2,1)S(1)}, u32[]{:S(2)}, u32[]{:S(2)}) collective-permute-start(bf16[2,2,2,256,128]{4,3,2,1,0:T(8,128)(2,1)S(1)} %pad_maximum_fusion.5.refs_4_), channel_id=1, source_target_pairs={{0,24},{1,25},{2,26},{3,27},{4,28},{5,29},{6,30},{7,31},{8,16},{9,... | collective-permute-start | bytes 1572872 | tf_op jit(solution)/shard_map/send_xPb/ppermute | solution.py:70
  45.2 13.4 %collective-permute-start.21 = (bf16[2,2,2,256,128]{4,3,2,1,0:T(8,128)(2,1)S(1)}, bf16[2,2,2,256,128]{4,3,2,1,0:T(8,128)(2,1)S(1)}, u32[]{:S(2)}, u32[]{:S(2)}) collective-permute-start(bf16[2,2,2,256,128]{4,3,2,1,0:T(8,128)(2,1)S(1)} %pad_maximum_fusion.5.refs_4_), channel_id=1, source_target_pairs={{0,8},{1,9},{2,10},{3,11},{4,12},{5,13},{6,14},{7,15},{8,0},{9,1},... | collective-permute-start | bytes 1572872 | tf_op jit(solution)/shard_map/send_xPa/ppermute | solution.py:70
  48.3 6.1 %collective-permute-start.4 = (bf16[1024,128]{1,0:T(8,128)(2,1)S(1)}, bf16[1024,128]{1,0:T(8,128)(2,1)S(1)}, u32[]{:S(2)}, u32[]{:S(2)}) collective-permute-start(bf16[1024,128]{1,0:T(8,128)(2,1)S(1)} %get-tuple-element.50), channel_id=1, source_target_pairs={{0,33},{1,32},{2,35},{3,34},{4,37},{5,36},{6,39},{7,38},{8,41},{9,... | collective-permute-start | bytes 786440 | tf_op jit(solution)/shard_map/send_Bzac/ppermute | solution.py:70
  54.4 8.3 %collective-permute-start.2 = (bf16[1024,128]{1,0:T(8,128)(2,1)S(1)}, bf16[1024,128]{1,0:T(8,128)(2,1)S(1)}, u32[]{:S(2)}, u32[]{:S(2)}) collective-permute-start(bf16[1024,128]{1,0:T(8,128)(2,1)S(1)} %get-tuple-element.46), channel_id=1, source_target_pairs={{0,64},{1,65},{2,66},{3,67},{4,68},{5,69},{6,70},{7,71},{8,72},{9,... | collective-permute-start | bytes 786440 | tf_op jit(solution)/shard_map/send_Az2/ppermute | solution.py:70
  55.7 13.9 %collective-permute-start.5 = (bf16[1024,128]{1,0:T(8,128)(2,1)S(1)}, bf16[1024,128]{1,0:T(8,128)(2,1)S(1)}, u32[]{:S(2)}, u32[]{:S(2)}) collective-permute-start(bf16[1024,128]{1,0:T(8,128)(2,1)S(1)} %get-tuple-element.51), channel_id=1, source_target_pairs={{0,96},{1,97},{2,98},{3,99},{4,100},{5,101},{6,102},{7,103},{8,104... | collective-permute-start | bytes 786440 | tf_op jit(solution)/shard_map/send_Az2c/ppermute | solution.py:70
  58.6 11.2 %collective-permute-start.19 = (bf16[2,2,2,256,128]{4,3,2,1,0:T(8,128)(2,1)S(1)}, bf16[2,2,2,256,128]{4,3,2,1,0:T(8,128)(2,1)S(1)}, u32[]{:S(2)}, u32[]{:S(2)}) collective-permute-start(bf16[2,2,2,256,128]{4,3,2,1,0:T(8,128)(2,1)S(1)} %collective-permute-done.18.refs_6_), channel_id=1, source_target_pairs={{0,8},{1,9},{2,10},{3,11},{4,12},{5,13},{6,14},{7,15},{8,0},{9,1},... | collective-permute-start | bytes 1572872 | tf_op jit(solution)/shard_map/send_xPf/ppermute | solution.py:70
  61.2 21.0 %collective-permute-start.22 = (bf16[4,2,2,256,128]{4,3,2,1,0:T(8,128)(2,1)S(1)}, bf16[4,2,2,256,128]{4,3,2,1,0:T(8,128)(2,1)S(1)}, u32[]{:S(2)}, u32[]{:S(2)}) collective-permute-start(bf16[4,2,2,256,128]{4,3,2,1,0:T(8,128)(2,1)S(1)} %pad_maximum_fusion.2.refs_4_), channel_id=1, source_target_pairs={{0,24},{1,25},{2,26},{3,27},{4,28},{5,29},{6,30},{7,31},{8,16},{9,... | collective-permute-start | bytes 3145736 | tf_op jit(solution)/shard_map/send_xQb/ppermute | solution.py:70
  62.8 20.2 %collective-permute-start.12 = (bf16[4,2,512,128]{3,2,1,0:T(8,128)(2,1)S(1)}, bf16[4,2,512,128]{3,2,1,0:T(8,128)(2,1)S(1)}, u32[]{:S(2)}, u32[]{:S(2)}) collective-permute-start(bf16[4,2,512,128]{3,2,1,0:T(8,128)(2,1)S(1)} %collective-permute-done.11.refs_2_), channel_id=1, source_target_pairs={{0,2},{1,3},{2,0},{3,1},{4,6},{5,7},{6,4},{7,5},{8,10},{9,11},{10,... | collective-permute-start | bytes 3145736 | tf_op jit(solution)/shard_map/send_y1f/ppermute | solution.py:70
  69.7 22.1 %collective-permute-start.15 = (bf16[4,2,512,128]{3,2,1,0:T(8,128)(2,1)S(1)}, bf16[4,2,512,128]{3,2,1,0:T(8,128)(2,1)S(1)}, u32[]{:S(2)}, u32[]{:S(2)}) collective-permute-start(bf16[4,2,512,128]{3,2,1,0:T(8,128)(2,1)S(1)} %pad_maximum_fusion.refs_0_), channel_id=1, source_target_pairs={{0,6},{1,7},{2,4},{3,5},{4,2},{5,3},{6,0},{7,1},{8,14},{9,15},{10,... | collective-permute-start | bytes 3145736 | tf_op jit(solution)/shard_map/send_y2b/ppermute | solution.py:70
  69.8 25.6 %collective-permute-start.20 = (bf16[4,2,2,256,128]{4,3,2,1,0:T(8,128)(2,1)S(1)}, bf16[4,2,2,256,128]{4,3,2,1,0:T(8,128)(2,1)S(1)}, u32[]{:S(2)}, u32[]{:S(2)}) collective-permute-start(bf16[4,2,2,256,128]{4,3,2,1,0:T(8,128)(2,1)S(1)} %pad_maximum_fusion.2.refs_4_), channel_id=1, source_target_pairs={{0,8},{1,9},{2,10},{3,11},{4,12},{5,13},{6,14},{7,15},{8,0},{9,1},... | collective-permute-start | bytes 3145736 | tf_op jit(solution)/shard_map/send_xQa/ppermute | solution.py:70
  72.4 22.8 %collective-permute-start.25 = (bf16[1024,128]{1,0:T(8,128)(2,1)S(1)}, bf16[1024,128]{1,0:T(8,128)(2,1)S(1)}, u32[]{:S(2)}, u32[]{:S(2)}) collective-permute-start(bf16[1024,128]{1,0:T(8,128)(2,1)S(1)} %get-tuple-element.69), channel_id=1, source_target_pairs={{0,64},{1,65},{2,66},{3,67},{4,68},{5,69},{6,70},{7,71},{8,72},{9,... | collective-permute-start | bytes 786440 | tf_op jit(solution)/shard_map/send_Bz2/ppermute | solution.py:70
  82.2 26.2 %collective-permute-start.23 = (bf16[4,2,2,256,128]{4,3,2,1,0:T(8,128)(2,1)S(1)}, bf16[4,2,2,256,128]{4,3,2,1,0:T(8,128)(2,1)S(1)}, u32[]{:S(2)}, u32[]{:S(2)}) collective-permute-start(bf16[4,2,2,256,128]{4,3,2,1,0:T(8,128)(2,1)S(1)} %collective-permute-done.22.refs_6_), channel_id=1, source_target_pairs={{0,8},{1,9},{2,10},{3,11},{4,12},{5,13},{6,14},{7,15},{8,0},{9,1},... | collective-permute-start | bytes 3145736 | tf_op jit(solution)/shard_map/send_xQf/ppermute | solution.py:70
  83.0 12.4 %collective-permute-start.26 = (bf16[1024,128]{1,0:T(8,128)(2,1)S(1)}, bf16[1024,128]{1,0:T(8,128)(2,1)S(1)}, u32[]{:S(2)}, u32[]{:S(2)}) collective-permute-start(bf16[1024,128]{1,0:T(8,128)(2,1)S(1)} %get-tuple-element.71), channel_id=1, source_target_pairs={{0,96},{1,97},{2,98},{3,99},{4,100},{5,101},{6,102},{7,103},{8,104... | collective-permute-start | bytes 786440 | tf_op jit(solution)/shard_map/send_Bz2c/ppermute | solution.py:70
  91.8 20.5 %collective-permute-start.13 = (bf16[4,2,512,128]{3,2,1,0:T(8,128)(2,1)S(1)}, bf16[4,2,512,128]{3,2,1,0:T(8,128)(2,1)S(1)}, u32[]{:S(2)}, u32[]{:S(2)}) collective-permute-start(bf16[4,2,512,128]{3,2,1,0:T(8,128)(2,1)S(1)} %pad_maximum_fusion.refs_0_), channel_id=1, source_target_pairs={{0,2},{1,3},{2,0},{3,1},{4,6},{5,7},{6,4},{7,5},{8,10},{9,11},{10,... | collective-permute-start | bytes 3145736 | tf_op jit(solution)/shard_map/send_y2a/ppermute | solution.py:70
  95.1 23.4 %collective-permute-start.16 = (bf16[4,2,512,128]{3,2,1,0:T(8,128)(2,1)S(1)}, bf16[4,2,512,128]{3,2,1,0:T(8,128)(2,1)S(1)}, u32[]{:S(2)}, u32[]{:S(2)}) collective-permute-start(bf16[4,2,512,128]{3,2,1,0:T(8,128)(2,1)S(1)} %collective-permute-done.15.refs_2_), channel_id=1, source_target_pairs={{0,2},{1,3},{2,0},{3,1},{4,6},{5,7},{6,4},{7,5},{8,10},{9,11},{10,... | collective-permute-start | bytes 3145736 | tf_op jit(solution)/shard_map/send_y2f/ppermute | solution.py:70
  95.4 10.5 %collective-permute-start.28 = (bf16[2,2,2,256,128]{4,3,2,1,0:T(8,128)(2,1)S(1)}, bf16[2,2,2,256,128]{4,3,2,1,0:T(8,128)(2,1)S(1)}, u32[]{:S(2)}, u32[]{:S(2)}) collective-permute-start(bf16[2,2,2,256,128]{4,3,2,1,0:T(8,128)(2,1)S(1)} %pad_maximum_fusion.6.refs_4_), channel_id=1, source_target_pairs={{0,24},{1,25},{2,26},{3,27},{4,28},{5,29},{6,30},{7,31},{8,16},{9,... | collective-permute-start | bytes 1572872 | tf_op jit(solution)/shard_map/send_xSb/ppermute | solution.py:70
  105.9 20.2 %collective-permute-start.29 = (bf16[2,2,2,256,128]{4,3,2,1,0:T(8,128)(2,1)S(1)}, bf16[2,2,2,256,128]{4,3,2,1,0:T(8,128)(2,1)S(1)}, u32[]{:S(2)}, u32[]{:S(2)}) collective-permute-start(bf16[2,2,2,256,128]{4,3,2,1,0:T(8,128)(2,1)S(1)} %collective-permute-done.28.refs_6_), channel_id=1, source_target_pairs={{0,8},{1,9},{2,10},{3,11},{4,12},{5,13},{6,14},{7,15},{8,0},{9,1},... | collective-permute-start | bytes 1572872 | tf_op jit(solution)/shard_map/send_xSf/ppermute | solution.py:70
  108.4 17.7 %collective-permute-start.27 = (bf16[2,2,2,256,128]{4,3,2,1,0:T(8,128)(2,1)S(1)}, bf16[2,2,2,256,128]{4,3,2,1,0:T(8,128)(2,1)S(1)}, u32[]{:S(2)}, u32[]{:S(2)}) collective-permute-start(bf16[2,2,2,256,128]{4,3,2,1,0:T(8,128)(2,1)S(1)} %pad_maximum_fusion.6.refs_4_), channel_id=1, source_target_pairs={{0,8},{1,9},{2,10},{3,11},{4,12},{5,13},{6,14},{7,15},{8,0},{9,1},... | collective-permute-start | bytes 1572872 | tf_op jit(solution)/shard_map/send_xSa/ppermute | solution.py:70
  122.3 11.2 %collective-permute-start.24 = (bf16[2,512,256]{2,1,0:T(8,128)(2,1)S(1)}, bf16[2,512,256]{2,1,0:T(8,128)(2,1)S(1)}, u32[]{:S(2)}, u32[]{:S(2)}) collective-permute-start(bf16[2,512,256]{2,1,0:T(8,128)(2,1)S(1)} %correlate.5), channel_id=1, source_target_pairs={{0,1},{1,0},{2,3},{3,2},{4,5},{5,4},{6,7},{7,6},{8,9},{9,8},{10,11... | collective-permute-start | bytes 1572872 | tf_op jit(solution)/shard_map/ppermute | solution.py:70
  (2 other events, 1.5 us)

commit v3 on v2

--- a/solution.py
+++ b/solution.py
@@ -14,6 +14,7 @@
 K_AUX = 4096
 AXES = ("layer", "row", "col")
 GROUP = 16
+SUB = 8
 STEP = 64
 BF16 = jnp.bfloat16
 F32 = jnp.float32
@@ -87,37 +88,40 @@
 
 def lag_rows(offsets):
     tick = jnp.arange(SAMPLES, dtype=jnp.int32)
-    lag = tick[None, :, None] - offsets.reshape(-1, 1, GROUP)
-    return lag.reshape(-1, 1, SAMPLES * GROUP)
+    lag = tick[None, :, None] - offsets.reshape(-1, 1, SUB)
+    return lag.reshape(-1, 1, SAMPLES * SUB)
 
 
 def spectra_kernel(halves, place, table, lags, traces, *refs):
     outs, weights, result, masks = refs[:8], refs[8], refs[9], refs[10]
     step = pl.program_id(0)
-    stations = lags.shape[0] * GROUP
-    lanes = SAMPLES * GROUP
+    stations = lags.shape[0] * SUB
+    lanes = SAMPLES * SUB
 
     @pl.when(step == 0)
     def _():
-        lane = lax.broadcasted_iota(jnp.int32, (16, 128), 1) % GROUP
-        for n in range(GROUP):
+        lane = lax.broadcasted_iota(jnp.int32, (16, 128), 1) % SUB
+        for n in range(SUB):
             masks[n] = jnp.where(lane == n, 1.0, 0.0).astype(BF16)
 
     def build(group):
-        lag = lags[pl.ds(step * (STEP // GROUP) + group, 1)].reshape(1, lanes)
         tick = lax.broadcasted_iota(jnp.int32, (SAMPLES, lanes), 0)
-        onehot = jnp.where(tick == lag, 1.0, 0.0).astype(BF16)
-        basis = jnp.dot(table[...], onehot, preferred_element_type=F32).astype(BF16)
-        for n in range(GROUP):
-            mask = masks[n]
-            for at in range(0, lanes, 128):
-                weights[group, pl.ds(n * 16, 16), pl.ds(at, 128)] = basis[:, at:at + 128] * mask
+        for sub in range(GROUP // SUB):
+            lag = lags[pl.ds(step * (STEP // SUB) + group * (GROUP // SUB) + sub, 1)].reshape(1, lanes)
+            onehot = jnp.where(tick == lag, 1.0, 0.0).astype(BF16)
+            basis = jnp.dot(table[...], onehot, preferred_element_type=F32).astype(BF16)
+            for n in range(SUB):
+                mask = masks[n]
+                for at in range(0, lanes, 128):
+                    weights[group, sub, pl.ds(n * 16, 16), pl.ds(at, 128)] = basis[:, at:at + 128] * mask
 
     def multiply(group):
-        block = traces[:, pl.ds(group * GROUP, GROUP), :].reshape(lanes, halves * 128)
-        spectrum = jnp.dot(weights[group], block, preferred_element_type=F32)
-        for half in range(halves):
-            result[group, half] = spectrum[:, half * 128:half * 128 + 128]
+        block = traces[:, pl.ds(group * GROUP, GROUP), :].astype(F32)
+        for sub in range(GROUP // SUB):
+            part = block[:, sub * SUB:(sub + 1) * SUB, :].reshape(lanes, halves * 128).astype(BF16)
+            spectrum = jnp.dot(weights[group, sub], part, preferred_element_type=F32)
+            for half in range(halves):
+                result[group, half, pl.ds(sub * 128, 128), :] = spectrum[:, half * 128:half * 128 + 128]
 
     def store(group):
         first = step * STEP + group * GROUP
@@ -156,9 +160,9 @@
             ],
             out_specs=[whole(rows, 128)] * 8,
             scratch_shapes=[
-                pltpu.VMEM((STEP // GROUP, 256, SAMPLES * GROUP), BF16),
+                pltpu.VMEM((STEP // GROUP, GROUP // SUB, SUB * 16, SAMPLES * SUB), BF16),
                 pltpu.VMEM((STEP // GROUP, width // 128, 256, 128), F32),
-                pltpu.VMEM((GROUP, 16, 128), BF16),
+                pltpu.VMEM((SUB, 16, 128), BF16),
             ],
         ),
         out_shape=[jax.ShapeDtypeStruct((rows, 128), BF16)] * 8,
@@ -262,27 +266,34 @@
 SEND = ((0, 1), (1, 0))
 
 
-def finish_kernel(place, got, whole, out):
-    del place, whole
-    out[0] = got[...].astype(F32)
-
-
-def finish(place, got, whole):
+def finish_kernel(got, whole, out, wide, sems):
+    del whole
+    slot = 1 - lax.axis_index("col") % 2
+    copies = []
+    for part in range(2):
+        for half in range(2):
+            rows = pl.ds(half * 256, 256)
+            wide[part, rows, :] = got[part, rows, :].astype(F32)
+            copies.append(
+                pltpu.make_async_copy(
+                    wide.at[part, rows], out.at[slot, part, rows], sems.at[2 * part + half]
+                )
+            )
+            copies[-1].start()
+    for copy in copies:
+        copy.wait()
+
+
+def finish(got, whole):
     return pl.pallas_call(
         finish_kernel,
-        grid_spec=pltpu.PrefetchScalarGridSpec(
-            num_scalar_prefetch=1,
-            grid=(2,),
-            in_specs=[
-                pl.BlockSpec((1, 512, 256), lambda s, _: (s, 0, 0)),
-                pl.BlockSpec(memory_space=pl.ANY),
-            ],
-            out_specs=pl.BlockSpec((1, 1, 512, 256), lambda s, place: (1 - place[0], s, 0, 0)),
-        ),
+        in_specs=[pl.BlockSpec(memory_space=pltpu.VMEM), pl.BlockSpec(memory_space=pl.ANY)],
+        out_specs=pl.BlockSpec(memory_space=pl.ANY),
+        scratch_shapes=[pltpu.VMEM((2, 512, 256), F32), pltpu.SemaphoreType.DMA((4,))],
         out_shape=jax.ShapeDtypeStruct((2, 2, 512, 256), F32),
-        input_output_aliases={2: 0},
+        input_output_aliases={1: 0},
         name="finish",
-    )(place, got, whole)
+    )(got, whole)
 
 
 def local(traces_rows, traces_cols, offsets_rows, offsets_cols, bins):
@@ -357,7 +368,7 @@
     leaves = correlate(place, pieces["y2"], pieces["xQ"], SEND, (1, 0), "send", send_early)
     arrived = send(leaves, HALVES)
     stays = correlate(after(place, leaves), pieces["y2"], pieces["xS"], KEEP, None, "keep", keep_early)
-    return finish(place, arrived, stays)
+    return finish(arrived, stays)
 
 
 def solution(mesh):

time: 138 us -> 136 us (0.986)
  Pallas kernels: 37.7 us -> 35.5 us
    pallas_call x2, Pallas kernels: 19.3 us -> 17.7 us  [spectra(): pl.pallas_call(functools.partial(spectra_kernel, width // 128), grid_spec...]
where the time goes in v3:
time: 136 us; the launch traced here: 135 us
  starting transfers between devices  47.3 us (35%)
  waiting for transfers between devices  44.6 us (33%)
  Pallas kernels  35.5 us (26%)
  other arithmetic  3.84 us (3%)
  local copies, waits for them, and re-layouts  3.03 us (2%)
    ppermute x30, starting transfers between devices, send(): return lax.ppermute(value, AXES, pairs)  47.3 us
    ppermute x30, waiting for transfers between devices, send(): return lax.ppermute(value, AXES, pairs)  44.6 us
    pallas_call x2, Pallas kernels, spectra(): pl.pallas_call(functools.partial(spectra_kernel, width // 128), grid_spec...  17.7 us
    pallas_call x4, Pallas kernels, correlate(): pl.pallas_call(functools.partial(correlate_kernel, pairs, picks, part_out...  15.8 us
  transfers between devices with their start and end apart: 30, of which 11 were waited for; matrix products, arithmetic and copies ran while one was open for 2% of the time, Pallas kernels for 17%

profile of v3, /device:TPU:1, one launch (start us, length us, event | category | flops | bytes accessed | tf_op | source)
XLA Modules:
  0.0 134.8 jit_solution(9613382944515417793)
XLA Ops:
  2.5 10.8 %spectra.2 = (bf16[1024,128]{1,0:T(8,128)(2,1)S(1)}, bf16[1024,128]{1,0:T(8,128)(2,1)S(1)}, bf16[1024,128]{1,0:T(8,128)(2,1)S(1)}, bf16[1024,128]{1,0:T(8,128)(2...) custom-call(s32[10]{0:T(128)S(1)} %stack.128.place, ...), custom_call_target="tpu_custom_call" | custom-call | flops 8589934592 | bytes 10485760 | tf_op jit(solution)/shard_map/spectra/pallas_call | solution.py:151
  13.2 2.5 %collective-permute-start.6 = (bf16[1024,128]{1,0:T(8,128)(2,1)}, bf16[1024,128]{1,0:T(8,128)(2,1)}, u32[]{:S(2)}, u32[]{:S(2)}) collective-permute-start(bf16[1024,128]{1,0:T(8,128)(2,1)} %get-tuple-element.52), channel_id=1, source_target_pairs={{0,65},{1,64},{2,67},{3,66},{4,69},{5,68},{6,71},{7,70},{8,73},{9,... | collective-permute-start | bytes 786440 | tf_op jit(solution)/shard_map/send_Azb/ppermute | solution.py:71
  15.7 2.7 %collective-permute-start.7 = (bf16[1024,128]{1,0:T(8,128)(2,1)}, bf16[1024,128]{1,0:T(8,128)(2,1)}, u32[]{:S(2)}, u32[]{:S(2)}) collective-permute-start(bf16[1024,128]{1,0:T(8,128)(2,1)} %get-tuple-element.53), channel_id=1, source_target_pairs={{0,33},{1,32},{2,35},{3,34},{4,37},{5,36},{6,39},{7,38},{8,41},{9,... | collective-permute-start | bytes 786440 | tf_op jit(solution)/shard_map/send_Azac/ppermute | solution.py:71
  18.4 2.9 %collective-permute-start.8 = (bf16[1024,128]{1,0:T(8,128)(2,1)S(1)}, bf16[1024,128]{1,0:T(8,128)(2,1)}, u32[]{:S(2)}, u32[]{:S(2)}) collective-permute-start(bf16[1024,128]{1,0:T(8,128)(2,1)S(1)} %get-tuple-element.54), channel_id=1, source_target_pairs={{0,1},{1,0},{2,3},{3,2},{4,5},{5,4},{6,7},{7,6},{8,9},{9,8},{10,11... | collective-permute-start | bytes 786440 | tf_op jit(solution)/shard_map/send_Aza/ppermute | solution.py:71
  22.1 6.9 %spectra.3 = (bf16[1024,128]{1,0:T(8,128)(2,1)S(1)}, bf16[1024,128]{1,0:T(8,128)(2,1)S(1)}, bf16[1024,128]{1,0:T(8,128)(2,1)S(1)}, bf16[1024,128]{1,0:T(8,128)(2...) custom-call(s32[10]{0:T(128)S(1)} %stack.128.place, ...), custom_call_target="tpu_custom_call" | custom-call | flops 8589934592 | bytes 10485760 | tf_op jit(solution)/shard_map/spectra/pallas_call | solution.py:151
  29.8 2.6 %collective-permute-start = (bf16[1024,128]{1,0:T(8,128)(2,1)}, bf16[1024,128]{1,0:T(8,128)(2,1)S(1)}, u32[]{:S(2)}, u32[]{:S(2)}) collective-permute-start(bf16[1024,128]{1,0:T(8,128)(2,1)} %copy-done), channel_id=1, source_target_pairs={{0,1},{1,0},{2,3},{3,2},{4,5},{5,4},{6,7},{7,6},{8,9},{9,8},{10,11... | collective-permute-start | bytes 786440 | tf_op jit(solution)/shard_map/send_Bza/ppermute | solution.py:71
  32.4 1.3 broadcast_select_fusion
  34.8 1.4 %collective-permute-start.11 = (bf16[4,2,512,128]{3,2,1,0:T(8,128)(2,1)S(1)}, bf16[4,2,512,128]{3,2,1,0:T(8,128)(2,1)S(1)}, u32[]{:S(2)}, u32[]{:S(2)}) collective-permute-start(bf16[4,2,512,128]{3,2,1,0:T(8,128)(2,1)S(1)} %pad_maximum_fusion.1.refs_0_), channel_id=1, source_target_pairs={{0,6},{1,7},{2,4},{3,5},{4,2},{5,3},{6,0},{7,1},{8,14},{9,15},{10,... | collective-permute-start | bytes 3145736 | tf_op jit(solution)/shard_map/send_y1b/ppermute | solution.py:71
  38.1 1.7 %collective-permute-start.1 = (bf16[1024,128]{1,0:T(8,128)(2,1)S(1)}, bf16[1024,128]{1,0:T(8,128)(2,1)S(1)}, u32[]{:S(2)}, u32[]{:S(2)}) collective-permute-start(bf16[1024,128]{1,0:T(8,128)(2,1)S(1)} %get-tuple-element.45), channel_id=1, source_target_pairs={{0,65},{1,64},{2,67},{3,66},{4,69},{5,68},{6,71},{7,70},{8,73},{9,... | collective-permute-start | bytes 786440 | tf_op jit(solution)/shard_map/send_Bzb/ppermute | solution.py:71
  41.1 2.4 %collective-permute-done.3 = bf16[1024,128]{1,0:T(8,128)(2,1)S(1)} collective-permute-done((bf16[1024,128]{1,0:T(8,128)(2,1)S(1)}, bf16[1024,128]{1,0:T(8,128)(2,1)S(1)}, u32[]{:S(2)}, u32[]{:S(2)}) %collective-permute-start.3) | collective-permute-done | bytes 262176 | tf_op jit(solution)/shard_map/send_Bzbc/ppermute | solution.py:71
  43.5 2.5 %collective-permute-start.21 = (bf16[2,2,2,256,128]{4,3,2,1,0:T(8,128)(2,1)S(1)}, bf16[2,2,2,256,128]{4,3,2,1,0:T(8,128)(2,1)S(1)}, u32[]{:S(2)}, u32[]{:S(2)}) collective-permute-start(bf16[2,2,2,256,128]{4,3,2,1,0:T(8,128)(2,1)S(1)} %pad_maximum_fusion.5.refs_4_), channel_id=1, source_target_pairs={{0,8},{1,9},{2,10},{3,11},{4,12},{5,13},{6,14},{7,15},{8,0},{9,1},... | collective-permute-start | bytes 1572872 | tf_op jit(solution)/shard_map/send_xPa/ppermute | solution.py:71
  46.6 1.8 %collective-permute-start.4 = (bf16[1024,128]{1,0:T(8,128)(2,1)S(1)}, bf16[1024,128]{1,0:T(8,128)(2,1)S(1)}, u32[]{:S(2)}, u32[]{:S(2)}) collective-permute-start(bf16[1024,128]{1,0:T(8,128)(2,1)S(1)} %get-tuple-element.50), channel_id=1, source_target_pairs={{0,33},{1,32},{2,35},{3,34},{4,37},{5,36},{6,39},{7,38},{8,41},{9,... | collective-permute-start | bytes 786440 | tf_op jit(solution)/shard_map/send_Bzac/ppermute | solution.py:71
  48.4 4.3 %collective-permute-done.4 = bf16[1024,128]{1,0:T(8,128)(2,1)S(1)} collective-permute-done((bf16[1024,128]{1,0:T(8,128)(2,1)S(1)}, bf16[1024,128]{1,0:T(8,128)(2,1)S(1)}, u32[]{:S(2)}, u32[]{:S(2)}) %collective-permute-start.4) | collective-permute-done | bytes 262176 | tf_op jit(solution)/shard_map/send_Bzac/ppermute | solution.py:71
  53.9 2.9 %collective-permute-start.5 = (bf16[1024,128]{1,0:T(8,128)(2,1)S(1)}, bf16[1024,128]{1,0:T(8,128)(2,1)S(1)}, u32[]{:S(2)}, u32[]{:S(2)}) collective-permute-start(bf16[1024,128]{1,0:T(8,128)(2,1)S(1)} %get-tuple-element.51), channel_id=1, source_target_pairs={{0,96},{1,97},{2,98},{3,99},{4,100},{5,101},{6,102},{7,103},{8,104... | collective-permute-start | bytes 786440 | tf_op jit(solution)/shard_map/send_Az2c/ppermute | solution.py:71
  56.8 2.5 %collective-permute-start.19 = (bf16[2,2,2,256,128]{4,3,2,1,0:T(8,128)(2,1)S(1)}, bf16[2,2,2,256,128]{4,3,2,1,0:T(8,128)(2,1)S(1)}, u32[]{:S(2)}, u32[]{:S(2)}) collective-permute-start(bf16[2,2,2,256,128]{4,3,2,1,0:T(8,128)(2,1)S(1)} %collective-permute-done.18.refs_6_), channel_id=1, source_target_pairs={{0,8},{1,9},{2,10},{3,11},{4,12},{5,13},{6,14},{7,15},{8,0},{9,1},... | collective-permute-start | bytes 1572872 | tf_op jit(solution)/shard_map/send_xPf/ppermute | solution.py:71
  59.5 1.5 %collective-permute-done.2 = bf16[1024,128]{1,0:T(8,128)(2,1)S(1)} collective-permute-done((bf16[1024,128]{1,0:T(8,128)(2,1)S(1)}, bf16[1024,128]{1,0:T(8,128)(2,1)S(1)}, u32[]{:S(2)}, u32[]{:S(2)}) %collective-permute-start.2) | collective-permute-done | bytes 262176 | tf_op jit(solution)/shard_map/send_Az2/ppermute | solution.py:71
  61.6 6.3 %collective-permute-done.5 = bf16[1024,128]{1,0:T(8,128)(2,1)S(1)} collective-permute-done((bf16[1024,128]{1,0:T(8,128)(2,1)S(1)}, bf16[1024,128]{1,0:T(8,128)(2,1)S(1)}, u32[]{:S(2)}, u32[]{:S(2)}) %collective-permute-start.5) | collective-permute-done | bytes 262176 | tf_op jit(solution)/shard_map/send_Az2c/ppermute | solution.py:71
  68.1 2.6 %collective-permute-start.20 = (bf16[4,2,2,256,128]{4,3,2,1,0:T(8,128)(2,1)S(1)}, bf16[4,2,2,256,128]{4,3,2,1,0:T(8,128)(2,1)S(1)}, u32[]{:S(2)}, u32[]{:S(2)}) collective-permute-start(bf16[4,2,2,256,128]{4,3,2,1,0:T(8,128)(2,1)S(1)} %pad_maximum_fusion.2.refs_4_), channel_id=1, source_target_pairs={{0,8},{1,9},{2,10},{3,11},{4,12},{5,13},{6,14},{7,15},{8,0},{9,1},... | collective-permute-start | bytes 3145736 | tf_op jit(solution)/shard_map/send_xQa/ppermute | solution.py:71
  70.6 1.5 %collective-permute-start.25 = (bf16[1024,128]{1,0:T(8,128)(2,1)S(1)}, bf16[1024,128]{1,0:T(8,128)(2,1)S(1)}, u32[]{:S(2)}, u32[]{:S(2)}) collective-permute-start(bf16[1024,128]{1,0:T(8,128)(2,1)S(1)} %get-tuple-element.69), channel_id=1, source_target_pairs={{0,64},{1,65},{2,66},{3,67},{4,68},{5,69},{6,70},{7,71},{8,72},{9,... | collective-permute-start | bytes 786440 | tf_op jit(solution)/shard_map/send_Bz2/ppermute | solution.py:71
  72.1 8.4 %collective-permute-done.22.refs_6_ = bf16[4,2,2,256,128]{4,3,2,1,0:T(8,128)(2,1)S(1)} collective-permute-done((bf16[4,2,2,256,128]{4,3,2,1,0:T(8,128)(2,1)S(1)}, bf16[4,2,2,256,128]{4,3,2,1,0:T(8,128)(2,1)S(1)}, u32[]{:S(2)}, u32[]{:S(2)}) %collective-permute-start.22) | collective-permute-done | bytes 1048608 | tf_op jit(solution)/shard_map/send_xQb/ppermute | solution.py:71
  81.2 6.9 %collective-permute-start.26 = (bf16[1024,128]{1,0:T(8,128)(2,1)S(1)}, bf16[1024,128]{1,0:T(8,128)(2,1)S(1)}, u32[]{:S(2)}, u32[]{:S(2)}) collective-permute-start(bf16[1024,128]{1,0:T(8,128)(2,1)S(1)} %get-tuple-element.71), channel_id=1, source_target_pairs={{0,96},{1,97},{2,98},{3,99},{4,100},{5,101},{6,102},{7,103},{8,104... | collective-permute-start | bytes 786440 | tf_op jit(solution)/shard_map/send_Bz2c/ppermute | solution.py:71
  88.1 1.9 %collective-permute-done.15.refs_2_ = bf16[4,2,512,128]{3,2,1,0:T(8,128)(2,1)S(1)} collective-permute-done((bf16[4,2,512,128]{3,2,1,0:T(8,128)(2,1)S(1)}, bf16[4,2,512,128]{3,2,1,0:T(8,128)(2,1)S(1)}, u32[]{:S(2)}, u32[]{:S(2)}) %collective-permute-start.15) | collective-permute-done | bytes 1048608 | tf_op jit(solution)/shard_map/send_y2b/ppermute | solution.py:71
  90.1 3.3 %collective-permute-start.13 = (bf16[4,2,512,128]{3,2,1,0:T(8,128)(2,1)S(1)}, bf16[4,2,512,128]{3,2,1,0:T(8,128)(2,1)S(1)}, u32[]{:S(2)}, u32[]{:S(2)}) collective-permute-start(bf16[4,2,512,128]{3,2,1,0:T(8,128)(2,1)S(1)} %pad_maximum_fusion.refs_0_), channel_id=1, source_target_pairs={{0,2},{1,3},{2,0},{3,1},{4,6},{5,7},{6,4},{7,5},{8,10},{9,11},{10,... | collective-permute-start | bytes 3145736 | tf_op jit(solution)/shard_map/send_y2a/ppermute | solution.py:71
  94.1 10.1 %collective-permute-done.28.refs_6_ = bf16[2,2,2,256,128]{4,3,2,1,0:T(8,128)(2,1)S(1)} collective-permute-done((bf16[2,2,2,256,128]{4,3,2,1,0:T(8,128)(2,1)S(1)}, bf16[2,2,2,256,128]{4,3,2,1,0:T(8,128)(2,1)S(1)}, u32[]{:S(2)}, u32[]{:S(2)}) %collective-permute-start.28) | collective-permute-done | bytes 524320 | tf_op jit(solution)/shard_map/send_xSb/ppermute | solution.py:71
  104.2 2.5 %collective-permute-start.29 = (bf16[2,2,2,256,128]{4,3,2,1,0:T(8,128)(2,1)S(1)}, bf16[2,2,2,256,128]{4,3,2,1,0:T(8,128)(2,1)S(1)}, u32[]{:S(2)}, u32[]{:S(2)}) collective-permute-start(bf16[2,2,2,256,128]{4,3,2,1,0:T(8,128)(2,1)S(1)} %collective-permute-done.28.refs_6_), channel_id=1, source_target_pairs={{0,8},{1,9},{2,10},{3,11},{4,12},{5,13},{6,14},{7,15},{8,0},{9,1},... | collective-permute-start | bytes 1572872 | tf_op jit(solution)/shard_map/send_xSf/ppermute | solution.py:71
  106.9 3.7 %correlate.4.refs_8_ = f32[2,512,256]{2,1,0:T(8,128)S(1)} custom-call(s32[10]{0:T(128)S(1)} %stack.128.place, bf16[4,2,512,128]{3,2,1,0:T(8,128)(2,1)S(1)} %pad_maximum_fusion.1.refs_0_, bf16[4,2,512,128]{3,2,1,0:T(8,128)(2,1)S(1)} %collective-permute-done.14.refs_1_, bf16[4,2,512,128]{3,2,1,0:T(8,128)(2,1)S(1)} %collective-permute-done.11.refs_2_, ...), custom_call_target="tpu_custom_call" | custom-call | flops 2147483648 | bytes 6291456 | tf_op jit(solution)/shard_map/correlate/pallas_call | solution.py:241
  110.6 6.2 %collective-permute-done.16.refs_3_ = bf16[4,2,512,128]{3,2,1,0:T(8,128)(2,1)S(1)} collective-permute-done((bf16[4,2,512,128]{3,2,1,0:T(8,128)(2,1)S(1)}, bf16[4,2,512,128]{3,2,1,0:T(8,128)(2,1)S(1)}, u32[]{:S(2)}, u32[]{:S(2)}) %collective-permute-start.16) | collective-permute-done | bytes 1048608 | tf_op jit(solution)/shard_map/send_y2f/ppermute | solution.py:71
  116.8 3.7 %correlate.5 = bf16[2,512,256]{2,1,0:T(8,128)(2,1)S(1)} custom-call(s32[10]{0:T(128)S(1)} %stack.128.place, bf16[4,2,512,128]{3,2,1,0:T(8,128)(2,1)S(1)} %pad_maximum_fusion.refs_0_, bf16[4,2,512,128]{3,2,1,0:T(8,128)(2,1)S(1)} %collective-permute-done.13.refs_1_, bf16[4,2,512,128]{3,2,1,0:T(8,128)(2,1)S(1)} %collective-permute-done.15.refs_2_, ...), custom_call_target="tpu_custom_call" | custom-call | flops 34359738368 | bytes 6291456 | tf_op jit(solution)/shard_map/correlate/pallas_call | solution.py:241
  120.6 3.7 %correlate.6.refs_8_ = f32[2,512,256]{2,1,0:T(8,128)S(1)} custom-call(s32[10]{0:T(128)S(1)} %stack.128.place, bf16[4,2,512,128]{3,2,1,0:T(8,128)(2,1)S(1)} %pad_maximum_fusion.1.refs_0_, bf16[4,2,512,128]{3,2,1,0:T(8,128)(2,1)S(1)} %collective-permute-done.14.refs_1_, bf16[4,2,512,128]{3,2,1,0:T(8,128)(2,1)S(1)} %collective-permute-done.11.refs_2_, ...), custom_call_target="tpu_custom_call" | custom-call | flops 2147483648 | bytes 6291456 | tf_op jit(solution)/shard_map/correlate/pallas_call | solution.py:241
  124.3 4.7 %correlate.7.whole = f32[2,2,512,256]{3,2,1,0:T(8,128)} custom-call(s32[10]{0:T(128)S(1)} %stack.128.place, bf16[4,2,512,128]{3,2,1,0:T(8,128)(2,1)S(1)} %pad_maximum_fusion.refs_0_, bf16[4,2,512,128]{3,2,1,0:T(8,128)(2,1)S(1)} %collective-permute-done.13.refs_1_, bf16[4,2,512,128]{3,2,1,0:T(8,128)(2,1)S(1)} %collective-permute-done.15.refs_2_, ...), custom_call_target="tpu_custom_call" | custom-call | flops 2147483648 | bytes 6291456 | tf_op jit(solution)/shard_map/correlate/pallas_call | solution.py:241
  129.0 2.8 %collective-permute-done.24.got = bf16[2,512,256]{2,1,0:T(8,128)(2,1)S(1)} collective-permute-done((bf16[2,512,256]{2,1,0:T(8,128)(2,1)S(1)}, bf16[2,512,256]{2,1,0:T(8,128)(2,1)S(1)}, u32[]{:S(2)}, u32[]{:S(2)}) %collective-permute-start.24) | collective-permute-done | bytes 524320 | tf_op jit(solution)/shard_map/ppermute | solution.py:71
  132.5 2.1 %finish.1 = f32[2,2,512,256]{3,2,1,0:T(8,128)} custom-call(bf16[2,512,256]{2,1,0:T(8,128)(2,1)} %copy-done.1, f32[2,2,512,256]{3,2,1,0:T(8,128)} %correlate.7.whole), custom_call_target="tpu_custom_call", output_to_operand_aliasing={{}: (1, {})} | custom-call | tf_op jit(solution)/shard_map/finish/pallas_call | solution.py:288
  (67 shorter events, 13.6 us)
Async XLA Ops:
  2.5 19.3 %copy-start.2 = (s32[256]{0:T(256)S(1)}, s32[256]{0:T(256)}, u32[]{:S(2)}) copy-start(s32[256]{0:T(256)} %param.8) | copy-start | bytes 3076
  13.2 16.5 %collective-permute-start.6 = (bf16[1024,128]{1,0:T(8,128)(2,1)}, bf16[1024,128]{1,0:T(8,128)(2,1)}, u32[]{:S(2)}, u32[]{:S(2)}) collective-permute-start(bf16[1024,128]{1,0:T(8,128)(2,1)} %get-tuple-element.52), channel_id=1, source_target_pairs={{0,65},{1,64},{2,67},{3,66},{4,69},{5,68},{6,71},{7,70},{8,73},{9,... | collective-permute-start | bytes 786440 | tf_op jit(solution)/shard_map/send_Azb/ppermute | solution.py:71
  15.7 16.7 %collective-permute-start.7 = (bf16[1024,128]{1,0:T(8,128)(2,1)}, bf16[1024,128]{1,0:T(8,128)(2,1)}, u32[]{:S(2)}, u32[]{:S(2)}) collective-permute-start(bf16[1024,128]{1,0:T(8,128)(2,1)} %get-tuple-element.53), channel_id=1, source_target_pairs={{0,33},{1,32},{2,35},{3,34},{4,37},{5,36},{6,39},{7,38},{8,41},{9,... | collective-permute-start | bytes 786440 | tf_op jit(solution)/shard_map/send_Azac/ppermute | solution.py:71
  18.4 14.0 %collective-permute-start.8 = (bf16[1024,128]{1,0:T(8,128)(2,1)S(1)}, bf16[1024,128]{1,0:T(8,128)(2,1)}, u32[]{:S(2)}, u32[]{:S(2)}) collective-permute-start(bf16[1024,128]{1,0:T(8,128)(2,1)S(1)} %get-tuple-element.54), channel_id=1, source_target_pairs={{0,1},{1,0},{2,3},{3,2},{4,5},{5,4},{6,7},{7,6},{8,9},{9,8},{10,11... | collective-permute-start | bytes 786440 | tf_op jit(solution)/shard_map/send_Aza/ppermute | solution.py:71
  21.3 11.1 %collective-permute-start.9 = (bf16[1024,128]{1,0:T(8,128)(2,1)S(1)}, bf16[1024,128]{1,0:T(8,128)(2,1)}, u32[]{:S(2)}, u32[]{:S(2)}) collective-permute-start(bf16[1024,128]{1,0:T(8,128)(2,1)S(1)} %get-tuple-element.55), channel_id=1, source_target_pairs={{0,97},{1,96},{2,99},{3,98},{4,101},{5,100},{6,103},{7,102},{8,105... | collective-permute-start | bytes 786440 | tf_op jit(solution)/shard_map/send_Azbc/ppermute | solution.py:71
  21.4 12.4 %collective-permute-start.10 = (bf16[1024,128]{1,0:T(8,128)(2,1)S(1)}, bf16[1024,128]{1,0:T(8,128)(2,1)}, u32[]{:S(2)}, u32[]{:S(2)}) collective-permute-start(bf16[1024,128]{1,0:T(8,128)(2,1)S(1)} %get-tuple-element.56), channel_id=1, source_target_pairs={{0,32},{1,33},{2,34},{3,35},{4,36},{5,37},{6,38},{7,39},{8,40},{9,... | collective-permute-start | bytes 786440 | tf_op jit(solution)/shard_map/send_Acc/ppermute | solution.py:71
  29.8 8.3 %collective-permute-start = (bf16[1024,128]{1,0:T(8,128)(2,1)}, bf16[1024,128]{1,0:T(8,128)(2,1)S(1)}, u32[]{:S(2)}, u32[]{:S(2)}) collective-permute-start(bf16[1024,128]{1,0:T(8,128)(2,1)} %copy-done), channel_id=1, source_target_pairs={{0,1},{1,0},{2,3},{3,2},{4,5},{5,4},{6,7},{7,6},{8,9},{9,8},{10,11... | collective-permute-start | bytes 786440 | tf_op jit(solution)/shard_map/send_Bza/ppermute | solution.py:71
  32.4 7.3 %collective-permute-start.17 = (bf16[1024,128]{1,0:T(8,128)(2,1)S(1)}, bf16[1024,128]{1,0:T(8,128)(2,1)S(1)}, u32[]{:S(2)}, u32[]{:S(2)}) collective-permute-start(bf16[1024,128]{1,0:T(8,128)(2,1)S(1)} %get-tuple-element.62), channel_id=1, source_target_pairs={{0,32},{1,33},{2,34},{3,35},{4,36},{5,37},{6,38},{7,39},{8,40},{9,... | collective-permute-start | bytes 786440 | tf_op jit(solution)/shard_map/send_Bcc/ppermute | solution.py:71
  34.8 24.7 %collective-permute-start.11 = (bf16[4,2,512,128]{3,2,1,0:T(8,128)(2,1)S(1)}, bf16[4,2,512,128]{3,2,1,0:T(8,128)(2,1)S(1)}, u32[]{:S(2)}, u32[]{:S(2)}) collective-permute-start(bf16[4,2,512,128]{3,2,1,0:T(8,128)(2,1)S(1)} %pad_maximum_fusion.1.refs_0_), channel_id=1, source_target_pairs={{0,6},{1,7},{2,4},{3,5},{4,2},{5,3},{6,0},{7,1},{8,14},{9,15},{10,... | collective-permute-start | bytes 3145736 | tf_op jit(solution)/shard_map/send_y1b/ppermute | solution.py:71
  36.2 7.3 %collective-permute-start.3 = (bf16[1024,128]{1,0:T(8,128)(2,1)S(1)}, bf16[1024,128]{1,0:T(8,128)(2,1)S(1)}, u32[]{:S(2)}, u32[]{:S(2)}) collective-permute-start(bf16[1024,128]{1,0:T(8,128)(2,1)S(1)} %get-tuple-element.49), channel_id=1, source_target_pairs={{0,97},{1,96},{2,99},{3,98},{4,101},{5,100},{6,103},{7,102},{8,105... | collective-permute-start | bytes 786440 | tf_op jit(solution)/shard_map/send_Bzbc/ppermute | solution.py:71
  37.0 31.0 %collective-permute-start.14 = (bf16[4,2,512,128]{3,2,1,0:T(8,128)(2,1)S(1)}, bf16[4,2,512,128]{3,2,1,0:T(8,128)(2,1)S(1)}, u32[]{:S(2)}, u32[]{:S(2)}) collective-permute-start(bf16[4,2,512,128]{3,2,1,0:T(8,128)(2,1)S(1)} %pad_maximum_fusion.1.refs_0_), channel_id=1, source_target_pairs={{0,2},{1,3},{2,0},{3,1},{4,6},{5,7},{6,4},{7,5},{8,10},{9,11},{10,... | collective-permute-start | bytes 3145736 | tf_op jit(solution)/shard_map/send_y1a/ppermute | solution.py:71
  38.1 8.5 %collective-permute-start.1 = (bf16[1024,128]{1,0:T(8,128)(2,1)S(1)}, bf16[1024,128]{1,0:T(8,128)(2,1)S(1)}, u32[]{:S(2)}, u32[]{:S(2)}) collective-permute-start(bf16[1024,128]{1,0:T(8,128)(2,1)S(1)} %get-tuple-element.45), channel_id=1, source_target_pairs={{0,65},{1,64},{2,67},{3,66},{4,69},{5,68},{6,71},{7,70},{8,73},{9,... | collective-permute-start | bytes 786440 | tf_op jit(solution)/shard_map/send_Bzb/ppermute | solution.py:71
  39.8 14.1 %collective-permute-start.18 = (bf16[2,2,2,256,128]{4,3,2,1,0:T(8,128)(2,1)S(1)}, bf16[2,2,2,256,128]{4,3,2,1,0:T(8,128)(2,1)S(1)}, u32[]{:S(2)}, u32[]{:S(2)}) collective-permute-start(bf16[2,2,2,256,128]{4,3,2,1,0:T(8,128)(2,1)S(1)} %pad_maximum_fusion.5.refs_4_), channel_id=1, source_target_pairs={{0,24},{1,25},{2,26},{3,27},{4,28},{5,29},{6,30},{7,31},{8,16},{9,... | collective-permute-start | bytes 1572872 | tf_op jit(solution)/shard_map/send_xPb/ppermute | solution.py:71
  43.5 13.4 %collective-permute-start.21 = (bf16[2,2,2,256,128]{4,3,2,1,0:T(8,128)(2,1)S(1)}, bf16[2,2,2,256,128]{4,3,2,1,0:T(8,128)(2,1)S(1)}, u32[]{:S(2)}, u32[]{:S(2)}) collective-permute-start(bf16[2,2,2,256,128]{4,3,2,1,0:T(8,128)(2,1)S(1)} %pad_maximum_fusion.5.refs_4_), channel_id=1, source_target_pairs={{0,8},{1,9},{2,10},{3,11},{4,12},{5,13},{6,14},{7,15},{8,0},{9,1},... | collective-permute-start | bytes 1572872 | tf_op jit(solution)/shard_map/send_xPa/ppermute | solution.py:71
  46.6 6.1 %collective-permute-start.4 = (bf16[1024,128]{1,0:T(8,128)(2,1)S(1)}, bf16[1024,128]{1,0:T(8,128)(2,1)S(1)}, u32[]{:S(2)}, u32[]{:S(2)}) collective-permute-start(bf16[1024,128]{1,0:T(8,128)(2,1)S(1)} %get-tuple-element.50), channel_id=1, source_target_pairs={{0,33},{1,32},{2,35},{3,34},{4,37},{5,36},{6,39},{7,38},{8,41},{9,... | collective-permute-start | bytes 786440 | tf_op jit(solution)/shard_map/send_Bzac/ppermute | solution.py:71
  52.7 8.3 %collective-permute-start.2 = (bf16[1024,128]{1,0:T(8,128)(2,1)S(1)}, bf16[1024,128]{1,0:T(8,128)(2,1)S(1)}, u32[]{:S(2)}, u32[]{:S(2)}) collective-permute-start(bf16[1024,128]{1,0:T(8,128)(2,1)S(1)} %get-tuple-element.46), channel_id=1, source_target_pairs={{0,64},{1,65},{2,66},{3,67},{4,68},{5,69},{6,70},{7,71},{8,72},{9,... | collective-permute-start | bytes 786440 | tf_op jit(solution)/shard_map/send_Az2/ppermute | solution.py:71
  53.9 13.9 %collective-permute-start.5 = (bf16[1024,128]{1,0:T(8,128)(2,1)S(1)}, bf16[1024,128]{1,0:T(8,128)(2,1)S(1)}, u32[]{:S(2)}, u32[]{:S(2)}) collective-permute-start(bf16[1024,128]{1,0:T(8,128)(2,1)S(1)} %get-tuple-element.51), channel_id=1, source_target_pairs={{0,96},{1,97},{2,98},{3,99},{4,100},{5,101},{6,102},{7,103},{8,104... | collective-permute-start | bytes 786440 | tf_op jit(solution)/shard_map/send_Az2c/ppermute | solution.py:71
  56.8 11.2 %collective-permute-start.19 = (bf16[2,2,2,256,128]{4,3,2,1,0:T(8,128)(2,1)S(1)}, bf16[2,2,2,256,128]{4,3,2,1,0:T(8,128)(2,1)S(1)}, u32[]{:S(2)}, u32[]{:S(2)}) collective-permute-start(bf16[2,2,2,256,128]{4,3,2,1,0:T(8,128)(2,1)S(1)} %collective-permute-done.18.refs_6_), channel_id=1, source_target_pairs={{0,8},{1,9},{2,10},{3,11},{4,12},{5,13},{6,14},{7,15},{8,0},{9,1},... | collective-permute-start | bytes 1572872 | tf_op jit(solution)/shard_map/send_xPf/ppermute | solution.py:71
  59.5 21.0 %collective-permute-start.22 = (bf16[4,2,2,256,128]{4,3,2,1,0:T(8,128)(2,1)S(1)}, bf16[4,2,2,256,128]{4,3,2,1,0:T(8,128)(2,1)S(1)}, u32[]{:S(2)}, u32[]{:S(2)}) collective-permute-start(bf16[4,2,2,256,128]{4,3,2,1,0:T(8,128)(2,1)S(1)} %pad_maximum_fusion.2.refs_4_), channel_id=1, source_target_pairs={{0,24},{1,25},{2,26},{3,27},{4,28},{5,29},{6,30},{7,31},{8,16},{9,... | collective-permute-start | bytes 3145736 | tf_op jit(solution)/shard_map/send_xQb/ppermute | solution.py:71
  61.0 20.2 %collective-permute-start.12 = (bf16[4,2,512,128]{3,2,1,0:T(8,128)(2,1)S(1)}, bf16[4,2,512,128]{3,2,1,0:T(8,128)(2,1)S(1)}, u32[]{:S(2)}, u32[]{:S(2)}) collective-permute-start(bf16[4,2,512,128]{3,2,1,0:T(8,128)(2,1)S(1)} %collective-permute-done.11.refs_2_), channel_id=1, source_target_pairs={{0,2},{1,3},{2,0},{3,1},{4,6},{5,7},{6,4},{7,5},{8,10},{9,11},{10,... | collective-permute-start | bytes 3145736 | tf_op jit(solution)/shard_map/send_y1f/ppermute | solution.py:71
  68.0 22.1 %collective-permute-start.15 = (bf16[4,2,512,128]{3,2,1,0:T(8,128)(2,1)S(1)}, bf16[4,2,512,128]{3,2,1,0:T(8,128)(2,1)S(1)}, u32[]{:S(2)}, u32[]{:S(2)}) collective-permute-start(bf16[4,2,512,128]{3,2,1,0:T(8,128)(2,1)S(1)} %pad_maximum_fusion.refs_0_), channel_id=1, source_target_pairs={{0,6},{1,7},{2,4},{3,5},{4,2},{5,3},{6,0},{7,1},{8,14},{9,15},{10,... | collective-permute-start | bytes 3145736 | tf_op jit(solution)/shard_map/send_y2b/ppermute | solution.py:71
  68.1 25.6 %collective-permute-start.20 = (bf16[4,2,2,256,128]{4,3,2,1,0:T(8,128)(2,1)S(1)}, bf16[4,2,2,256,128]{4,3,2,1,0:T(8,128)(2,1)S(1)}, u32[]{:S(2)}, u32[]{:S(2)}) collective-permute-start(bf16[4,2,2,256,128]{4,3,2,1,0:T(8,128)(2,1)S(1)} %pad_maximum_fusion.2.refs_4_), channel_id=1, source_target_pairs={{0,8},{1,9},{2,10},{3,11},{4,12},{5,13},{6,14},{7,15},{8,0},{9,1},... | collective-permute-start | bytes 3145736 | tf_op jit(solution)/shard_map/send_xQa/ppermute | solution.py:71
  70.6 22.7 %collective-permute-start.25 = (bf16[1024,128]{1,0:T(8,128)(2,1)S(1)}, bf16[1024,128]{1,0:T(8,128)(2,1)S(1)}, u32[]{:S(2)}, u32[]{:S(2)}) collective-permute-start(bf16[1024,128]{1,0:T(8,128)(2,1)S(1)} %get-tuple-element.69), channel_id=1, source_target_pairs={{0,64},{1,65},{2,66},{3,67},{4,68},{5,69},{6,70},{7,71},{8,72},{9,... | collective-permute-start | bytes 786440 | tf_op jit(solution)/shard_map/send_Bz2/ppermute | solution.py:71
  80.5 26.1 %collective-permute-start.23 = (bf16[4,2,2,256,128]{4,3,2,1,0:T(8,128)(2,1)S(1)}, bf16[4,2,2,256,128]{4,3,2,1,0:T(8,128)(2,1)S(1)}, u32[]{:S(2)}, u32[]{:S(2)}) collective-permute-start(bf16[4,2,2,256,128]{4,3,2,1,0:T(8,128)(2,1)S(1)} %collective-permute-done.22.refs_6_), channel_id=1, source_target_pairs={{0,8},{1,9},{2,10},{3,11},{4,12},{5,13},{6,14},{7,15},{8,0},{9,1},... | collective-permute-start | bytes 3145736 | tf_op jit(solution)/shard_map/send_xQf/ppermute | solution.py:71
  81.2 12.3 %collective-permute-start.26 = (bf16[1024,128]{1,0:T(8,128)(2,1)S(1)}, bf16[1024,128]{1,0:T(8,128)(2,1)S(1)}, u32[]{:S(2)}, u32[]{:S(2)}) collective-permute-start(bf16[1024,128]{1,0:T(8,128)(2,1)S(1)} %get-tuple-element.71), channel_id=1, source_target_pairs={{0,96},{1,97},{2,98},{3,99},{4,100},{5,101},{6,102},{7,103},{8,104... | collective-permute-start | bytes 786440 | tf_op jit(solution)/shard_map/send_Bz2c/ppermute | solution.py:71
  90.1 20.5 %collective-permute-start.13 = (bf16[4,2,512,128]{3,2,1,0:T(8,128)(2,1)S(1)}, bf16[4,2,512,128]{3,2,1,0:T(8,128)(2,1)S(1)}, u32[]{:S(2)}, u32[]{:S(2)}) collective-permute-start(bf16[4,2,512,128]{3,2,1,0:T(8,128)(2,1)S(1)} %pad_maximum_fusion.refs_0_), channel_id=1, source_target_pairs={{0,2},{1,3},{2,0},{3,1},{4,6},{5,7},{6,4},{7,5},{8,10},{9,11},{10,... | collective-permute-start | bytes 3145736 | tf_op jit(solution)/shard_map/send_y2a/ppermute | solution.py:71
  93.3 23.4 %collective-permute-start.16 = (bf16[4,2,512,128]{3,2,1,0:T(8,128)(2,1)S(1)}, bf16[4,2,512,128]{3,2,1,0:T(8,128)(2,1)S(1)}, u32[]{:S(2)}, u32[]{:S(2)}) collective-permute-start(bf16[4,2,512,128]{3,2,1,0:T(8,128)(2,1)S(1)} %collective-permute-done.15.refs_2_), channel_id=1, source_target_pairs={{0,2},{1,3},{2,0},{3,1},{4,6},{5,7},{6,4},{7,5},{8,10},{9,11},{10,... | collective-permute-start | bytes 3145736 | tf_op jit(solution)/shard_map/send_y2f/ppermute | solution.py:71
  93.6 10.5 %collective-permute-start.28 = (bf16[2,2,2,256,128]{4,3,2,1,0:T(8,128)(2,1)S(1)}, bf16[2,2,2,256,128]{4,3,2,1,0:T(8,128)(2,1)S(1)}, u32[]{:S(2)}, u32[]{:S(2)}) collective-permute-start(bf16[2,2,2,256,128]{4,3,2,1,0:T(8,128)(2,1)S(1)} %pad_maximum_fusion.6.refs_4_), channel_id=1, source_target_pairs={{0,24},{1,25},{2,26},{3,27},{4,28},{5,29},{6,30},{7,31},{8,16},{9,... | collective-permute-start | bytes 1572872 | tf_op jit(solution)/shard_map/send_xSb/ppermute | solution.py:71
  104.2 20.1 %collective-permute-start.29 = (bf16[2,2,2,256,128]{4,3,2,1,0:T(8,128)(2,1)S(1)}, bf16[2,2,2,256,128]{4,3,2,1,0:T(8,128)(2,1)S(1)}, u32[]{:S(2)}, u32[]{:S(2)}) collective-permute-start(bf16[2,2,2,256,128]{4,3,2,1,0:T(8,128)(2,1)S(1)} %collective-permute-done.28.refs_6_), channel_id=1, source_target_pairs={{0,8},{1,9},{2,10},{3,11},{4,12},{5,13},{6,14},{7,15},{8,0},{9,1},... | collective-permute-start | bytes 1572872 | tf_op jit(solution)/shard_map/send_xSf/ppermute | solution.py:71
  106.6 17.6 %collective-permute-start.27 = (bf16[2,2,2,256,128]{4,3,2,1,0:T(8,128)(2,1)S(1)}, bf16[2,2,2,256,128]{4,3,2,1,0:T(8,128)(2,1)S(1)}, u32[]{:S(2)}, u32[]{:S(2)}) collective-permute-start(bf16[2,2,2,256,128]{4,3,2,1,0:T(8,128)(2,1)S(1)} %pad_maximum_fusion.6.refs_4_), channel_id=1, source_target_pairs={{0,8},{1,9},{2,10},{3,11},{4,12},{5,13},{6,14},{7,15},{8,0},{9,1},... | collective-permute-start | bytes 1572872 | tf_op jit(solution)/shard_map/send_xSa/ppermute | solution.py:71
  120.5 11.3 %collective-permute-start.24 = (bf16[2,512,256]{2,1,0:T(8,128)(2,1)S(1)}, bf16[2,512,256]{2,1,0:T(8,128)(2,1)S(1)}, u32[]{:S(2)}, u32[]{:S(2)}) collective-permute-start(bf16[2,512,256]{2,1,0:T(8,128)(2,1)S(1)} %correlate.5), channel_id=1, source_target_pairs={{0,1},{1,0},{2,3},{3,2},{4,5},{5,4},{6,7},{7,6},{8,9},{9,8},{10,11... | collective-permute-start | bytes 1572872 | tf_op jit(solution)/shard_map/ppermute | solution.py:71
  131.8 0.8 copy-start.1
  (1 other events, 0.7 us)

commit v4 on v3

--- a/solution.py
+++ b/solution.py
@@ -172,7 +172,7 @@
     )(place, table, lags, traces)
 
 
-def correlate_kernel(pairs, picks, part_out, has_start, place, *refs):
+def correlate_kernel(pairs, picks, parts, part_out, has_start, place, *refs):
     a_in, b_in, refs = refs[:4], refs[4:8], refs[8:]
     start, refs = (refs[0], refs[1:]) if has_start else (None, refs)
     out, a_all, b_all, total, a_sems, b_sems = refs
@@ -193,7 +193,7 @@
     for n in range(4):
         a_copies[n].wait()
         q = place[2 + n]
-        for part in range(2):
+        for at, part in enumerate(parts):
             right = []
             for z, half in pairs:
                 for other in range(2):
@@ -216,34 +216,35 @@
                     preferred_element_type=F32,
                 )
                 if n > 0:
-                    term += total[part, rows, :]
+                    term += total[at, rows, :]
                 elif has_start:
-                    term += start[part, rows, :]
+                    term += start[at, rows, :]
                 if n < 3:
-                    total[part, rows, :] = term
+                    total[at, rows, :] = term
                 elif part_out == "sum":
-                    out[part, rows, :] = term
+                    out[at, rows, :] = term
                 elif part_out == "send":
-                    out[part, rows, :] = (term * scale).astype(BF16)
+                    out[at, rows, :] = (term * scale).astype(BF16)
                 else:
-                    out[0, part, rows, :] = term * scale
-
-
-def correlate(place, a_pieces, b_pieces, pairs, picks, part_out, start=None):
+                    out[0, at, rows, :] = term * scale
+
+
+def correlate(place, a_pieces, b_pieces, pairs, picks, part_out, start=None, parts=(0, 1)):
     whole = lambda *shape: pl.BlockSpec(shape, lambda s, _: (0,) * len(shape))
     out, out_spec = jax.ShapeDtypeStruct((2, 512, 256), F32), whole(2, 512, 256)
     if part_out == "send":
-        out = jax.ShapeDtypeStruct((2, 512, 256), BF16)
+        out, out_spec = jax.ShapeDtypeStruct((len(parts), 512, 256), BF16), whole(len(parts), 512, 256)
     elif part_out == "keep":
         out = jax.ShapeDtypeStruct((2, 2, 512, 256), F32)
         out_spec = pl.BlockSpec((1, 2, 512, 256), lambda s, place: (place[0], 0, 0, 0))
     starts = [] if start is None else [start]
     return pl.pallas_call(
-        functools.partial(correlate_kernel, pairs, picks, part_out, start is not None),
+        functools.partial(correlate_kernel, pairs, picks, parts, part_out, start is not None),
         grid_spec=pltpu.PrefetchScalarGridSpec(
             num_scalar_prefetch=1,
             grid=(1,),
-            in_specs=[pl.BlockSpec(memory_space=pl.ANY)] * 8 + [whole(2, 512, 256)] * len(starts),
+            in_specs=[pl.BlockSpec(memory_space=pl.ANY)] * 8
+            + [pl.BlockSpec((len(parts), 512, 256), lambda s, _: (parts[0] // len(parts), 0, 0))] * len(starts),
             out_specs=out_spec,
             scratch_shapes=[
                 pltpu.VMEM((4, 4, 2, 512, 128), BF16),
@@ -266,32 +267,42 @@
 SEND = ((0, 1), (1, 0))
 
 
-def finish_kernel(got, whole, out, wide, sems):
+def finish_kernel(to, got, whole, out, narrow, wide, in_sems, out_sems):
     del whole
     slot = 1 - lax.axis_index("col") % 2
-    copies = []
-    for part in range(2):
-        for half in range(2):
-            rows = pl.ds(half * 256, 256)
-            wide[part, rows, :] = got[part, rows, :].astype(F32)
-            copies.append(
-                pltpu.make_async_copy(
-                    wide.at[part, rows], out.at[slot, part, rows], sems.at[2 * part + half]
-                )
-            )
-            copies[-1].start()
-    for copy in copies:
+    blocks = [(part, pl.ds(half * 256, 256)) for part in range(got.shape[0]) for half in range(2)]
+    ins = [
+        pltpu.make_async_copy(got.at[part, rows], narrow.at[part, rows], in_sems.at[n])
+        for n, (part, rows) in enumerate(blocks)
+    ]
+    outs = [
+        pltpu.make_async_copy(wide.at[part, rows], out.at[slot, to + part, rows], out_sems.at[n])
+        for n, (part, rows) in enumerate(blocks)
+    ]
+    for copy in ins:
+        copy.start()
+    for n, (part, rows) in enumerate(blocks):
+        ins[n].wait()
+        wide[part, rows, :] = narrow[part, rows, :].astype(F32)
+        outs[n].start()
+    for copy in outs:
         copy.wait()
 
 
-def finish(got, whole):
+def finish(got, whole, part):
     return pl.pallas_call(
-        finish_kernel,
-        in_specs=[pl.BlockSpec(memory_space=pltpu.VMEM), pl.BlockSpec(memory_space=pl.ANY)],
+        functools.partial(finish_kernel, part),
+        in_specs=[pl.BlockSpec(memory_space=pl.ANY)] * 2,
         out_specs=pl.BlockSpec(memory_space=pl.ANY),
-        scratch_shapes=[pltpu.VMEM((2, 512, 256), F32), pltpu.SemaphoreType.DMA((4,))],
+        scratch_shapes=[
+            pltpu.VMEM(got.shape, BF16),
+            pltpu.VMEM(got.shape, F32),
+            pltpu.SemaphoreType.DMA((2,)),
+            pltpu.SemaphoreType.DMA((2,)),
+        ],
         out_shape=jax.ShapeDtypeStruct((2, 2, 512, 256), F32),
         input_output_aliases={1: 0},
+        compiler_params=pltpu.CompilerParams(vmem_limit_bytes=8 << 20),
         name="finish",
     )(got, whole)
 
@@ -365,10 +376,17 @@
     }
     keep_early = correlate(place, pieces["y1"], pieces["xP"], KEEP, None, "sum")
     send_early = correlate(place, pieces["y1"], pieces["xQ"], SEND, (0, 1), "sum")
-    leaves = correlate(place, pieces["y2"], pieces["xQ"], SEND, (1, 0), "send", send_early)
-    arrived = send(leaves, HALVES)
+    arrived, wait = [], (keep_early,)
+    for part in range(2):
+        leaves = correlate(
+            after(place, *wait), pieces["y2"], pieces["xQ"], SEND, (1, 0), "send", send_early, (part,)
+        )
+        arrived.append(send(leaves, HALVES))
+        wait = (leaves,)
     stays = correlate(after(place, leaves), pieces["y2"], pieces["xS"], KEEP, None, "keep", keep_early)
-    return finish(arrived, stays)
+    for part, half in enumerate(arrived):
+        stays = finish(half, stays, part)
+    return stays
 
 
 def solution(mesh):

time: 136 us -> 133 us (0.978)
  waiting for transfers between devices: 44.6 us -> 39.8 us
  starting transfers between devices: 47.3 us -> 49.1 us
  Pallas kernels: 35.5 us -> 37.2 us
    ppermute x30 -> x31, waiting for transfers between devices: 44.6 us -> 39.8 us  [send(): return lax.ppermute(value, AXES, pairs)]
    ppermute x30 -> x31, starting transfers between devices: 47.3 us -> 49.1 us  [send(): return lax.ppermute(value, AXES, pairs)]
    pallas_call x5 -> x7, Pallas kernels: 17.8 us -> 19.6 us  [the longest x5 17.3 us: correlate(): pl.pallas_call(functools.partial(correlate_kernel, pairs, picks, parts, p...]
  transfers between devices with their start and end apart: 30 -> 31, of which waited for: 11 -> 10; matrix products, arithmetic and copies ran while one was open for 2% -> 2% of each run, Pallas kernels for 17% -> 19%
where the time goes in v4:
time: 133 us
  starting transfers between devices  49.1 us (37%)
  waiting for transfers between devices  39.8 us (30%)
  Pallas kernels  37.2 us (28%)
  other arithmetic  3.84 us (3%)
  local copies, waits for them, and re-layouts  2.24 us (2%)
    ppermute x31, starting transfers between devices, send(): return lax.ppermute(value, AXES, pairs)  49.1 us
    ppermute x31, waiting for transfers between devices, send(): return lax.ppermute(value, AXES, pairs)  39.8 us
    pallas_call x2, Pallas kernels, spectra(): pl.pallas_call(functools.partial(spectra_kernel, width // 128), grid_spec...  17.6 us
    pallas_call x5, Pallas kernels, correlate(): pl.pallas_call(functools.partial(correlate_kernel, pairs, picks, parts, p...  17.3 us
  transfers between devices with their start and end apart: 31, of which 10 were waited for; matrix products, arithmetic and copies ran while one was open for 2% of the time, Pallas kernels for 19%

profile of v4, /device:TPU:1, one launch (start us, length us, event | category | flops | bytes accessed | tf_op | source)
XLA Modules:
  0.0 132.7 jit_solution(15541681194614945756)
XLA Ops:
  2.5 10.7 %spectra.2 = (bf16[1024,128]{1,0:T(8,128)(2,1)S(1)}, bf16[1024,128]{1,0:T(8,128)(2,1)S(1)}, bf16[1024,128]{1,0:T(8,128)(2,1)}, bf16[1024,128]{1,0:T(8,128)(2,1)}...) custom-call(s32[10]{0:T(128)S(1)} %stack.128.place, ...), custom_call_target="tpu_custom_call" | custom-call | flops 8589934592 | bytes 10485760 | tf_op jit(solution)/shard_map/spectra/pallas_call | solution.py:151
  13.2 1.4 %collective-permute-start = (bf16[1024,128]{1,0:T(8,128)(2,1)S(1)}, bf16[1024,128]{1,0:T(8,128)(2,1)}, u32[]{:S(2)}, u32[]{:S(2)}) collective-permute-start(bf16[1024,128]{1,0:T(8,128)(2,1)S(1)} %get-tuple-element.43), channel_id=1, source_target_pairs={{0,32},{1,33},{2,34},{3,35},{4,36},{5,37},{6,38},{7,39},{8,40},{9,... | collective-permute-start | bytes 786440 | tf_op jit(solution)/shard_map/send_Acc/ppermute | solution.py:71
  14.6 3.8 %collective-permute-start.1 = (bf16[1024,128]{1,0:T(8,128)(2,1)}, bf16[1024,128]{1,0:T(8,128)(2,1)}, u32[]{:S(2)}, u32[]{:S(2)}) collective-permute-start(bf16[1024,128]{1,0:T(8,128)(2,1)} %get-tuple-element.44), channel_id=1, source_target_pairs={{0,1},{1,0},{2,3},{3,2},{4,5},{5,4},{6,7},{7,6},{8,9},{9,8},{10,11... | collective-permute-start | bytes 786440 | tf_op jit(solution)/shard_map/send_Aza/ppermute | solution.py:71
  18.5 3.3 %collective-permute-start.4 = (bf16[1024,128]{1,0:T(8,128)(2,1)S(1)}, bf16[1024,128]{1,0:T(8,128)(2,1)}, u32[]{:S(2)}, u32[]{:S(2)}) collective-permute-start(bf16[1024,128]{1,0:T(8,128)(2,1)S(1)} %get-tuple-element.47), channel_id=1, source_target_pairs={{0,33},{1,32},{2,35},{3,34},{4,37},{5,36},{6,39},{7,38},{8,41},{9,... | collective-permute-start | bytes 786440 | tf_op jit(solution)/shard_map/send_Azac/ppermute | solution.py:71
  22.1 6.9 %spectra.3 = (bf16[1024,128]{1,0:T(8,128)(2,1)S(1)}, bf16[1024,128]{1,0:T(8,128)(2,1)S(1)}, bf16[1024,128]{1,0:T(8,128)(2,1)S(1)}, bf16[1024,128]{1,0:T(8,128)(2...) custom-call(s32[10]{0:T(128)S(1)} %stack.128.place, ...), custom_call_target="tpu_custom_call" | custom-call | flops 8589934592 | bytes 10485760 | tf_op jit(solution)/shard_map/spectra/pallas_call | solution.py:151
  29.8 2.7 %collective-permute-start.12 = (bf16[1024,128]{1,0:T(8,128)(2,1)}, bf16[1024,128]{1,0:T(8,128)(2,1)S(1)}, u32[]{:S(2)}, u32[]{:S(2)}) collective-permute-start(bf16[1024,128]{1,0:T(8,128)(2,1)} %copy-done), channel_id=1, source_target_pairs={{0,1},{1,0},{2,3},{3,2},{4,5},{5,4},{6,7},{7,6},{8,9},{9,8},{10,11... | collective-permute-start | bytes 786440 | tf_op jit(solution)/shard_map/send_Bza/ppermute | solution.py:71
  32.4 1.3 broadcast_select_fusion
  34.8 1.4 %collective-permute-start.6 = (bf16[4,2,512,128]{3,2,1,0:T(8,128)(2,1)S(1)}, bf16[4,2,512,128]{3,2,1,0:T(8,128)(2,1)S(1)}, u32[]{:S(2)}, u32[]{:S(2)}) collective-permute-start(bf16[4,2,512,128]{3,2,1,0:T(8,128)(2,1)S(1)} %pad_maximum_fusion.refs_0_), channel_id=1, source_target_pairs={{0,6},{1,7},{2,4},{3,5},{4,2},{5,3},{6,0},{7,1},{8,14},{9,15},{10,... | collective-permute-start | bytes 3145736 | tf_op jit(solution)/shard_map/send_y1b/ppermute | solution.py:71
  39.0 1.3 collective-permute-start.10
  40.3 3.8 %collective-permute-done.15 = bf16[1024,128]{1,0:T(8,128)(2,1)S(1)} collective-permute-done((bf16[1024,128]{1,0:T(8,128)(2,1)S(1)}, bf16[1024,128]{1,0:T(8,128)(2,1)S(1)}, u32[]{:S(2)}, u32[]{:S(2)}) %collective-permute-start.15) | collective-permute-done | bytes 262176 | tf_op jit(solution)/shard_map/send_Bzbc/ppermute | solution.py:71
  44.0 2.5 %collective-permute-start.9 = (bf16[2,2,2,256,128]{4,3,2,1,0:T(8,128)(2,1)S(1)}, bf16[2,2,2,256,128]{4,3,2,1,0:T(8,128)(2,1)S(1)}, u32[]{:S(2)}, u32[]{:S(2)}) collective-permute-start(bf16[2,2,2,256,128]{4,3,2,1,0:T(8,128)(2,1)S(1)} %pad_maximum_fusion.5.refs_4_), channel_id=1, source_target_pairs={{0,8},{1,9},{2,10},{3,11},{4,12},{5,13},{6,14},{7,15},{8,0},{9,1},... | collective-permute-start | bytes 1572872 | tf_op jit(solution)/shard_map/send_xPa/ppermute | solution.py:71
  47.6 5.0 %collective-permute-done.16 = bf16[1024,128]{1,0:T(8,128)(2,1)S(1)} collective-permute-done((bf16[1024,128]{1,0:T(8,128)(2,1)S(1)}, bf16[1024,128]{1,0:T(8,128)(2,1)S(1)}, u32[]{:S(2)}, u32[]{:S(2)}) %collective-permute-start.16) | collective-permute-done | bytes 262176 | tf_op jit(solution)/shard_map/send_Bzac/ppermute | solution.py:71
  52.6 1.5 %collective-permute-start.14 = (bf16[1024,128]{1,0:T(8,128)(2,1)S(1)}, bf16[1024,128]{1,0:T(8,128)(2,1)S(1)}, u32[]{:S(2)}, u32[]{:S(2)}) collective-permute-start(bf16[1024,128]{1,0:T(8,128)(2,1)S(1)} %get-tuple-element.58), channel_id=1, source_target_pairs={{0,64},{1,65},{2,66},{3,67},{4,68},{5,69},{6,70},{7,71},{8,72},{9,... | collective-permute-start | bytes 786440 | tf_op jit(solution)/shard_map/send_Az2/ppermute | solution.py:71
  54.1 3.3 %collective-permute-start.17 = (bf16[1024,128]{1,0:T(8,128)(2,1)S(1)}, bf16[1024,128]{1,0:T(8,128)(2,1)S(1)}, u32[]{:S(2)}, u32[]{:S(2)}) collective-permute-start(bf16[1024,128]{1,0:T(8,128)(2,1)S(1)} %get-tuple-element.63), channel_id=1, source_target_pairs={{0,96},{1,97},{2,98},{3,99},{4,100},{5,101},{6,102},{7,103},{8,104... | collective-permute-start | bytes 786440 | tf_op jit(solution)/shard_map/send_Az2c/ppermute | solution.py:71
  57.4 2.5 %collective-permute-start.11 = (bf16[2,2,2,256,128]{4,3,2,1,0:T(8,128)(2,1)S(1)}, bf16[2,2,2,256,128]{4,3,2,1,0:T(8,128)(2,1)S(1)}, u32[]{:S(2)}, u32[]{:S(2)}) collective-permute-start(bf16[2,2,2,256,128]{4,3,2,1,0:T(8,128)(2,1)S(1)} %collective-permute-done.10.refs_6_), channel_id=1, source_target_pairs={{0,8},{1,9},{2,10},{3,11},{4,12},{5,13},{6,14},{7,15},{8,0},{9,1},... | collective-permute-start | bytes 1572872 | tf_op jit(solution)/shard_map/send_xPf/ppermute | solution.py:71
  60.2 1.8 %collective-permute-start.7 = (bf16[4,2,512,128]{3,2,1,0:T(8,128)(2,1)S(1)}, bf16[4,2,512,128]{3,2,1,0:T(8,128)(2,1)S(1)}, u32[]{:S(2)}, u32[]{:S(2)}) collective-permute-start(bf16[4,2,512,128]{3,2,1,0:T(8,128)(2,1)S(1)} %collective-permute-done.6.refs_2_), channel_id=1, source_target_pairs={{0,2},{1,3},{2,0},{3,1},{4,6},{5,7},{6,4},{7,5},{8,10},{9,11},{10,... | collective-permute-start | bytes 3145736 | tf_op jit(solution)/shard_map/send_y1f/ppermute | solution.py:71
  62.1 5.7 %collective-permute-done.17 = bf16[1024,128]{1,0:T(8,128)(2,1)S(1)} collective-permute-done((bf16[1024,128]{1,0:T(8,128)(2,1)S(1)}, bf16[1024,128]{1,0:T(8,128)(2,1)S(1)}, u32[]{:S(2)}, u32[]{:S(2)}) %collective-permute-start.17) | collective-permute-done | bytes 262176 | tf_op jit(solution)/shard_map/send_Az2c/ppermute | solution.py:71
  68.6 2.5 %collective-permute-start.21 = (bf16[4,2,2,256,128]{4,3,2,1,0:T(8,128)(2,1)S(1)}, bf16[4,2,2,256,128]{4,3,2,1,0:T(8,128)(2,1)S(1)}, u32[]{:S(2)}, u32[]{:S(2)}) collective-permute-start(bf16[4,2,2,256,128]{4,3,2,1,0:T(8,128)(2,1)S(1)} %pad_maximum_fusion.2.refs_4_), channel_id=1, source_target_pairs={{0,8},{1,9},{2,10},{3,11},{4,12},{5,13},{6,14},{7,15},{8,0},{9,1},... | collective-permute-start | bytes 3145736 | tf_op jit(solution)/shard_map/send_xQa/ppermute | solution.py:71
  72.3 8.3 %collective-permute-done.22.refs_6_ = bf16[4,2,2,256,128]{4,3,2,1,0:T(8,128)(2,1)S(1)} collective-permute-done((bf16[4,2,2,256,128]{4,3,2,1,0:T(8,128)(2,1)S(1)}, bf16[4,2,2,256,128]{4,3,2,1,0:T(8,128)(2,1)S(1)}, u32[]{:S(2)}, u32[]{:S(2)}) %collective-permute-start.22) | collective-permute-done | bytes 1048608 | tf_op jit(solution)/shard_map/send_xQb/ppermute | solution.py:71
  81.7 5.3 %collective-permute-start.27 = (bf16[1024,128]{1,0:T(8,128)(2,1)S(1)}, bf16[1024,128]{1,0:T(8,128)(2,1)S(1)}, u32[]{:S(2)}, u32[]{:S(2)}) collective-permute-start(bf16[1024,128]{1,0:T(8,128)(2,1)S(1)} %get-tuple-element.75), channel_id=1, source_target_pairs={{0,96},{1,97},{2,98},{3,99},{4,100},{5,101},{6,102},{7,103},{8,104... | collective-permute-start | bytes 786440 | tf_op jit(solution)/shard_map/send_Bz2c/ppermute | solution.py:71
  87.0 3.6 %collective-permute-done.19.refs_2_ = bf16[4,2,512,128]{3,2,1,0:T(8,128)(2,1)S(1)} collective-permute-done((bf16[4,2,512,128]{3,2,1,0:T(8,128)(2,1)S(1)}, bf16[4,2,512,128]{3,2,1,0:T(8,128)(2,1)S(1)}, u32[]{:S(2)}, u32[]{:S(2)}) %collective-permute-start.19) | collective-permute-done | bytes 1048608 | tf_op jit(solution)/shard_map/send_y2b/ppermute | solution.py:71
  90.6 2.0 %collective-permute-start.18 = (bf16[4,2,512,128]{3,2,1,0:T(8,128)(2,1)S(1)}, bf16[4,2,512,128]{3,2,1,0:T(8,128)(2,1)S(1)}, u32[]{:S(2)}, u32[]{:S(2)}) collective-permute-start(bf16[4,2,512,128]{3,2,1,0:T(8,128)(2,1)S(1)} %pad_maximum_fusion.1.refs_0_), channel_id=1, source_target_pairs={{0,2},{1,3},{2,0},{3,1},{4,6},{5,7},{6,4},{7,5},{8,10},{9,11},{10,... | collective-permute-start | bytes 3145736 | tf_op jit(solution)/shard_map/send_y2a/ppermute | solution.py:71
  93.4 1.4 %collective-permute-start.29 = (bf16[2,2,2,256,128]{4,3,2,1,0:T(8,128)(2,1)S(1)}, bf16[2,2,2,256,128]{4,3,2,1,0:T(8,128)(2,1)S(1)}, u32[]{:S(2)}, u32[]{:S(2)}) collective-permute-start(bf16[2,2,2,256,128]{4,3,2,1,0:T(8,128)(2,1)S(1)} %pad_maximum_fusion.6.refs_4_), channel_id=1, source_target_pairs={{0,24},{1,25},{2,26},{3,27},{4,28},{5,29},{6,30},{7,31},{8,16},{9,... | collective-permute-start | bytes 1572872 | tf_op jit(solution)/shard_map/send_xSb/ppermute | solution.py:71
  94.7 3.7 %correlate.5.refs_8_ = f32[2,512,256]{2,1,0:T(8,128)S(1)} custom-call(s32[10]{0:T(128)S(1)} %stack.128.place, bf16[4,2,512,128]{3,2,1,0:T(8,128)(2,1)S(1)} %pad_maximum_fusion.refs_0_, bf16[4,2,512,128]{3,2,1,0:T(8,128)(2,1)S(1)} %collective-permute-done.5.refs_1_, bf16[4,2,512,128]{3,2,1,0:T(8,128)(2,1)S(1)} %collective-permute-done.6.refs_2_, ...), custom_call_target="tpu_custom_call" | custom-call | flops 2147483648 | bytes 6291456 | tf_op jit(solution)/shard_map/correlate/pallas_call | solution.py:241
  98.4 5.8 %collective-permute-done.29.refs_6_ = bf16[2,2,2,256,128]{4,3,2,1,0:T(8,128)(2,1)S(1)} collective-permute-done((bf16[2,2,2,256,128]{4,3,2,1,0:T(8,128)(2,1)S(1)}, bf16[2,2,2,256,128]{4,3,2,1,0:T(8,128)(2,1)S(1)}, u32[]{:S(2)}, u32[]{:S(2)}) %collective-permute-start.29) | collective-permute-done | bytes 524320 | tf_op jit(solution)/shard_map/send_xSb/ppermute | solution.py:71
  104.2 2.5 %collective-permute-start.30 = (bf16[2,2,2,256,128]{4,3,2,1,0:T(8,128)(2,1)S(1)}, bf16[2,2,2,256,128]{4,3,2,1,0:T(8,128)(2,1)S(1)}, u32[]{:S(2)}, u32[]{:S(2)}) collective-permute-start(bf16[2,2,2,256,128]{4,3,2,1,0:T(8,128)(2,1)S(1)} %collective-permute-done.29.refs_6_), channel_id=1, source_target_pairs={{0,8},{1,9},{2,10},{3,11},{4,12},{5,13},{6,14},{7,15},{8,0},{9,1},... | collective-permute-start | bytes 1572872 | tf_op jit(solution)/shard_map/send_xSf/ppermute | solution.py:71
  106.9 3.7 %correlate.6.refs_8_ = f32[2,512,256]{2,1,0:T(8,128)S(1)} custom-call(s32[10]{0:T(128)S(1)} %stack.128.place, bf16[4,2,512,128]{3,2,1,0:T(8,128)(2,1)S(1)} %pad_maximum_fusion.refs_0_, bf16[4,2,512,128]{3,2,1,0:T(8,128)(2,1)S(1)} %collective-permute-done.5.refs_1_, bf16[4,2,512,128]{3,2,1,0:T(8,128)(2,1)S(1)} %collective-permute-done.6.refs_2_, ...), custom_call_target="tpu_custom_call" | custom-call | flops 2147483648 | bytes 6291456 | tf_op jit(solution)/shard_map/correlate/pallas_call | solution.py:241
  110.6 6.2 %collective-permute-done.20.refs_3_ = bf16[4,2,512,128]{3,2,1,0:T(8,128)(2,1)S(1)} collective-permute-done((bf16[4,2,512,128]{3,2,1,0:T(8,128)(2,1)S(1)}, bf16[4,2,512,128]{3,2,1,0:T(8,128)(2,1)S(1)}, u32[]{:S(2)}, u32[]{:S(2)}) %collective-permute-start.20) | collective-permute-done | bytes 1048608 | tf_op jit(solution)/shard_map/send_y2f/ppermute | solution.py:71
  116.7 2.6 %correlate.7 = bf16[1,512,256]{2,1,0:T(8,128)(2,1)S(1)} custom-call(s32[10]{0:T(128)S(1)} %stack.128.place, bf16[4,2,512,128]{3,2,1,0:T(8,128)(2,1)S(1)} %pad_maximum_fusion.1.refs_0_, bf16[4,2,512,128]{3,2,1,0:T(8,128)(2,1)S(1)} %collective-permute-done.18.refs_1_, bf16[4,2,512,128]{3,2,1,0:T(8,128)(2,1)S(1)} %collective-permute-done.19.refs_2_, ...), custom_call_target="tpu_custom_call" | custom-call | flops 34359738368 | bytes 6291456 | tf_op jit(solution)/shard_map/correlate/pallas_call | solution.py:241
  119.4 2.7 %collective-permute-start.25 = (bf16[1,512,256]{2,1,0:T(8,128)(2,1)S(1)}, bf16[1,512,256]{2,1,0:T(8,128)(2,1)S(1)}, u32[]{:S(2)}, u32[]{:S(2)}) collective-permute-start(bf16[1,512,256]{2,1,0:T(8,128)(2,1)S(1)} %correlate.7), channel_id=1, source_target_pairs={{0,1},{1,0},{2,3},{3,2},{4,5},{5,4},{6,7},{7,6},{8,9},{9,8},{10,11... | collective-permute-start | bytes 786440 | tf_op jit(solution)/shard_map/ppermute | solution.py:71
  122.0 2.6 %correlate.8 = bf16[1,512,256]{2,1,0:T(8,128)(2,1)S(1)} custom-call(s32[10]{0:T(128)S(1)} %stack.128.place, bf16[4,2,512,128]{3,2,1,0:T(8,128)(2,1)S(1)} %pad_maximum_fusion.1.refs_0_, bf16[4,2,512,128]{3,2,1,0:T(8,128)(2,1)S(1)} %collective-permute-done.18.refs_1_, bf16[4,2,512,128]{3,2,1,0:T(8,128)(2,1)S(1)} %collective-permute-done.19.refs_2_, ...), custom_call_target="tpu_custom_call" | custom-call | flops 34359738368 | bytes 6291456 | tf_op jit(solution)/shard_map/correlate/pallas_call | solution.py:241
  124.8 4.7 %correlate.9.whole = f32[2,2,512,256]{3,2,1,0:T(8,128)} custom-call(s32[10]{0:T(128)S(1)} %stack.128.place, bf16[4,2,512,128]{3,2,1,0:T(8,128)(2,1)S(1)} %pad_maximum_fusion.1.refs_0_, bf16[4,2,512,128]{3,2,1,0:T(8,128)(2,1)S(1)} %collective-permute-done.18.refs_1_, bf16[4,2,512,128]{3,2,1,0:T(8,128)(2,1)S(1)} %collective-permute-done.19.refs_2_, ...), custom_call_target="tpu_custom_call" | custom-call | flops 2147483648 | bytes 6291456 | tf_op jit(solution)/shard_map/correlate/pallas_call | solution.py:241
  (69 shorter events, 16.0 us)
Async XLA Ops:
  2.5 19.2 %copy-start.1 = (s32[256]{0:T(256)S(1)}, s32[256]{0:T(256)}, u32[]{:S(2)}) copy-start(s32[256]{0:T(256)} %param.8) | copy-start | bytes 3076
  13.2 20.5 %collective-permute-start = (bf16[1024,128]{1,0:T(8,128)(2,1)S(1)}, bf16[1024,128]{1,0:T(8,128)(2,1)}, u32[]{:S(2)}, u32[]{:S(2)}) collective-permute-start(bf16[1024,128]{1,0:T(8,128)(2,1)S(1)} %get-tuple-element.43), channel_id=1, source_target_pairs={{0,32},{1,33},{2,34},{3,35},{4,36},{5,37},{6,38},{7,39},{8,40},{9,... | collective-permute-start | bytes 786440 | tf_op jit(solution)/shard_map/send_Acc/ppermute | solution.py:71
  14.6 15.1 %collective-permute-start.1 = (bf16[1024,128]{1,0:T(8,128)(2,1)}, bf16[1024,128]{1,0:T(8,128)(2,1)}, u32[]{:S(2)}, u32[]{:S(2)}) collective-permute-start(bf16[1024,128]{1,0:T(8,128)(2,1)} %get-tuple-element.44), channel_id=1, source_target_pairs={{0,1},{1,0},{2,3},{3,2},{4,5},{5,4},{6,7},{7,6},{8,9},{9,8},{10,11... | collective-permute-start | bytes 786440 | tf_op jit(solution)/shard_map/send_Aza/ppermute | solution.py:71
  18.5 11.3 %collective-permute-start.2 = (bf16[1024,128]{1,0:T(8,128)(2,1)}, bf16[1024,128]{1,0:T(8,128)(2,1)}, u32[]{:S(2)}, u32[]{:S(2)}) collective-permute-start(bf16[1024,128]{1,0:T(8,128)(2,1)} %get-tuple-element.45), channel_id=1, source_target_pairs={{0,97},{1,96},{2,99},{3,98},{4,101},{5,100},{6,103},{7,102},{8,105... | collective-permute-start | bytes 786440 | tf_op jit(solution)/shard_map/send_Azbc/ppermute | solution.py:71
  18.5 14.0 %collective-permute-start.3 = (bf16[1024,128]{1,0:T(8,128)(2,1)S(1)}, bf16[1024,128]{1,0:T(8,128)(2,1)}, u32[]{:S(2)}, u32[]{:S(2)}) collective-permute-start(bf16[1024,128]{1,0:T(8,128)(2,1)S(1)} %get-tuple-element.46), channel_id=1, source_target_pairs={{0,65},{1,64},{2,67},{3,66},{4,69},{5,68},{6,71},{7,70},{8,73},{9,... | collective-permute-start | bytes 786440 | tf_op jit(solution)/shard_map/send_Azb/ppermute | solution.py:71
  18.5 14.0 %collective-permute-start.4 = (bf16[1024,128]{1,0:T(8,128)(2,1)S(1)}, bf16[1024,128]{1,0:T(8,128)(2,1)}, u32[]{:S(2)}, u32[]{:S(2)}) collective-permute-start(bf16[1024,128]{1,0:T(8,128)(2,1)S(1)} %get-tuple-element.47), channel_id=1, source_target_pairs={{0,33},{1,32},{2,35},{3,34},{4,37},{5,36},{6,39},{7,38},{8,41},{9,... | collective-permute-start | bytes 786440 | tf_op jit(solution)/shard_map/send_Azac/ppermute | solution.py:71
  29.7 9.2 %collective-permute-start.8 = (bf16[1024,128]{1,0:T(8,128)(2,1)S(1)}, bf16[1024,128]{1,0:T(8,128)(2,1)S(1)}, u32[]{:S(2)}, u32[]{:S(2)}) collective-permute-start(bf16[1024,128]{1,0:T(8,128)(2,1)S(1)} %get-tuple-element.51), channel_id=1, source_target_pairs={{0,32},{1,33},{2,34},{3,35},{4,36},{5,37},{6,38},{7,39},{8,40},{9,... | collective-permute-start | bytes 786440 | tf_op jit(solution)/shard_map/send_Bcc/ppermute | solution.py:71
  29.8 8.3 %collective-permute-start.12 = (bf16[1024,128]{1,0:T(8,128)(2,1)}, bf16[1024,128]{1,0:T(8,128)(2,1)S(1)}, u32[]{:S(2)}, u32[]{:S(2)}) collective-permute-start(bf16[1024,128]{1,0:T(8,128)(2,1)} %copy-done), channel_id=1, source_target_pairs={{0,1},{1,0},{2,3},{3,2},{4,5},{5,4},{6,7},{7,6},{8,9},{9,8},{10,11... | collective-permute-start | bytes 786440 | tf_op jit(solution)/shard_map/send_Bza/ppermute | solution.py:71
  34.8 25.2 %collective-permute-start.6 = (bf16[4,2,512,128]{3,2,1,0:T(8,128)(2,1)S(1)}, bf16[4,2,512,128]{3,2,1,0:T(8,128)(2,1)S(1)}, u32[]{:S(2)}, u32[]{:S(2)}) collective-permute-start(bf16[4,2,512,128]{3,2,1,0:T(8,128)(2,1)S(1)} %pad_maximum_fusion.refs_0_), channel_id=1, source_target_pairs={{0,6},{1,7},{2,4},{3,5},{4,2},{5,3},{6,0},{7,1},{8,14},{9,15},{10,... | collective-permute-start | bytes 3145736 | tf_op jit(solution)/shard_map/send_y1b/ppermute | solution.py:71
  36.2 7.8 %collective-permute-start.15 = (bf16[1024,128]{1,0:T(8,128)(2,1)S(1)}, bf16[1024,128]{1,0:T(8,128)(2,1)S(1)}, u32[]{:S(2)}, u32[]{:S(2)}) collective-permute-start(bf16[1024,128]{1,0:T(8,128)(2,1)S(1)} %get-tuple-element.61), channel_id=1, source_target_pairs={{0,97},{1,96},{2,99},{3,98},{4,101},{5,100},{6,103},{7,102},{8,105... | collective-permute-start | bytes 786440 | tf_op jit(solution)/shard_map/send_Bzbc/ppermute | solution.py:71
  37.3 30.5 %collective-permute-start.5 = (bf16[4,2,512,128]{3,2,1,0:T(8,128)(2,1)S(1)}, bf16[4,2,512,128]{3,2,1,0:T(8,128)(2,1)S(1)}, u32[]{:S(2)}, u32[]{:S(2)}) collective-permute-start(bf16[4,2,512,128]{3,2,1,0:T(8,128)(2,1)S(1)} %pad_maximum_fusion.refs_0_), channel_id=1, source_target_pairs={{0,2},{1,3},{2,0},{3,1},{4,6},{5,7},{6,4},{7,5},{8,10},{9,11},{10,... | collective-permute-start | bytes 3145736 | tf_op jit(solution)/shard_map/send_y1a/ppermute | solution.py:71
  38.1 8.4 %collective-permute-start.13 = (bf16[1024,128]{1,0:T(8,128)(2,1)S(1)}, bf16[1024,128]{1,0:T(8,128)(2,1)S(1)}, u32[]{:S(2)}, u32[]{:S(2)}) collective-permute-start(bf16[1024,128]{1,0:T(8,128)(2,1)S(1)} %get-tuple-element.57), channel_id=1, source_target_pairs={{0,65},{1,64},{2,67},{3,66},{4,69},{5,68},{6,71},{7,70},{8,73},{9,... | collective-permute-start | bytes 786440 | tf_op jit(solution)/shard_map/send_Bzb/ppermute | solution.py:71
  39.0 15.1 %collective-permute-start.10 = (bf16[2,2,2,256,128]{4,3,2,1,0:T(8,128)(2,1)S(1)}, bf16[2,2,2,256,128]{4,3,2,1,0:T(8,128)(2,1)S(1)}, u32[]{:S(2)}, u32[]{:S(2)}) collective-permute-start(bf16[2,2,2,256,128]{4,3,2,1,0:T(8,128)(2,1)S(1)} %pad_maximum_fusion.5.refs_4_), channel_id=1, source_target_pairs={{0,24},{1,25},{2,26},{3,27},{4,28},{5,29},{6,30},{7,31},{8,16},{9,... | collective-permute-start | bytes 1572872 | tf_op jit(solution)/shard_map/send_xPb/ppermute | solution.py:71
  44.0 13.4 %collective-permute-start.9 = (bf16[2,2,2,256,128]{4,3,2,1,0:T(8,128)(2,1)S(1)}, bf16[2,2,2,256,128]{4,3,2,1,0:T(8,128)(2,1)S(1)}, u32[]{:S(2)}, u32[]{:S(2)}) collective-permute-start(bf16[2,2,2,256,128]{4,3,2,1,0:T(8,128)(2,1)S(1)} %pad_maximum_fusion.5.refs_4_), channel_id=1, source_target_pairs={{0,8},{1,9},{2,10},{3,11},{4,12},{5,13},{6,14},{7,15},{8,0},{9,1},... | collective-permute-start | bytes 1572872 | tf_op jit(solution)/shard_map/send_xPa/ppermute | solution.py:71
  46.5 6.1 %collective-permute-start.16 = (bf16[1024,128]{1,0:T(8,128)(2,1)S(1)}, bf16[1024,128]{1,0:T(8,128)(2,1)S(1)}, u32[]{:S(2)}, u32[]{:S(2)}) collective-permute-start(bf16[1024,128]{1,0:T(8,128)(2,1)S(1)} %get-tuple-element.62), channel_id=1, source_target_pairs={{0,33},{1,32},{2,35},{3,34},{4,37},{5,36},{6,39},{7,38},{8,41},{9,... | collective-permute-start | bytes 786440 | tf_op jit(solution)/shard_map/send_Bzac/ppermute | solution.py:71
  52.6 7.6 %collective-permute-start.14 = (bf16[1024,128]{1,0:T(8,128)(2,1)S(1)}, bf16[1024,128]{1,0:T(8,128)(2,1)S(1)}, u32[]{:S(2)}, u32[]{:S(2)}) collective-permute-start(bf16[1024,128]{1,0:T(8,128)(2,1)S(1)} %get-tuple-element.58), channel_id=1, source_target_pairs={{0,64},{1,65},{2,66},{3,67},{4,68},{5,69},{6,70},{7,71},{8,72},{9,... | collective-permute-start | bytes 786440 | tf_op jit(solution)/shard_map/send_Az2/ppermute | solution.py:71
  54.1 13.6 %collective-permute-start.17 = (bf16[1024,128]{1,0:T(8,128)(2,1)S(1)}, bf16[1024,128]{1,0:T(8,128)(2,1)S(1)}, u32[]{:S(2)}, u32[]{:S(2)}) collective-permute-start(bf16[1024,128]{1,0:T(8,128)(2,1)S(1)} %get-tuple-element.63), channel_id=1, source_target_pairs={{0,96},{1,97},{2,98},{3,99},{4,100},{5,101},{6,102},{7,103},{8,104... | collective-permute-start | bytes 786440 | tf_op jit(solution)/shard_map/send_Az2c/ppermute | solution.py:71
  57.4 11.2 %collective-permute-start.11 = (bf16[2,2,2,256,128]{4,3,2,1,0:T(8,128)(2,1)S(1)}, bf16[2,2,2,256,128]{4,3,2,1,0:T(8,128)(2,1)S(1)}, u32[]{:S(2)}, u32[]{:S(2)}) collective-permute-start(bf16[2,2,2,256,128]{4,3,2,1,0:T(8,128)(2,1)S(1)} %collective-permute-done.10.refs_6_), channel_id=1, source_target_pairs={{0,8},{1,9},{2,10},{3,11},{4,12},{5,13},{6,14},{7,15},{8,0},{9,1},... | collective-permute-start | bytes 1572872 | tf_op jit(solution)/shard_map/send_xPf/ppermute | solution.py:71
  60.0 20.6 %collective-permute-start.22 = (bf16[4,2,2,256,128]{4,3,2,1,0:T(8,128)(2,1)S(1)}, bf16[4,2,2,256,128]{4,3,2,1,0:T(8,128)(2,1)S(1)}, u32[]{:S(2)}, u32[]{:S(2)}) collective-permute-start(bf16[4,2,2,256,128]{4,3,2,1,0:T(8,128)(2,1)S(1)} %pad_maximum_fusion.2.refs_4_), channel_id=1, source_target_pairs={{0,24},{1,25},{2,26},{3,27},{4,28},{5,29},{6,30},{7,31},{8,16},{9,... | collective-permute-start | bytes 3145736 | tf_op jit(solution)/shard_map/send_xQb/ppermute | solution.py:71
  60.2 21.4 %collective-permute-start.7 = (bf16[4,2,512,128]{3,2,1,0:T(8,128)(2,1)S(1)}, bf16[4,2,512,128]{3,2,1,0:T(8,128)(2,1)S(1)}, u32[]{:S(2)}, u32[]{:S(2)}) collective-permute-start(bf16[4,2,512,128]{3,2,1,0:T(8,128)(2,1)S(1)} %collective-permute-done.6.refs_2_), channel_id=1, source_target_pairs={{0,2},{1,3},{2,0},{3,1},{4,6},{5,7},{6,4},{7,5},{8,10},{9,11},{10,... | collective-permute-start | bytes 3145736 | tf_op jit(solution)/shard_map/send_y1f/ppermute | solution.py:71
  67.9 22.8 %collective-permute-start.19 = (bf16[4,2,512,128]{3,2,1,0:T(8,128)(2,1)S(1)}, bf16[4,2,512,128]{3,2,1,0:T(8,128)(2,1)S(1)}, u32[]{:S(2)}, u32[]{:S(2)}) collective-permute-start(bf16[4,2,512,128]{3,2,1,0:T(8,128)(2,1)S(1)} %pad_maximum_fusion.1.refs_0_), channel_id=1, source_target_pairs={{0,6},{1,7},{2,4},{3,5},{4,2},{5,3},{6,0},{7,1},{8,14},{9,15},{10,... | collective-permute-start | bytes 3145736 | tf_op jit(solution)/shard_map/send_y2b/ppermute | solution.py:71
  68.6 24.8 %collective-permute-start.21 = (bf16[4,2,2,256,128]{4,3,2,1,0:T(8,128)(2,1)S(1)}, bf16[4,2,2,256,128]{4,3,2,1,0:T(8,128)(2,1)S(1)}, u32[]{:S(2)}, u32[]{:S(2)}) collective-permute-start(bf16[4,2,2,256,128]{4,3,2,1,0:T(8,128)(2,1)S(1)} %pad_maximum_fusion.2.refs_4_), channel_id=1, source_target_pairs={{0,8},{1,9},{2,10},{3,11},{4,12},{5,13},{6,14},{7,15},{8,0},{9,1},... | collective-permute-start | bytes 3145736 | tf_op jit(solution)/shard_map/send_xQa/ppermute | solution.py:71
  71.1 21.6 %collective-permute-start.26 = (bf16[1024,128]{1,0:T(8,128)(2,1)S(1)}, bf16[1024,128]{1,0:T(8,128)(2,1)S(1)}, u32[]{:S(2)}, u32[]{:S(2)}) collective-permute-start(bf16[1024,128]{1,0:T(8,128)(2,1)S(1)} %get-tuple-element.73), channel_id=1, source_target_pairs={{0,64},{1,65},{2,66},{3,67},{4,68},{5,69},{6,70},{7,71},{8,72},{9,... | collective-permute-start | bytes 786440 | tf_op jit(solution)/shard_map/send_Bz2/ppermute | solution.py:71
  80.6 26.1 %collective-permute-start.23 = (bf16[4,2,2,256,128]{4,3,2,1,0:T(8,128)(2,1)S(1)}, bf16[4,2,2,256,128]{4,3,2,1,0:T(8,128)(2,1)S(1)}, u32[]{:S(2)}, u32[]{:S(2)}) collective-permute-start(bf16[4,2,2,256,128]{4,3,2,1,0:T(8,128)(2,1)S(1)} %collective-permute-done.22.refs_6_), channel_id=1, source_target_pairs={{0,8},{1,9},{2,10},{3,11},{4,12},{5,13},{6,14},{7,15},{8,0},{9,1},... | collective-permute-start | bytes 3145736 | tf_op jit(solution)/shard_map/send_xQf/ppermute | solution.py:71
  81.7 11.6 %collective-permute-start.27 = (bf16[1024,128]{1,0:T(8,128)(2,1)S(1)}, bf16[1024,128]{1,0:T(8,128)(2,1)S(1)}, u32[]{:S(2)}, u32[]{:S(2)}) collective-permute-start(bf16[1024,128]{1,0:T(8,128)(2,1)S(1)} %get-tuple-element.75), channel_id=1, source_target_pairs={{0,96},{1,97},{2,98},{3,99},{4,100},{5,101},{6,102},{7,103},{8,104... | collective-permute-start | bytes 786440 | tf_op jit(solution)/shard_map/send_Bz2c/ppermute | solution.py:71
  90.6 19.9 %collective-permute-start.18 = (bf16[4,2,512,128]{3,2,1,0:T(8,128)(2,1)S(1)}, bf16[4,2,512,128]{3,2,1,0:T(8,128)(2,1)S(1)}, u32[]{:S(2)}, u32[]{:S(2)}) collective-permute-start(bf16[4,2,512,128]{3,2,1,0:T(8,128)(2,1)S(1)} %pad_maximum_fusion.1.refs_0_), channel_id=1, source_target_pairs={{0,2},{1,3},{2,0},{3,1},{4,6},{5,7},{6,4},{7,5},{8,10},{9,11},{10,... | collective-permute-start | bytes 3145736 | tf_op jit(solution)/shard_map/send_y2a/ppermute | solution.py:71
  92.7 24.1 %collective-permute-start.20 = (bf16[4,2,512,128]{3,2,1,0:T(8,128)(2,1)S(1)}, bf16[4,2,512,128]{3,2,1,0:T(8,128)(2,1)S(1)}, u32[]{:S(2)}, u32[]{:S(2)}) collective-permute-start(bf16[4,2,512,128]{3,2,1,0:T(8,128)(2,1)S(1)} %collective-permute-done.19.refs_2_), channel_id=1, source_target_pairs={{0,2},{1,3},{2,0},{3,1},{4,6},{5,7},{6,4},{7,5},{8,10},{9,11},{10,... | collective-permute-start | bytes 3145736 | tf_op jit(solution)/shard_map/send_y2f/ppermute | solution.py:71
  93.4 10.8 %collective-permute-start.29 = (bf16[2,2,2,256,128]{4,3,2,1,0:T(8,128)(2,1)S(1)}, bf16[2,2,2,256,128]{4,3,2,1,0:T(8,128)(2,1)S(1)}, u32[]{:S(2)}, u32[]{:S(2)}) collective-permute-start(bf16[2,2,2,256,128]{4,3,2,1,0:T(8,128)(2,1)S(1)} %pad_maximum_fusion.6.refs_4_), channel_id=1, source_target_pairs={{0,24},{1,25},{2,26},{3,27},{4,28},{5,29},{6,30},{7,31},{8,16},{9,... | collective-permute-start | bytes 1572872 | tf_op jit(solution)/shard_map/send_xSb/ppermute | solution.py:71
  104.2 20.6 %collective-permute-start.30 = (bf16[2,2,2,256,128]{4,3,2,1,0:T(8,128)(2,1)S(1)}, bf16[2,2,2,256,128]{4,3,2,1,0:T(8,128)(2,1)S(1)}, u32[]{:S(2)}, u32[]{:S(2)}) collective-permute-start(bf16[2,2,2,256,128]{4,3,2,1,0:T(8,128)(2,1)S(1)} %collective-permute-done.29.refs_6_), channel_id=1, source_target_pairs={{0,8},{1,9},{2,10},{3,11},{4,12},{5,13},{6,14},{7,15},{8,0},{9,1},... | collective-permute-start | bytes 1572872 | tf_op jit(solution)/shard_map/send_xSf/ppermute | solution.py:71
  106.7 18.1 %collective-permute-start.28 = (bf16[2,2,2,256,128]{4,3,2,1,0:T(8,128)(2,1)S(1)}, bf16[2,2,2,256,128]{4,3,2,1,0:T(8,128)(2,1)S(1)}, u32[]{:S(2)}, u32[]{:S(2)}) collective-permute-start(bf16[2,2,2,256,128]{4,3,2,1,0:T(8,128)(2,1)S(1)} %pad_maximum_fusion.6.refs_4_), channel_id=1, source_target_pairs={{0,8},{1,9},{2,10},{3,11},{4,12},{5,13},{6,14},{7,15},{8,0},{9,1},... | collective-permute-start | bytes 1572872 | tf_op jit(solution)/shard_map/send_xSa/ppermute | solution.py:71
  119.4 10.1 %collective-permute-start.25 = (bf16[1,512,256]{2,1,0:T(8,128)(2,1)S(1)}, bf16[1,512,256]{2,1,0:T(8,128)(2,1)S(1)}, u32[]{:S(2)}, u32[]{:S(2)}) collective-permute-start(bf16[1,512,256]{2,1,0:T(8,128)(2,1)S(1)} %correlate.7), channel_id=1, source_target_pairs={{0,1},{1,0},{2,3},{3,2},{4,5},{5,4},{6,7},{7,6},{8,9},{9,8},{10,11... | collective-permute-start | bytes 786440 | tf_op jit(solution)/shard_map/ppermute | solution.py:71
  124.7 6.8 %collective-permute-start.24 = (bf16[1,512,256]{2,1,0:T(8,128)(2,1)S(1)}, bf16[1,512,256]{2,1,0:T(8,128)(2,1)S(1)}, u32[]{:S(2)}, u32[]{:S(2)}) collective-permute-start(bf16[1,512,256]{2,1,0:T(8,128)(2,1)S(1)} %correlate.8), channel_id=1, source_target_pairs={{0,1},{1,0},{2,3},{3,2},{4,5},{5,4},{6,7},{7,6},{8,9},{9,8},{10,11... | collective-permute-start | bytes 786440 | tf_op jit(solution)/shard_map/ppermute | solution.py:71
  (1 other events, 0.7 us)

commit v5 on v4

--- a/solution.py
+++ b/solution.py
@@ -15,7 +15,7 @@
 AXES = ("layer", "row", "col")
 GROUP = 16
 SUB = 8
-STEP = 64
+STEP = 128
 BF16 = jnp.bfloat16
 F32 = jnp.float32
 

time: 133 us -> 131 us (0.985)
  waiting for transfers between devices: 39.8 us -> 42.4 us
  starting transfers between devices: 49.1 us -> 46.8 us
  Pallas kernels: 37.2 us -> 35.3 us
    ppermute x31, waiting for transfers between devices: 39.8 us -> 42.4 us  [send(): return lax.ppermute(value, AXES, pairs)]
    ppermute x31, starting transfers between devices: 49.1 us -> 46.8 us  [send(): return lax.ppermute(value, AXES, pairs)]
    pallas_call x2, Pallas kernels: 17.6 us -> 15.7 us  [spectra(): pl.pallas_call(functools.partial(spectra_kernel, width // 128), grid_spec...]
where the time goes in v5:
time: 131 us
  starting transfers between devices  46.8 us (36%)
  waiting for transfers between devices  42.4 us (32%)
  Pallas kernels  35.3 us (27%)
  other arithmetic  3.84 us (3%)
  local copies, waits for them, and re-layouts  2.24 us (2%)
    ppermute x31, starting transfers between devices, send(): return lax.ppermute(value, AXES, pairs)  46.8 us
    ppermute x31, waiting for transfers between devices, send(): return lax.ppermute(value, AXES, pairs)  42.4 us
    pallas_call x5, Pallas kernels, correlate(): pl.pallas_call(functools.partial(correlate_kernel, pairs, picks, parts, p...  17.3 us
    pallas_call x2, Pallas kernels, spectra(): pl.pallas_call(functools.partial(spectra_kernel, width // 128), grid_spec...  15.7 us
  transfers between devices with their start and end apart: 31, of which 10 were waited for; matrix products, arithmetic and copies ran while one was open for 2% of the time, Pallas kernels for 19%

profile of v5, /device:TPU:1, one launch (start us, length us, event | category | flops | bytes accessed | tf_op | source)
XLA Modules:
  0.0 131.1 jit_solution(3810049254657577554)
XLA Ops:
  2.5 9.2 %spectra.2 = (bf16[1024,128]{1,0:T(8,128)(2,1)S(1)}, bf16[1024,128]{1,0:T(8,128)(2,1)S(1)}, bf16[1024,128]{1,0:T(8,128)(2,1)}, bf16[1024,128]{1,0:T(8,128)(2,1)}...) custom-call(s32[10]{0:T(128)S(1)} %stack.128.place, ...), custom_call_target="tpu_custom_call" | custom-call | flops 8589934592 | bytes 10485760 | tf_op jit(solution)/shard_map/spectra/pallas_call | solution.py:151
  11.7 1.4 %collective-permute-start = (bf16[1024,128]{1,0:T(8,128)(2,1)S(1)}, bf16[1024,128]{1,0:T(8,128)(2,1)}, u32[]{:S(2)}, u32[]{:S(2)}) collective-permute-start(bf16[1024,128]{1,0:T(8,128)(2,1)S(1)} %get-tuple-element.43), channel_id=1, source_target_pairs={{0,32},{1,33},{2,34},{3,35},{4,36},{5,37},{6,38},{7,39},{8,40},{9,... | collective-permute-start | bytes 786440 | tf_op jit(solution)/shard_map/send_Acc/ppermute | solution.py:71
  13.1 3.8 %collective-permute-start.1 = (bf16[1024,128]{1,0:T(8,128)(2,1)}, bf16[1024,128]{1,0:T(8,128)(2,1)}, u32[]{:S(2)}, u32[]{:S(2)}) collective-permute-start(bf16[1024,128]{1,0:T(8,128)(2,1)} %get-tuple-element.44), channel_id=1, source_target_pairs={{0,1},{1,0},{2,3},{3,2},{4,5},{5,4},{6,7},{7,6},{8,9},{9,8},{10,11... | collective-permute-start | bytes 786440 | tf_op jit(solution)/shard_map/send_Aza/ppermute | solution.py:71
  16.9 3.3 %collective-permute-start.4 = (bf16[1024,128]{1,0:T(8,128)(2,1)S(1)}, bf16[1024,128]{1,0:T(8,128)(2,1)}, u32[]{:S(2)}, u32[]{:S(2)}) collective-permute-start(bf16[1024,128]{1,0:T(8,128)(2,1)S(1)} %get-tuple-element.47), channel_id=1, source_target_pairs={{0,33},{1,32},{2,35},{3,34},{4,37},{5,36},{6,39},{7,38},{8,41},{9,... | collective-permute-start | bytes 786440 | tf_op jit(solution)/shard_map/send_Azac/ppermute | solution.py:71
  20.6 6.5 %spectra.3 = (bf16[1024,128]{1,0:T(8,128)(2,1)S(1)}, bf16[1024,128]{1,0:T(8,128)(2,1)S(1)}, bf16[1024,128]{1,0:T(8,128)(2,1)S(1)}, bf16[1024,128]{1,0:T(8,128)(2...) custom-call(s32[10]{0:T(128)S(1)} %stack.128.place, ...), custom_call_target="tpu_custom_call" | custom-call | flops 8589934592 | bytes 10485760 | tf_op jit(solution)/shard_map/spectra/pallas_call | solution.py:151
  27.9 2.6 %collective-permute-start.12 = (bf16[1024,128]{1,0:T(8,128)(2,1)}, bf16[1024,128]{1,0:T(8,128)(2,1)S(1)}, u32[]{:S(2)}, u32[]{:S(2)}) collective-permute-start(bf16[1024,128]{1,0:T(8,128)(2,1)} %copy-done), channel_id=1, source_target_pairs={{0,1},{1,0},{2,3},{3,2},{4,5},{5,4},{6,7},{7,6},{8,9},{9,8},{10,11... | collective-permute-start | bytes 786440 | tf_op jit(solution)/shard_map/send_Bza/ppermute | solution.py:71
  30.5 1.3 broadcast_select_fusion
  32.9 1.4 %collective-permute-start.6 = (bf16[4,2,512,128]{3,2,1,0:T(8,128)(2,1)S(1)}, bf16[4,2,512,128]{3,2,1,0:T(8,128)(2,1)S(1)}, u32[]{:S(2)}, u32[]{:S(2)}) collective-permute-start(bf16[4,2,512,128]{3,2,1,0:T(8,128)(2,1)S(1)} %pad_maximum_fusion.refs_0_), channel_id=1, source_target_pairs={{0,6},{1,7},{2,4},{3,5},{4,2},{5,3},{6,0},{7,1},{8,14},{9,15},{10,... | collective-permute-start | bytes 3145736 | tf_op jit(solution)/shard_map/send_y1b/ppermute | solution.py:71
  36.2 1.2 collective-permute-start.13
  37.4 1.3 collective-permute-start.10
  38.7 3.8 %collective-permute-done.15 = bf16[1024,128]{1,0:T(8,128)(2,1)S(1)} collective-permute-done((bf16[1024,128]{1,0:T(8,128)(2,1)S(1)}, bf16[1024,128]{1,0:T(8,128)(2,1)S(1)}, u32[]{:S(2)}, u32[]{:S(2)}) %collective-permute-start.15) | collective-permute-done | bytes 262176 | tf_op jit(solution)/shard_map/send_Bzbc/ppermute | solution.py:71
  42.5 2.5 %collective-permute-start.9 = (bf16[2,2,2,256,128]{4,3,2,1,0:T(8,128)(2,1)S(1)}, bf16[2,2,2,256,128]{4,3,2,1,0:T(8,128)(2,1)S(1)}, u32[]{:S(2)}, u32[]{:S(2)}) collective-permute-start(bf16[2,2,2,256,128]{4,3,2,1,0:T(8,128)(2,1)S(1)} %pad_maximum_fusion.5.refs_4_), channel_id=1, source_target_pairs={{0,8},{1,9},{2,10},{3,11},{4,12},{5,13},{6,14},{7,15},{8,0},{9,1},... | collective-permute-start | bytes 1572872 | tf_op jit(solution)/shard_map/send_xPa/ppermute | solution.py:71
  46.0 5.0 %collective-permute-done.16 = bf16[1024,128]{1,0:T(8,128)(2,1)S(1)} collective-permute-done((bf16[1024,128]{1,0:T(8,128)(2,1)S(1)}, bf16[1024,128]{1,0:T(8,128)(2,1)S(1)}, u32[]{:S(2)}, u32[]{:S(2)}) %collective-permute-start.16) | collective-permute-done | bytes 262176 | tf_op jit(solution)/shard_map/send_Bzac/ppermute | solution.py:71
  52.2 3.7 %collective-permute-start.17 = (bf16[1024,128]{1,0:T(8,128)(2,1)S(1)}, bf16[1024,128]{1,0:T(8,128)(2,1)S(1)}, u32[]{:S(2)}, u32[]{:S(2)}) collective-permute-start(bf16[1024,128]{1,0:T(8,128)(2,1)S(1)} %get-tuple-element.63), channel_id=1, source_target_pairs={{0,96},{1,97},{2,98},{3,99},{4,100},{5,101},{6,102},{7,103},{8,104... | collective-permute-start | bytes 786440 | tf_op jit(solution)/shard_map/send_Az2c/ppermute | solution.py:71
  55.8 2.5 %collective-permute-start.11 = (bf16[2,2,2,256,128]{4,3,2,1,0:T(8,128)(2,1)S(1)}, bf16[2,2,2,256,128]{4,3,2,1,0:T(8,128)(2,1)S(1)}, u32[]{:S(2)}, u32[]{:S(2)}) collective-permute-start(bf16[2,2,2,256,128]{4,3,2,1,0:T(8,128)(2,1)S(1)} %collective-permute-done.10.refs_6_), channel_id=1, source_target_pairs={{0,8},{1,9},{2,10},{3,11},{4,12},{5,13},{6,14},{7,15},{8,0},{9,1},... | collective-permute-start | bytes 1572872 | tf_op jit(solution)/shard_map/send_xPf/ppermute | solution.py:71
  59.7 6.5 %collective-permute-done.17 = bf16[1024,128]{1,0:T(8,128)(2,1)S(1)} collective-permute-done((bf16[1024,128]{1,0:T(8,128)(2,1)S(1)}, bf16[1024,128]{1,0:T(8,128)(2,1)S(1)}, u32[]{:S(2)}, u32[]{:S(2)}) %collective-permute-start.17) | collective-permute-done | bytes 262176 | tf_op jit(solution)/shard_map/send_Az2c/ppermute | solution.py:71
  66.7 2.5 %collective-permute-start.21 = (bf16[4,2,2,256,128]{4,3,2,1,0:T(8,128)(2,1)S(1)}, bf16[4,2,2,256,128]{4,3,2,1,0:T(8,128)(2,1)S(1)}, u32[]{:S(2)}, u32[]{:S(2)}) collective-permute-start(bf16[4,2,2,256,128]{4,3,2,1,0:T(8,128)(2,1)S(1)} %pad_maximum_fusion.2.refs_4_), channel_id=1, source_target_pairs={{0,8},{1,9},{2,10},{3,11},{4,12},{5,13},{6,14},{7,15},{8,0},{9,1},... | collective-permute-start | bytes 3145736 | tf_op jit(solution)/shard_map/send_xQa/ppermute | solution.py:71
  69.2 1.4 %collective-permute-start.26 = (bf16[1024,128]{1,0:T(8,128)(2,1)S(1)}, bf16[1024,128]{1,0:T(8,128)(2,1)S(1)}, u32[]{:S(2)}, u32[]{:S(2)}) collective-permute-start(bf16[1024,128]{1,0:T(8,128)(2,1)S(1)} %get-tuple-element.73), channel_id=1, source_target_pairs={{0,64},{1,65},{2,66},{3,67},{4,68},{5,69},{6,70},{7,71},{8,72},{9,... | collective-permute-start | bytes 786440 | tf_op jit(solution)/shard_map/send_Bz2/ppermute | solution.py:71
  70.6 8.8 %collective-permute-done.22.refs_6_ = bf16[4,2,2,256,128]{4,3,2,1,0:T(8,128)(2,1)S(1)} collective-permute-done((bf16[4,2,2,256,128]{4,3,2,1,0:T(8,128)(2,1)S(1)}, bf16[4,2,2,256,128]{4,3,2,1,0:T(8,128)(2,1)S(1)}, u32[]{:S(2)}, u32[]{:S(2)}) %collective-permute-start.22) | collective-permute-done | bytes 1048608 | tf_op jit(solution)/shard_map/send_xQb/ppermute | solution.py:71
  80.4 4.2 %collective-permute-start.27 = (bf16[1024,128]{1,0:T(8,128)(2,1)S(1)}, bf16[1024,128]{1,0:T(8,128)(2,1)S(1)}, u32[]{:S(2)}, u32[]{:S(2)}) collective-permute-start(bf16[1024,128]{1,0:T(8,128)(2,1)S(1)} %get-tuple-element.75), channel_id=1, source_target_pairs={{0,96},{1,97},{2,98},{3,99},{4,100},{5,101},{6,102},{7,103},{8,104... | collective-permute-start | bytes 786440 | tf_op jit(solution)/shard_map/send_Bz2c/ppermute | solution.py:71
  84.6 4.5 %collective-permute-done.19.refs_2_ = bf16[4,2,512,128]{3,2,1,0:T(8,128)(2,1)S(1)} collective-permute-done((bf16[4,2,512,128]{3,2,1,0:T(8,128)(2,1)S(1)}, bf16[4,2,512,128]{3,2,1,0:T(8,128)(2,1)S(1)}, u32[]{:S(2)}, u32[]{:S(2)}) %collective-permute-start.19) | collective-permute-done | bytes 1048608 | tf_op jit(solution)/shard_map/send_y2b/ppermute | solution.py:71
  89.1 2.3 %collective-permute-start.18 = (bf16[4,2,512,128]{3,2,1,0:T(8,128)(2,1)S(1)}, bf16[4,2,512,128]{3,2,1,0:T(8,128)(2,1)S(1)}, u32[]{:S(2)}, u32[]{:S(2)}) collective-permute-start(bf16[4,2,512,128]{3,2,1,0:T(8,128)(2,1)S(1)} %pad_maximum_fusion.1.refs_0_), channel_id=1, source_target_pairs={{0,2},{1,3},{2,0},{3,1},{4,6},{5,7},{6,4},{7,5},{8,10},{9,11},{10,... | collective-permute-start | bytes 3145736 | tf_op jit(solution)/shard_map/send_y2a/ppermute | solution.py:71
  93.0 3.7 %correlate.5.refs_8_ = f32[2,512,256]{2,1,0:T(8,128)S(1)} custom-call(s32[10]{0:T(128)S(1)} %stack.128.place, bf16[4,2,512,128]{3,2,1,0:T(8,128)(2,1)S(1)} %pad_maximum_fusion.refs_0_, bf16[4,2,512,128]{3,2,1,0:T(8,128)(2,1)S(1)} %collective-permute-done.5.refs_1_, bf16[4,2,512,128]{3,2,1,0:T(8,128)(2,1)S(1)} %collective-permute-done.6.refs_2_, ...), custom_call_target="tpu_custom_call" | custom-call | flops 2147483648 | bytes 6291456 | tf_op jit(solution)/shard_map/correlate/pallas_call | solution.py:241
  96.7 6.2 %collective-permute-done.29.refs_6_ = bf16[2,2,2,256,128]{4,3,2,1,0:T(8,128)(2,1)S(1)} collective-permute-done((bf16[2,2,2,256,128]{4,3,2,1,0:T(8,128)(2,1)S(1)}, bf16[2,2,2,256,128]{4,3,2,1,0:T(8,128)(2,1)S(1)}, u32[]{:S(2)}, u32[]{:S(2)}) %collective-permute-start.29) | collective-permute-done | bytes 524320 | tf_op jit(solution)/shard_map/send_xSb/ppermute | solution.py:71
  102.9 2.5 %collective-permute-start.30 = (bf16[2,2,2,256,128]{4,3,2,1,0:T(8,128)(2,1)S(1)}, bf16[2,2,2,256,128]{4,3,2,1,0:T(8,128)(2,1)S(1)}, u32[]{:S(2)}, u32[]{:S(2)}) collective-permute-start(bf16[2,2,2,256,128]{4,3,2,1,0:T(8,128)(2,1)S(1)} %collective-permute-done.29.refs_6_), channel_id=1, source_target_pairs={{0,8},{1,9},{2,10},{3,11},{4,12},{5,13},{6,14},{7,15},{8,0},{9,1},... | collective-permute-start | bytes 1572872 | tf_op jit(solution)/shard_map/send_xSf/ppermute | solution.py:71
  105.6 3.7 %correlate.6.refs_8_ = f32[2,512,256]{2,1,0:T(8,128)S(1)} custom-call(s32[10]{0:T(128)S(1)} %stack.128.place, bf16[4,2,512,128]{3,2,1,0:T(8,128)(2,1)S(1)} %pad_maximum_fusion.refs_0_, bf16[4,2,512,128]{3,2,1,0:T(8,128)(2,1)S(1)} %collective-permute-done.5.refs_1_, bf16[4,2,512,128]{3,2,1,0:T(8,128)(2,1)S(1)} %collective-permute-done.6.refs_2_, ...), custom_call_target="tpu_custom_call" | custom-call | flops 2147483648 | bytes 6291456 | tf_op jit(solution)/shard_map/correlate/pallas_call | solution.py:241
  109.3 5.9 %collective-permute-done.20.refs_3_ = bf16[4,2,512,128]{3,2,1,0:T(8,128)(2,1)S(1)} collective-permute-done((bf16[4,2,512,128]{3,2,1,0:T(8,128)(2,1)S(1)}, bf16[4,2,512,128]{3,2,1,0:T(8,128)(2,1)S(1)}, u32[]{:S(2)}, u32[]{:S(2)}) %collective-permute-start.20) | collective-permute-done | bytes 1048608 | tf_op jit(solution)/shard_map/send_y2f/ppermute | solution.py:71
  115.2 2.6 %correlate.7 = bf16[1,512,256]{2,1,0:T(8,128)(2,1)S(1)} custom-call(s32[10]{0:T(128)S(1)} %stack.128.place, bf16[4,2,512,128]{3,2,1,0:T(8,128)(2,1)S(1)} %pad_maximum_fusion.1.refs_0_, bf16[4,2,512,128]{3,2,1,0:T(8,128)(2,1)S(1)} %collective-permute-done.18.refs_1_, bf16[4,2,512,128]{3,2,1,0:T(8,128)(2,1)S(1)} %collective-permute-done.19.refs_2_, ...), custom_call_target="tpu_custom_call" | custom-call | flops 34359738368 | bytes 6291456 | tf_op jit(solution)/shard_map/correlate/pallas_call | solution.py:241
  117.8 2.1 %collective-permute-start.25 = (bf16[1,512,256]{2,1,0:T(8,128)(2,1)S(1)}, bf16[1,512,256]{2,1,0:T(8,128)(2,1)S(1)}, u32[]{:S(2)}, u32[]{:S(2)}) collective-permute-start(bf16[1,512,256]{2,1,0:T(8,128)(2,1)S(1)} %correlate.7), channel_id=1, source_target_pairs={{0,1},{1,0},{2,3},{3,2},{4,5},{5,4},{6,7},{7,6},{8,9},{9,8},{10,11... | collective-permute-start | bytes 786440 | tf_op jit(solution)/shard_map/ppermute | solution.py:71
  119.9 2.6 %correlate.8 = bf16[1,512,256]{2,1,0:T(8,128)(2,1)S(1)} custom-call(s32[10]{0:T(128)S(1)} %stack.128.place, bf16[4,2,512,128]{3,2,1,0:T(8,128)(2,1)S(1)} %pad_maximum_fusion.1.refs_0_, bf16[4,2,512,128]{3,2,1,0:T(8,128)(2,1)S(1)} %collective-permute-done.18.refs_1_, bf16[4,2,512,128]{3,2,1,0:T(8,128)(2,1)S(1)} %collective-permute-done.19.refs_2_, ...), custom_call_target="tpu_custom_call" | custom-call | flops 34359738368 | bytes 6291456 | tf_op jit(solution)/shard_map/correlate/pallas_call | solution.py:241
  122.6 4.7 %correlate.9.whole = f32[2,2,512,256]{3,2,1,0:T(8,128)} custom-call(s32[10]{0:T(128)S(1)} %stack.128.place, bf16[4,2,512,128]{3,2,1,0:T(8,128)(2,1)S(1)} %pad_maximum_fusion.1.refs_0_, bf16[4,2,512,128]{3,2,1,0:T(8,128)(2,1)S(1)} %collective-permute-done.18.refs_1_, bf16[4,2,512,128]{3,2,1,0:T(8,128)(2,1)S(1)} %collective-permute-done.19.refs_2_, ...), custom_call_target="tpu_custom_call" | custom-call | flops 2147483648 | bytes 6291456 | tf_op jit(solution)/shard_map/correlate/pallas_call | solution.py:241
  128.6 1.2 collective-permute-done.24.got
  (69 shorter events, 15.8 us)
Async XLA Ops:
  2.5 17.7 %copy-start.1 = (s32[256]{0:T(256)S(1)}, s32[256]{0:T(256)}, u32[]{:S(2)}) copy-start(s32[256]{0:T(256)} %param.8) | copy-start | bytes 3076
  11.7 20.1 %collective-permute-start = (bf16[1024,128]{1,0:T(8,128)(2,1)S(1)}, bf16[1024,128]{1,0:T(8,128)(2,1)}, u32[]{:S(2)}, u32[]{:S(2)}) collective-permute-start(bf16[1024,128]{1,0:T(8,128)(2,1)S(1)} %get-tuple-element.43), channel_id=1, source_target_pairs={{0,32},{1,33},{2,34},{3,35},{4,36},{5,37},{6,38},{7,39},{8,40},{9,... | collective-permute-start | bytes 786440 | tf_op jit(solution)/shard_map/send_Acc/ppermute | solution.py:71
  13.1 14.7 %collective-permute-start.1 = (bf16[1024,128]{1,0:T(8,128)(2,1)}, bf16[1024,128]{1,0:T(8,128)(2,1)}, u32[]{:S(2)}, u32[]{:S(2)}) collective-permute-start(bf16[1024,128]{1,0:T(8,128)(2,1)} %get-tuple-element.44), channel_id=1, source_target_pairs={{0,1},{1,0},{2,3},{3,2},{4,5},{5,4},{6,7},{7,6},{8,9},{9,8},{10,11... | collective-permute-start | bytes 786440 | tf_op jit(solution)/shard_map/send_Aza/ppermute | solution.py:71
  16.9 10.9 %collective-permute-start.2 = (bf16[1024,128]{1,0:T(8,128)(2,1)}, bf16[1024,128]{1,0:T(8,128)(2,1)}, u32[]{:S(2)}, u32[]{:S(2)}) collective-permute-start(bf16[1024,128]{1,0:T(8,128)(2,1)} %get-tuple-element.45), channel_id=1, source_target_pairs={{0,97},{1,96},{2,99},{3,98},{4,101},{5,100},{6,103},{7,102},{8,105... | collective-permute-start | bytes 786440 | tf_op jit(solution)/shard_map/send_Azbc/ppermute | solution.py:71
  16.9 13.6 %collective-permute-start.3 = (bf16[1024,128]{1,0:T(8,128)(2,1)S(1)}, bf16[1024,128]{1,0:T(8,128)(2,1)}, u32[]{:S(2)}, u32[]{:S(2)}) collective-permute-start(bf16[1024,128]{1,0:T(8,128)(2,1)S(1)} %get-tuple-element.46), channel_id=1, source_target_pairs={{0,65},{1,64},{2,67},{3,66},{4,69},{5,68},{6,71},{7,70},{8,73},{9,... | collective-permute-start | bytes 786440 | tf_op jit(solution)/shard_map/send_Azb/ppermute | solution.py:71
  16.9 13.6 %collective-permute-start.4 = (bf16[1024,128]{1,0:T(8,128)(2,1)S(1)}, bf16[1024,128]{1,0:T(8,128)(2,1)}, u32[]{:S(2)}, u32[]{:S(2)}) collective-permute-start(bf16[1024,128]{1,0:T(8,128)(2,1)S(1)} %get-tuple-element.47), channel_id=1, source_target_pairs={{0,33},{1,32},{2,35},{3,34},{4,37},{5,36},{6,39},{7,38},{8,41},{9,... | collective-permute-start | bytes 786440 | tf_op jit(solution)/shard_map/send_Azac/ppermute | solution.py:71
  27.8 9.6 %collective-permute-start.8 = (bf16[1024,128]{1,0:T(8,128)(2,1)S(1)}, bf16[1024,128]{1,0:T(8,128)(2,1)S(1)}, u32[]{:S(2)}, u32[]{:S(2)}) collective-permute-start(bf16[1024,128]{1,0:T(8,128)(2,1)S(1)} %get-tuple-element.51), channel_id=1, source_target_pairs={{0,32},{1,33},{2,34},{3,35},{4,36},{5,37},{6,38},{7,39},{8,40},{9,... | collective-permute-start | bytes 786440 | tf_op jit(solution)/shard_map/send_Bcc/ppermute | solution.py:71
  27.9 8.3 %collective-permute-start.12 = (bf16[1024,128]{1,0:T(8,128)(2,1)}, bf16[1024,128]{1,0:T(8,128)(2,1)S(1)}, u32[]{:S(2)}, u32[]{:S(2)}) collective-permute-start(bf16[1024,128]{1,0:T(8,128)(2,1)} %copy-done), channel_id=1, source_target_pairs={{0,1},{1,0},{2,3},{3,2},{4,5},{5,4},{6,7},{7,6},{8,9},{9,8},{10,11... | collective-permute-start | bytes 786440 | tf_op jit(solution)/shard_map/send_Bza/ppermute | solution.py:71
  32.9 25.6 %collective-permute-start.6 = (bf16[4,2,512,128]{3,2,1,0:T(8,128)(2,1)S(1)}, bf16[4,2,512,128]{3,2,1,0:T(8,128)(2,1)S(1)}, u32[]{:S(2)}, u32[]{:S(2)}) collective-permute-start(bf16[4,2,512,128]{3,2,1,0:T(8,128)(2,1)S(1)} %pad_maximum_fusion.refs_0_), channel_id=1, source_target_pairs={{0,6},{1,7},{2,4},{3,5},{4,2},{5,3},{6,0},{7,1},{8,14},{9,15},{10,... | collective-permute-start | bytes 3145736 | tf_op jit(solution)/shard_map/send_y1b/ppermute | solution.py:71
  34.2 8.2 %collective-permute-start.15 = (bf16[1024,128]{1,0:T(8,128)(2,1)S(1)}, bf16[1024,128]{1,0:T(8,128)(2,1)S(1)}, u32[]{:S(2)}, u32[]{:S(2)}) collective-permute-start(bf16[1024,128]{1,0:T(8,128)(2,1)S(1)} %get-tuple-element.61), channel_id=1, source_target_pairs={{0,97},{1,96},{2,99},{3,98},{4,101},{5,100},{6,103},{7,102},{8,105... | collective-permute-start | bytes 786440 | tf_op jit(solution)/shard_map/send_Bzbc/ppermute | solution.py:71
  35.4 30.9 %collective-permute-start.5 = (bf16[4,2,512,128]{3,2,1,0:T(8,128)(2,1)S(1)}, bf16[4,2,512,128]{3,2,1,0:T(8,128)(2,1)S(1)}, u32[]{:S(2)}, u32[]{:S(2)}) collective-permute-start(bf16[4,2,512,128]{3,2,1,0:T(8,128)(2,1)S(1)} %pad_maximum_fusion.refs_0_), channel_id=1, source_target_pairs={{0,2},{1,3},{2,0},{3,1},{4,6},{5,7},{6,4},{7,5},{8,10},{9,11},{10,... | collective-permute-start | bytes 3145736 | tf_op jit(solution)/shard_map/send_y1a/ppermute | solution.py:71
  36.2 8.8 %collective-permute-start.13 = (bf16[1024,128]{1,0:T(8,128)(2,1)S(1)}, bf16[1024,128]{1,0:T(8,128)(2,1)S(1)}, u32[]{:S(2)}, u32[]{:S(2)}) collective-permute-start(bf16[1024,128]{1,0:T(8,128)(2,1)S(1)} %get-tuple-element.57), channel_id=1, source_target_pairs={{0,65},{1,64},{2,67},{3,66},{4,69},{5,68},{6,71},{7,70},{8,73},{9,... | collective-permute-start | bytes 786440 | tf_op jit(solution)/shard_map/send_Bzb/ppermute | solution.py:71
  37.4 14.7 %collective-permute-start.10 = (bf16[2,2,2,256,128]{4,3,2,1,0:T(8,128)(2,1)S(1)}, bf16[2,2,2,256,128]{4,3,2,1,0:T(8,128)(2,1)S(1)}, u32[]{:S(2)}, u32[]{:S(2)}) collective-permute-start(bf16[2,2,2,256,128]{4,3,2,1,0:T(8,128)(2,1)S(1)} %pad_maximum_fusion.5.refs_4_), channel_id=1, source_target_pairs={{0,24},{1,25},{2,26},{3,27},{4,28},{5,29},{6,30},{7,31},{8,16},{9,... | collective-permute-start | bytes 1572872 | tf_op jit(solution)/shard_map/send_xPb/ppermute | solution.py:71
  42.5 13.4 %collective-permute-start.9 = (bf16[2,2,2,256,128]{4,3,2,1,0:T(8,128)(2,1)S(1)}, bf16[2,2,2,256,128]{4,3,2,1,0:T(8,128)(2,1)S(1)}, u32[]{:S(2)}, u32[]{:S(2)}) collective-permute-start(bf16[2,2,2,256,128]{4,3,2,1,0:T(8,128)(2,1)S(1)} %pad_maximum_fusion.5.refs_4_), channel_id=1, source_target_pairs={{0,8},{1,9},{2,10},{3,11},{4,12},{5,13},{6,14},{7,15},{8,0},{9,1},... | collective-permute-start | bytes 1572872 | tf_op jit(solution)/shard_map/send_xPa/ppermute | solution.py:71
  45.0 6.1 %collective-permute-start.16 = (bf16[1024,128]{1,0:T(8,128)(2,1)S(1)}, bf16[1024,128]{1,0:T(8,128)(2,1)S(1)}, u32[]{:S(2)}, u32[]{:S(2)}) collective-permute-start(bf16[1024,128]{1,0:T(8,128)(2,1)S(1)} %get-tuple-element.62), channel_id=1, source_target_pairs={{0,33},{1,32},{2,35},{3,34},{4,37},{5,36},{6,39},{7,38},{8,41},{9,... | collective-permute-start | bytes 786440 | tf_op jit(solution)/shard_map/send_Bzac/ppermute | solution.py:71
  51.1 7.7 %collective-permute-start.14 = (bf16[1024,128]{1,0:T(8,128)(2,1)S(1)}, bf16[1024,128]{1,0:T(8,128)(2,1)S(1)}, u32[]{:S(2)}, u32[]{:S(2)}) collective-permute-start(bf16[1024,128]{1,0:T(8,128)(2,1)S(1)} %get-tuple-element.58), channel_id=1, source_target_pairs={{0,64},{1,65},{2,66},{3,67},{4,68},{5,69},{6,70},{7,71},{8,72},{9,... | collective-permute-start | bytes 786440 | tf_op jit(solution)/shard_map/send_Az2/ppermute | solution.py:71
  52.2 14.0 %collective-permute-start.17 = (bf16[1024,128]{1,0:T(8,128)(2,1)S(1)}, bf16[1024,128]{1,0:T(8,128)(2,1)S(1)}, u32[]{:S(2)}, u32[]{:S(2)}) collective-permute-start(bf16[1024,128]{1,0:T(8,128)(2,1)S(1)} %get-tuple-element.63), channel_id=1, source_target_pairs={{0,96},{1,97},{2,98},{3,99},{4,100},{5,101},{6,102},{7,103},{8,104... | collective-permute-start | bytes 786440 | tf_op jit(solution)/shard_map/send_Az2c/ppermute | solution.py:71
  55.8 10.9 %collective-permute-start.11 = (bf16[2,2,2,256,128]{4,3,2,1,0:T(8,128)(2,1)S(1)}, bf16[2,2,2,256,128]{4,3,2,1,0:T(8,128)(2,1)S(1)}, u32[]{:S(2)}, u32[]{:S(2)}) collective-permute-start(bf16[2,2,2,256,128]{4,3,2,1,0:T(8,128)(2,1)S(1)} %collective-permute-done.10.refs_6_), channel_id=1, source_target_pairs={{0,8},{1,9},{2,10},{3,11},{4,12},{5,13},{6,14},{7,15},{8,0},{9,1},... | collective-permute-start | bytes 1572872 | tf_op jit(solution)/shard_map/send_xPf/ppermute | solution.py:71
  58.5 21.0 %collective-permute-start.22 = (bf16[4,2,2,256,128]{4,3,2,1,0:T(8,128)(2,1)S(1)}, bf16[4,2,2,256,128]{4,3,2,1,0:T(8,128)(2,1)S(1)}, u32[]{:S(2)}, u32[]{:S(2)}) collective-permute-start(bf16[4,2,2,256,128]{4,3,2,1,0:T(8,128)(2,1)S(1)} %pad_maximum_fusion.2.refs_4_), channel_id=1, source_target_pairs={{0,24},{1,25},{2,26},{3,27},{4,28},{5,29},{6,30},{7,31},{8,16},{9,... | collective-permute-start | bytes 3145736 | tf_op jit(solution)/shard_map/send_xQb/ppermute | solution.py:71
  58.7 21.6 %collective-permute-start.7 = (bf16[4,2,512,128]{3,2,1,0:T(8,128)(2,1)S(1)}, bf16[4,2,512,128]{3,2,1,0:T(8,128)(2,1)S(1)}, u32[]{:S(2)}, u32[]{:S(2)}) collective-permute-start(bf16[4,2,512,128]{3,2,1,0:T(8,128)(2,1)S(1)} %collective-permute-done.6.refs_2_), channel_id=1, source_target_pairs={{0,2},{1,3},{2,0},{3,1},{4,6},{5,7},{6,4},{7,5},{8,10},{9,11},{10,... | collective-permute-start | bytes 3145736 | tf_op jit(solution)/shard_map/send_y1f/ppermute | solution.py:71
  66.3 22.8 %collective-permute-start.19 = (bf16[4,2,512,128]{3,2,1,0:T(8,128)(2,1)S(1)}, bf16[4,2,512,128]{3,2,1,0:T(8,128)(2,1)S(1)}, u32[]{:S(2)}, u32[]{:S(2)}) collective-permute-start(bf16[4,2,512,128]{3,2,1,0:T(8,128)(2,1)S(1)} %pad_maximum_fusion.1.refs_0_), channel_id=1, source_target_pairs={{0,6},{1,7},{2,4},{3,5},{4,2},{5,3},{6,0},{7,1},{8,14},{9,15},{10,... | collective-permute-start | bytes 3145736 | tf_op jit(solution)/shard_map/send_y2b/ppermute | solution.py:71
  66.7 25.1 %collective-permute-start.21 = (bf16[4,2,2,256,128]{4,3,2,1,0:T(8,128)(2,1)S(1)}, bf16[4,2,2,256,128]{4,3,2,1,0:T(8,128)(2,1)S(1)}, u32[]{:S(2)}, u32[]{:S(2)}) collective-permute-start(bf16[4,2,2,256,128]{4,3,2,1,0:T(8,128)(2,1)S(1)} %pad_maximum_fusion.2.refs_4_), channel_id=1, source_target_pairs={{0,8},{1,9},{2,10},{3,11},{4,12},{5,13},{6,14},{7,15},{8,0},{9,1},... | collective-permute-start | bytes 3145736 | tf_op jit(solution)/shard_map/send_xQa/ppermute | solution.py:71
  69.2 22.1 %collective-permute-start.26 = (bf16[1024,128]{1,0:T(8,128)(2,1)S(1)}, bf16[1024,128]{1,0:T(8,128)(2,1)S(1)}, u32[]{:S(2)}, u32[]{:S(2)}) collective-permute-start(bf16[1024,128]{1,0:T(8,128)(2,1)S(1)} %get-tuple-element.73), channel_id=1, source_target_pairs={{0,64},{1,65},{2,66},{3,67},{4,68},{5,69},{6,70},{7,71},{8,72},{9,... | collective-permute-start | bytes 786440 | tf_op jit(solution)/shard_map/send_Bz2/ppermute | solution.py:71
  79.4 26.0 %collective-permute-start.23 = (bf16[4,2,2,256,128]{4,3,2,1,0:T(8,128)(2,1)S(1)}, bf16[4,2,2,256,128]{4,3,2,1,0:T(8,128)(2,1)S(1)}, u32[]{:S(2)}, u32[]{:S(2)}) collective-permute-start(bf16[4,2,2,256,128]{4,3,2,1,0:T(8,128)(2,1)S(1)} %collective-permute-done.22.refs_6_), channel_id=1, source_target_pairs={{0,8},{1,9},{2,10},{3,11},{4,12},{5,13},{6,14},{7,15},{8,0},{9,1},... | collective-permute-start | bytes 3145736 | tf_op jit(solution)/shard_map/send_xQf/ppermute | solution.py:71
  80.4 11.4 %collective-permute-start.27 = (bf16[1024,128]{1,0:T(8,128)(2,1)S(1)}, bf16[1024,128]{1,0:T(8,128)(2,1)S(1)}, u32[]{:S(2)}, u32[]{:S(2)}) collective-permute-start(bf16[1024,128]{1,0:T(8,128)(2,1)S(1)} %get-tuple-element.75), channel_id=1, source_target_pairs={{0,96},{1,97},{2,98},{3,99},{4,100},{5,101},{6,102},{7,103},{8,104... | collective-permute-start | bytes 786440 | tf_op jit(solution)/shard_map/send_Bz2c/ppermute | solution.py:71
  89.1 20.2 %collective-permute-start.18 = (bf16[4,2,512,128]{3,2,1,0:T(8,128)(2,1)S(1)}, bf16[4,2,512,128]{3,2,1,0:T(8,128)(2,1)S(1)}, u32[]{:S(2)}, u32[]{:S(2)}) collective-permute-start(bf16[4,2,512,128]{3,2,1,0:T(8,128)(2,1)S(1)} %pad_maximum_fusion.1.refs_0_), channel_id=1, source_target_pairs={{0,2},{1,3},{2,0},{3,1},{4,6},{5,7},{6,4},{7,5},{8,10},{9,11},{10,... | collective-permute-start | bytes 3145736 | tf_op jit(solution)/shard_map/send_y2a/ppermute | solution.py:71
  91.3 23.8 %collective-permute-start.20 = (bf16[4,2,512,128]{3,2,1,0:T(8,128)(2,1)S(1)}, bf16[4,2,512,128]{3,2,1,0:T(8,128)(2,1)S(1)}, u32[]{:S(2)}, u32[]{:S(2)}) collective-permute-start(bf16[4,2,512,128]{3,2,1,0:T(8,128)(2,1)S(1)} %collective-permute-done.19.refs_2_), channel_id=1, source_target_pairs={{0,2},{1,3},{2,0},{3,1},{4,6},{5,7},{6,4},{7,5},{8,10},{9,11},{10,... | collective-permute-start | bytes 3145736 | tf_op jit(solution)/shard_map/send_y2f/ppermute | solution.py:71
  91.8 11.1 %collective-permute-start.29 = (bf16[2,2,2,256,128]{4,3,2,1,0:T(8,128)(2,1)S(1)}, bf16[2,2,2,256,128]{4,3,2,1,0:T(8,128)(2,1)S(1)}, u32[]{:S(2)}, u32[]{:S(2)}) collective-permute-start(bf16[2,2,2,256,128]{4,3,2,1,0:T(8,128)(2,1)S(1)} %pad_maximum_fusion.6.refs_4_), channel_id=1, source_target_pairs={{0,24},{1,25},{2,26},{3,27},{4,28},{5,29},{6,30},{7,31},{8,16},{9,... | collective-permute-start | bytes 1572872 | tf_op jit(solution)/shard_map/send_xSb/ppermute | solution.py:71
  102.9 19.7 %collective-permute-start.30 = (bf16[2,2,2,256,128]{4,3,2,1,0:T(8,128)(2,1)S(1)}, bf16[2,2,2,256,128]{4,3,2,1,0:T(8,128)(2,1)S(1)}, u32[]{:S(2)}, u32[]{:S(2)}) collective-permute-start(bf16[2,2,2,256,128]{4,3,2,1,0:T(8,128)(2,1)S(1)} %collective-permute-done.29.refs_6_), channel_id=1, source_target_pairs={{0,8},{1,9},{2,10},{3,11},{4,12},{5,13},{6,14},{7,15},{8,0},{9,1},... | collective-permute-start | bytes 1572872 | tf_op jit(solution)/shard_map/send_xSf/ppermute | solution.py:71
  105.4 17.2 %collective-permute-start.28 = (bf16[2,2,2,256,128]{4,3,2,1,0:T(8,128)(2,1)S(1)}, bf16[2,2,2,256,128]{4,3,2,1,0:T(8,128)(2,1)S(1)}, u32[]{:S(2)}, u32[]{:S(2)}) collective-permute-start(bf16[2,2,2,256,128]{4,3,2,1,0:T(8,128)(2,1)S(1)} %pad_maximum_fusion.6.refs_4_), channel_id=1, source_target_pairs={{0,8},{1,9},{2,10},{3,11},{4,12},{5,13},{6,14},{7,15},{8,0},{9,1},... | collective-permute-start | bytes 1572872 | tf_op jit(solution)/shard_map/send_xSa/ppermute | solution.py:71
  117.8 9.5 %collective-permute-start.25 = (bf16[1,512,256]{2,1,0:T(8,128)(2,1)S(1)}, bf16[1,512,256]{2,1,0:T(8,128)(2,1)S(1)}, u32[]{:S(2)}, u32[]{:S(2)}) collective-permute-start(bf16[1,512,256]{2,1,0:T(8,128)(2,1)S(1)} %correlate.7), channel_id=1, source_target_pairs={{0,1},{1,0},{2,3},{3,2},{4,5},{5,4},{6,7},{7,6},{8,9},{9,8},{10,11... | collective-permute-start | bytes 786440 | tf_op jit(solution)/shard_map/ppermute | solution.py:71
  122.5 7.2 %collective-permute-start.24 = (bf16[1,512,256]{2,1,0:T(8,128)(2,1)S(1)}, bf16[1,512,256]{2,1,0:T(8,128)(2,1)S(1)}, u32[]{:S(2)}, u32[]{:S(2)}) collective-permute-start(bf16[1,512,256]{2,1,0:T(8,128)(2,1)S(1)} %correlate.8), channel_id=1, source_target_pairs={{0,1},{1,0},{2,3},{3,2},{4,5},{5,4},{6,7},{7,6},{8,9},{9,8},{10,11... | collective-permute-start | bytes 786440 | tf_op jit(solution)/shard_map/ppermute | solution.py:71
  (1 other events, 0.7 us)

commit v6 on v5

--- a/solution.py
+++ b/solution.py
@@ -166,7 +166,7 @@
             ],
         ),
         out_shape=[jax.ShapeDtypeStruct((rows, 128), BF16)] * 8,
-        compiler_params=pltpu.CompilerParams(vmem_limit_bytes=48 << 20),
+        compiler_params=pltpu.CompilerParams(vmem_limit_bytes=(48 if width == 128 else 28) << 20),
         cost_estimate=pl.CostEstimate(flops=8 << 30, bytes_accessed=10 << 20, transcendentals=0),
         name="spectra",
     )(place, table, lags, traces)

time: 131 us -> 132 us (level)
  local copies, waits for them, and re-layouts: 2.24 us -> 5.62 us
  waiting for transfers between devices: 42.4 us -> 40.1 us
  Pallas kernels: 35.3 us -> 33.9 us
    unnamed x4 -> x6, local copies, waits for them, and re-layouts: 0.7 us -> 4.07 us
    ppermute x31, waiting for transfers between devices: 42.4 us -> 40.1 us  [send(): return lax.ppermute(value, AXES, pairs)]
    pallas_call x2, Pallas kernels: 15.7 us -> 14 us  [spectra(): pl.pallas_call(functools.partial(spectra_kernel, width // 128), grid_spec...]
  transfers between devices with their start and end apart: 31 -> 31, of which waited for: 10 -> 12; matrix products, arithmetic and copies ran while one was open for 2% -> 2% of each run, Pallas kernels for 19% -> 18%
where the time goes in v6:
time: 132 us
  starting transfers between devices  48 us (36%)
  waiting for transfers between devices  40.1 us (30%)
  Pallas kernels  33.9 us (26%)
  local copies, waits for them, and re-layouts  5.62 us (4%)
  other arithmetic  3.84 us (3%)
    ppermute x31, starting transfers between devices, send(): return lax.ppermute(value, AXES, pairs)  48 us
    ppermute x31, waiting for transfers between devices, send(): return lax.ppermute(value, AXES, pairs)  40.1 us
    pallas_call x5, Pallas kernels, correlate(): pl.pallas_call(functools.partial(correlate_kernel, pairs, picks, parts, p...  17.5 us
    pallas_call x2, Pallas kernels, spectra(): pl.pallas_call(functools.partial(spectra_kernel, width // 128), grid_spec...  14 us
    unnamed x6, local copies, waits for them, and re-layouts  4.07 us
  transfers between devices with their start and end apart: 31, of which 12 were waited for; matrix products, arithmetic and copies ran while one was open for 2% of the time, Pallas kernels for 18%

profile of v6, /device:TPU:1, one launch (start us, length us, event | category | flops | bytes accessed | tf_op | source)
XLA Modules:
  0.0 131.9 jit_solution(1889042330251406860)
XLA Ops:
  2.5 9.2 %spectra.2 = (bf16[1024,128]{1,0:T(8,128)(2,1)S(1)}, bf16[1024,128]{1,0:T(8,128)(2,1)S(1)}, bf16[1024,128]{1,0:T(8,128)(2,1)}, bf16[1024,128]{1,0:T(8,128)(2,1)}...) custom-call(s32[10]{0:T(128)S(1)} %stack.128.place, ...), custom_call_target="tpu_custom_call" | custom-call | flops 8589934592 | bytes 10485760 | tf_op jit(solution)/shard_map/spectra/pallas_call | solution.py:151
  11.7 1.4 %collective-permute-start = (bf16[1024,128]{1,0:T(8,128)(2,1)S(1)}, bf16[1024,128]{1,0:T(8,128)(2,1)}, u32[]{:S(2)}, u32[]{:S(2)}) collective-permute-start(bf16[1024,128]{1,0:T(8,128)(2,1)S(1)} %get-tuple-element.43), channel_id=1, source_target_pairs={{0,32},{1,33},{2,34},{3,35},{4,36},{5,37},{6,38},{7,39},{8,40},{9,... | collective-permute-start | bytes 786440 | tf_op jit(solution)/shard_map/send_Acc/ppermute | solution.py:71
  13.1 3.8 %collective-permute-start.1 = (bf16[1024,128]{1,0:T(8,128)(2,1)}, bf16[1024,128]{1,0:T(8,128)(2,1)}, u32[]{:S(2)}, u32[]{:S(2)}) collective-permute-start(bf16[1024,128]{1,0:T(8,128)(2,1)} %get-tuple-element.44), channel_id=1, source_target_pairs={{0,1},{1,0},{2,3},{3,2},{4,5},{5,4},{6,7},{7,6},{8,9},{9,8},{10,11... | collective-permute-start | bytes 786440 | tf_op jit(solution)/shard_map/send_Aza/ppermute | solution.py:71
  16.9 3.3 %collective-permute-start.4 = (bf16[1024,128]{1,0:T(8,128)(2,1)S(1)}, bf16[1024,128]{1,0:T(8,128)(2,1)}, u32[]{:S(2)}, u32[]{:S(2)}) collective-permute-start(bf16[1024,128]{1,0:T(8,128)(2,1)S(1)} %get-tuple-element.47), channel_id=1, source_target_pairs={{0,33},{1,32},{2,35},{3,34},{4,37},{5,36},{6,39},{7,38},{8,41},{9,... | collective-permute-start | bytes 786440 | tf_op jit(solution)/shard_map/send_Azac/ppermute | solution.py:71
  20.6 3.4 %copy-done = bf16[64,256,256]{2,1,0:T(8,128)(2,1)S(1)} copy-done((bf16[64,256,256]{2,1,0:T(8,128)(2,1)S(1)}, bf16[64,256,256]{2,1,0:T(8,128)(2,1)}, u32[]{:S(2)}) %copy-start) | copy-done | bytes 8388632
  23.9 4.9 %spectra.3 = (bf16[1024,128]{1,0:T(8,128)(2,1)S(1)}, bf16[1024,128]{1,0:T(8,128)(2,1)S(1)}, bf16[1024,128]{1,0:T(8,128)(2,1)S(1)}, bf16[1024,128]{1,0:T(8,128)(2...) custom-call(s32[10]{0:T(128)S(1)} %stack.128.place, ...), custom_call_target="tpu_custom_call" | custom-call | flops 8589934592 | bytes 10485760 | tf_op jit(solution)/shard_map/spectra/pallas_call | solution.py:151
  29.6 2.6 %collective-permute-start.12 = (bf16[1024,128]{1,0:T(8,128)(2,1)}, bf16[1024,128]{1,0:T(8,128)(2,1)S(1)}, u32[]{:S(2)}, u32[]{:S(2)}) collective-permute-start(bf16[1024,128]{1,0:T(8,128)(2,1)} %copy-done.1), channel_id=1, source_target_pairs={{0,1},{1,0},{2,3},{3,2},{4,5},{5,4},{6,7},{7,6},{8,9},{9,8},{10,11... | collective-permute-start | bytes 786440 | tf_op jit(solution)/shard_map/send_Bza/ppermute | solution.py:71
  34.6 1.4 %collective-permute-start.6 = (bf16[4,2,512,128]{3,2,1,0:T(8,128)(2,1)S(1)}, bf16[4,2,512,128]{3,2,1,0:T(8,128)(2,1)S(1)}, u32[]{:S(2)}, u32[]{:S(2)}) collective-permute-start(bf16[4,2,512,128]{3,2,1,0:T(8,128)(2,1)S(1)} %pad_maximum_fusion.refs_0_), channel_id=1, source_target_pairs={{0,6},{1,7},{2,4},{3,5},{4,2},{5,3},{6,0},{7,1},{8,14},{9,15},{10,... | collective-permute-start | bytes 3145736 | tf_op jit(solution)/shard_map/send_y1b/ppermute | solution.py:71
  39.2 4.0 %collective-permute-done.15 = bf16[1024,128]{1,0:T(8,128)(2,1)S(1)} collective-permute-done((bf16[1024,128]{1,0:T(8,128)(2,1)S(1)}, bf16[1024,128]{1,0:T(8,128)(2,1)S(1)}, u32[]{:S(2)}, u32[]{:S(2)}) %collective-permute-start.15) | collective-permute-done | bytes 262176 | tf_op jit(solution)/shard_map/send_Bzbc/ppermute | solution.py:71
  43.3 2.5 %collective-permute-start.9 = (bf16[2,2,2,256,128]{4,3,2,1,0:T(8,128)(2,1)S(1)}, bf16[2,2,2,256,128]{4,3,2,1,0:T(8,128)(2,1)S(1)}, u32[]{:S(2)}, u32[]{:S(2)}) collective-permute-start(bf16[2,2,2,256,128]{4,3,2,1,0:T(8,128)(2,1)S(1)} %pad_maximum_fusion.5.refs_4_), channel_id=1, source_target_pairs={{0,8},{1,9},{2,10},{3,11},{4,12},{5,13},{6,14},{7,15},{8,0},{9,1},... | collective-permute-start | bytes 1572872 | tf_op jit(solution)/shard_map/send_xPa/ppermute | solution.py:71
  47.0 4.9 %collective-permute-done.16 = bf16[1024,128]{1,0:T(8,128)(2,1)S(1)} collective-permute-done((bf16[1024,128]{1,0:T(8,128)(2,1)S(1)}, bf16[1024,128]{1,0:T(8,128)(2,1)S(1)}, u32[]{:S(2)}, u32[]{:S(2)}) %collective-permute-start.16) | collective-permute-done | bytes 262176 | tf_op jit(solution)/shard_map/send_Bzac/ppermute | solution.py:71
  51.9 2.0 %collective-permute-start.14 = (bf16[1024,128]{1,0:T(8,128)(2,1)S(1)}, bf16[1024,128]{1,0:T(8,128)(2,1)S(1)}, u32[]{:S(2)}, u32[]{:S(2)}) collective-permute-start(bf16[1024,128]{1,0:T(8,128)(2,1)S(1)} %get-tuple-element.58), channel_id=1, source_target_pairs={{0,64},{1,65},{2,66},{3,67},{4,68},{5,69},{6,70},{7,71},{8,72},{9,... | collective-permute-start | bytes 786440 | tf_op jit(solution)/shard_map/send_Az2/ppermute | solution.py:71
  53.9 2.7 %collective-permute-start.17 = (bf16[1024,128]{1,0:T(8,128)(2,1)S(1)}, bf16[1024,128]{1,0:T(8,128)(2,1)S(1)}, u32[]{:S(2)}, u32[]{:S(2)}) collective-permute-start(bf16[1024,128]{1,0:T(8,128)(2,1)S(1)} %get-tuple-element.63), channel_id=1, source_target_pairs={{0,96},{1,97},{2,98},{3,99},{4,100},{5,101},{6,102},{7,103},{8,104... | collective-permute-start | bytes 786440 | tf_op jit(solution)/shard_map/send_Az2c/ppermute | solution.py:71
  56.6 2.5 %collective-permute-start.11 = (bf16[2,2,2,256,128]{4,3,2,1,0:T(8,128)(2,1)S(1)}, bf16[2,2,2,256,128]{4,3,2,1,0:T(8,128)(2,1)S(1)}, u32[]{:S(2)}, u32[]{:S(2)}) collective-permute-start(bf16[2,2,2,256,128]{4,3,2,1,0:T(8,128)(2,1)S(1)} %collective-permute-done.10.refs_6_), channel_id=1, source_target_pairs={{0,8},{1,9},{2,10},{3,11},{4,12},{5,13},{6,14},{7,15},{8,0},{9,1},... | collective-permute-start | bytes 1572872 | tf_op jit(solution)/shard_map/send_xPf/ppermute | solution.py:71
  60.0 2.4 %collective-permute-start.7 = (bf16[4,2,512,128]{3,2,1,0:T(8,128)(2,1)S(1)}, bf16[4,2,512,128]{3,2,1,0:T(8,128)(2,1)S(1)}, u32[]{:S(2)}, u32[]{:S(2)}) collective-permute-start(bf16[4,2,512,128]{3,2,1,0:T(8,128)(2,1)S(1)} %collective-permute-done.6.refs_2_), channel_id=1, source_target_pairs={{0,2},{1,3},{2,0},{3,1},{4,6},{5,7},{6,4},{7,5},{8,10},{9,11},{10,... | collective-permute-start | bytes 3145736 | tf_op jit(solution)/shard_map/send_y1f/ppermute | solution.py:71
  62.4 4.6 %collective-permute-done.17 = bf16[1024,128]{1,0:T(8,128)(2,1)S(1)} collective-permute-done((bf16[1024,128]{1,0:T(8,128)(2,1)S(1)}, bf16[1024,128]{1,0:T(8,128)(2,1)S(1)}, u32[]{:S(2)}, u32[]{:S(2)}) %collective-permute-start.17) | collective-permute-done | bytes 262176 | tf_op jit(solution)/shard_map/send_Az2c/ppermute | solution.py:71
  67.2 2.9 %collective-permute-done.11.refs_7_ = bf16[2,2,2,256,128]{4,3,2,1,0:T(8,128)(2,1)S(1)} collective-permute-done((bf16[2,2,2,256,128]{4,3,2,1,0:T(8,128)(2,1)S(1)}, bf16[2,2,2,256,128]{4,3,2,1,0:T(8,128)(2,1)S(1)}, u32[]{:S(2)}, u32[]{:S(2)}) %collective-permute-start.11) | collective-permute-done | bytes 524320 | tf_op jit(solution)/shard_map/send_xPf/ppermute | solution.py:71
  70.1 2.5 %collective-permute-start.21 = (bf16[4,2,2,256,128]{4,3,2,1,0:T(8,128)(2,1)S(1)}, bf16[4,2,2,256,128]{4,3,2,1,0:T(8,128)(2,1)S(1)}, u32[]{:S(2)}, u32[]{:S(2)}) collective-permute-start(bf16[4,2,2,256,128]{4,3,2,1,0:T(8,128)(2,1)S(1)} %pad_maximum_fusion.2.refs_4_), channel_id=1, source_target_pairs={{0,8},{1,9},{2,10},{3,11},{4,12},{5,13},{6,14},{7,15},{8,0},{9,1},... | collective-permute-start | bytes 3145736 | tf_op jit(solution)/shard_map/send_xQa/ppermute | solution.py:71
  72.6 6.5 %collective-permute-done.22.refs_6_ = bf16[4,2,2,256,128]{4,3,2,1,0:T(8,128)(2,1)S(1)} collective-permute-done((bf16[4,2,2,256,128]{4,3,2,1,0:T(8,128)(2,1)S(1)}, bf16[4,2,2,256,128]{4,3,2,1,0:T(8,128)(2,1)S(1)}, u32[]{:S(2)}, u32[]{:S(2)}) %collective-permute-start.22) | collective-permute-done | bytes 1048608 | tf_op jit(solution)/shard_map/send_xQb/ppermute | solution.py:71
  80.1 8.0 %collective-permute-start.27 = (bf16[1024,128]{1,0:T(8,128)(2,1)S(1)}, bf16[1024,128]{1,0:T(8,128)(2,1)S(1)}, u32[]{:S(2)}, u32[]{:S(2)}) collective-permute-start(bf16[1024,128]{1,0:T(8,128)(2,1)S(1)} %get-tuple-element.75), channel_id=1, source_target_pairs={{0,96},{1,97},{2,98},{3,99},{4,100},{5,101},{6,102},{7,103},{8,104... | collective-permute-start | bytes 786440 | tf_op jit(solution)/shard_map/send_Bz2c/ppermute | solution.py:71
  88.1 1.8 %collective-permute-done.19.refs_2_ = bf16[4,2,512,128]{3,2,1,0:T(8,128)(2,1)S(1)} collective-permute-done((bf16[4,2,512,128]{3,2,1,0:T(8,128)(2,1)S(1)}, bf16[4,2,512,128]{3,2,1,0:T(8,128)(2,1)S(1)}, u32[]{:S(2)}, u32[]{:S(2)}) %collective-permute-start.19) | collective-permute-done | bytes 1048608 | tf_op jit(solution)/shard_map/send_y2b/ppermute | solution.py:71
  89.9 3.1 %collective-permute-start.18 = (bf16[4,2,512,128]{3,2,1,0:T(8,128)(2,1)S(1)}, bf16[4,2,512,128]{3,2,1,0:T(8,128)(2,1)S(1)}, u32[]{:S(2)}, u32[]{:S(2)}) collective-permute-start(bf16[4,2,512,128]{3,2,1,0:T(8,128)(2,1)S(1)} %pad_maximum_fusion.1.refs_0_), channel_id=1, source_target_pairs={{0,2},{1,3},{2,0},{3,1},{4,6},{5,7},{6,4},{7,5},{8,10},{9,11},{10,... | collective-permute-start | bytes 3145736 | tf_op jit(solution)/shard_map/send_y2a/ppermute | solution.py:71
  94.2 3.8 %correlate.5.refs_8_ = f32[2,512,256]{2,1,0:T(8,128)S(1)} custom-call(s32[10]{0:T(128)S(1)} %stack.128.place, bf16[4,2,512,128]{3,2,1,0:T(8,128)(2,1)S(1)} %pad_maximum_fusion.refs_0_, bf16[4,2,512,128]{3,2,1,0:T(8,128)(2,1)S(1)} %collective-permute-done.5.refs_1_, bf16[4,2,512,128]{3,2,1,0:T(8,128)(2,1)S(1)} %collective-permute-done.6.refs_2_, ...), custom_call_target="tpu_custom_call" | custom-call | flops 2147483648 | bytes 6291456 | tf_op jit(solution)/shard_map/correlate/pallas_call | solution.py:241
  98.0 5.4 %collective-permute-done.29.refs_6_ = bf16[2,2,2,256,128]{4,3,2,1,0:T(8,128)(2,1)S(1)} collective-permute-done((bf16[2,2,2,256,128]{4,3,2,1,0:T(8,128)(2,1)S(1)}, bf16[2,2,2,256,128]{4,3,2,1,0:T(8,128)(2,1)S(1)}, u32[]{:S(2)}, u32[]{:S(2)}) %collective-permute-start.29) | collective-permute-done | bytes 524320 | tf_op jit(solution)/shard_map/send_xSb/ppermute | solution.py:71
  103.4 1.6 %collective-permute-start.30 = (bf16[2,2,2,256,128]{4,3,2,1,0:T(8,128)(2,1)S(1)}, bf16[2,2,2,256,128]{4,3,2,1,0:T(8,128)(2,1)S(1)}, u32[]{:S(2)}, u32[]{:S(2)}) collective-permute-start(bf16[2,2,2,256,128]{4,3,2,1,0:T(8,128)(2,1)S(1)} %collective-permute-done.29.refs_6_), channel_id=1, source_target_pairs={{0,8},{1,9},{2,10},{3,11},{4,12},{5,13},{6,14},{7,15},{8,0},{9,1},... | collective-permute-start | bytes 1572872 | tf_op jit(solution)/shard_map/send_xSf/ppermute | solution.py:71
  106.0 3.8 %correlate.6.refs_8_ = f32[2,512,256]{2,1,0:T(8,128)S(1)} custom-call(s32[10]{0:T(128)S(1)} %stack.128.place, bf16[4,2,512,128]{3,2,1,0:T(8,128)(2,1)S(1)} %pad_maximum_fusion.refs_0_, bf16[4,2,512,128]{3,2,1,0:T(8,128)(2,1)S(1)} %collective-permute-done.5.refs_1_, bf16[4,2,512,128]{3,2,1,0:T(8,128)(2,1)S(1)} %collective-permute-done.6.refs_2_, ...), custom_call_target="tpu_custom_call" | custom-call | flops 2147483648 | bytes 6291456 | tf_op jit(solution)/shard_map/correlate/pallas_call | solution.py:241
  109.8 6.6 %collective-permute-done.20.refs_3_ = bf16[4,2,512,128]{3,2,1,0:T(8,128)(2,1)S(1)} collective-permute-done((bf16[4,2,512,128]{3,2,1,0:T(8,128)(2,1)S(1)}, bf16[4,2,512,128]{3,2,1,0:T(8,128)(2,1)S(1)}, u32[]{:S(2)}, u32[]{:S(2)}) %collective-permute-start.20) | collective-permute-done | bytes 1048608 | tf_op jit(solution)/shard_map/send_y2f/ppermute | solution.py:71
  116.4 2.6 %correlate.7 = bf16[1,512,256]{2,1,0:T(8,128)(2,1)S(1)} custom-call(s32[10]{0:T(128)S(1)} %stack.128.place, bf16[4,2,512,128]{3,2,1,0:T(8,128)(2,1)S(1)} %pad_maximum_fusion.1.refs_0_, bf16[4,2,512,128]{3,2,1,0:T(8,128)(2,1)S(1)} %collective-permute-done.18.refs_1_, bf16[4,2,512,128]{3,2,1,0:T(8,128)(2,1)S(1)} %collective-permute-done.19.refs_2_, ...), custom_call_target="tpu_custom_call" | custom-call | flops 34359738368 | bytes 6291456 | tf_op jit(solution)/shard_map/correlate/pallas_call | solution.py:241
  119.1 2.6 %correlate.8 = bf16[1,512,256]{2,1,0:T(8,128)(2,1)S(1)} custom-call(s32[10]{0:T(128)S(1)} %stack.128.place, bf16[4,2,512,128]{3,2,1,0:T(8,128)(2,1)S(1)} %pad_maximum_fusion.1.refs_0_, bf16[4,2,512,128]{3,2,1,0:T(8,128)(2,1)S(1)} %collective-permute-done.18.refs_1_, bf16[4,2,512,128]{3,2,1,0:T(8,128)(2,1)S(1)} %collective-permute-done.19.refs_2_, ...), custom_call_target="tpu_custom_call" | custom-call | flops 34359738368 | bytes 6291456 | tf_op jit(solution)/shard_map/correlate/pallas_call | solution.py:241
  121.8 1.5 %collective-permute-start.24 = (bf16[1,512,256]{2,1,0:T(8,128)(2,1)S(1)}, bf16[1,512,256]{2,1,0:T(8,128)(2,1)S(1)}, u32[]{:S(2)}, u32[]{:S(2)}) collective-permute-start(bf16[1,512,256]{2,1,0:T(8,128)(2,1)S(1)} %correlate.8), channel_id=1, source_target_pairs={{0,1},{1,0},{2,3},{3,2},{4,5},{5,4},{6,7},{7,6},{8,9},{9,8},{10,11... | collective-permute-start | bytes 786440 | tf_op jit(solution)/shard_map/ppermute | solution.py:71
  123.3 4.7 %correlate.9.whole = f32[2,2,512,256]{3,2,1,0:T(8,128)} custom-call(s32[10]{0:T(128)S(1)} %stack.128.place, bf16[4,2,512,128]{3,2,1,0:T(8,128)(2,1)S(1)} %pad_maximum_fusion.1.refs_0_, bf16[4,2,512,128]{3,2,1,0:T(8,128)(2,1)S(1)} %collective-permute-done.18.refs_1_, bf16[4,2,512,128]{3,2,1,0:T(8,128)(2,1)S(1)} %collective-permute-done.19.refs_2_, ...), custom_call_target="tpu_custom_call" | custom-call | flops 2147483648 | bytes 6291456 | tf_op jit(solution)/shard_map/correlate/pallas_call | solution.py:241
  129.2 1.4 %collective-permute-done.24.got = bf16[1,512,256]{2,1,0:T(8,128)(2,1)S(1)} collective-permute-done((bf16[1,512,256]{2,1,0:T(8,128)(2,1)S(1)}, bf16[1,512,256]{2,1,0:T(8,128)(2,1)S(1)}, u32[]{:S(2)}, u32[]{:S(2)}) %collective-permute-start.24) | collective-permute-done | bytes 262176 | tf_op jit(solution)/shard_map/ppermute | solution.py:71
  (71 shorter events, 17.1 us)
Async XLA Ops:
  2.5 17.7 %copy-start.2 = (s32[256]{0:T(256)S(1)}, s32[256]{0:T(256)}, u32[]{:S(2)}) copy-start(s32[256]{0:T(256)} %param.8) | copy-start | bytes 3076
  11.7 21.9 %collective-permute-start = (bf16[1024,128]{1,0:T(8,128)(2,1)S(1)}, bf16[1024,128]{1,0:T(8,128)(2,1)}, u32[]{:S(2)}, u32[]{:S(2)}) collective-permute-start(bf16[1024,128]{1,0:T(8,128)(2,1)S(1)} %get-tuple-element.43), channel_id=1, source_target_pairs={{0,32},{1,33},{2,34},{3,35},{4,36},{5,37},{6,38},{7,39},{8,40},{9,... | collective-permute-start | bytes 786440 | tf_op jit(solution)/shard_map/send_Acc/ppermute | solution.py:71
  13.1 16.4 %collective-permute-start.1 = (bf16[1024,128]{1,0:T(8,128)(2,1)}, bf16[1024,128]{1,0:T(8,128)(2,1)}, u32[]{:S(2)}, u32[]{:S(2)}) collective-permute-start(bf16[1024,128]{1,0:T(8,128)(2,1)} %get-tuple-element.44), channel_id=1, source_target_pairs={{0,1},{1,0},{2,3},{3,2},{4,5},{5,4},{6,7},{7,6},{8,9},{9,8},{10,11... | collective-permute-start | bytes 786440 | tf_op jit(solution)/shard_map/send_Aza/ppermute | solution.py:71
  16.9 12.7 %collective-permute-start.2 = (bf16[1024,128]{1,0:T(8,128)(2,1)}, bf16[1024,128]{1,0:T(8,128)(2,1)}, u32[]{:S(2)}, u32[]{:S(2)}) collective-permute-start(bf16[1024,128]{1,0:T(8,128)(2,1)} %get-tuple-element.45), channel_id=1, source_target_pairs={{0,97},{1,96},{2,99},{3,98},{4,101},{5,100},{6,103},{7,102},{8,105... | collective-permute-start | bytes 786440 | tf_op jit(solution)/shard_map/send_Azbc/ppermute | solution.py:71
  16.9 15.3 %collective-permute-start.3 = (bf16[1024,128]{1,0:T(8,128)(2,1)S(1)}, bf16[1024,128]{1,0:T(8,128)(2,1)}, u32[]{:S(2)}, u32[]{:S(2)}) collective-permute-start(bf16[1024,128]{1,0:T(8,128)(2,1)S(1)} %get-tuple-element.46), channel_id=1, source_target_pairs={{0,65},{1,64},{2,67},{3,66},{4,69},{5,68},{6,71},{7,70},{8,73},{9,... | collective-permute-start | bytes 786440 | tf_op jit(solution)/shard_map/send_Azb/ppermute | solution.py:71
  16.9 15.3 %collective-permute-start.4 = (bf16[1024,128]{1,0:T(8,128)(2,1)S(1)}, bf16[1024,128]{1,0:T(8,128)(2,1)}, u32[]{:S(2)}, u32[]{:S(2)}) collective-permute-start(bf16[1024,128]{1,0:T(8,128)(2,1)S(1)} %get-tuple-element.47), channel_id=1, source_target_pairs={{0,33},{1,32},{2,35},{3,34},{4,37},{5,36},{6,39},{7,38},{8,41},{9,... | collective-permute-start | bytes 786440 | tf_op jit(solution)/shard_map/send_Azac/ppermute | solution.py:71
  29.5 8.4 %collective-permute-start.8 = (bf16[1024,128]{1,0:T(8,128)(2,1)S(1)}, bf16[1024,128]{1,0:T(8,128)(2,1)S(1)}, u32[]{:S(2)}, u32[]{:S(2)}) collective-permute-start(bf16[1024,128]{1,0:T(8,128)(2,1)S(1)} %get-tuple-element.51), channel_id=1, source_target_pairs={{0,32},{1,33},{2,34},{3,35},{4,36},{5,37},{6,38},{7,39},{8,40},{9,... | collective-permute-start | bytes 786440 | tf_op jit(solution)/shard_map/send_Bcc/ppermute | solution.py:71
  29.6 8.3 %collective-permute-start.12 = (bf16[1024,128]{1,0:T(8,128)(2,1)}, bf16[1024,128]{1,0:T(8,128)(2,1)S(1)}, u32[]{:S(2)}, u32[]{:S(2)}) collective-permute-start(bf16[1024,128]{1,0:T(8,128)(2,1)} %copy-done.1), channel_id=1, source_target_pairs={{0,1},{1,0},{2,3},{3,2},{4,5},{5,4},{6,7},{7,6},{8,9},{9,8},{10,11... | collective-permute-start | bytes 786440 | tf_op jit(solution)/shard_map/send_Bza/ppermute | solution.py:71
  34.6 24.7 %collective-permute-start.6 = (bf16[4,2,512,128]{3,2,1,0:T(8,128)(2,1)S(1)}, bf16[4,2,512,128]{3,2,1,0:T(8,128)(2,1)S(1)}, u32[]{:S(2)}, u32[]{:S(2)}) collective-permute-start(bf16[4,2,512,128]{3,2,1,0:T(8,128)(2,1)S(1)} %pad_maximum_fusion.refs_0_), channel_id=1, source_target_pairs={{0,6},{1,7},{2,4},{3,5},{4,2},{5,3},{6,0},{7,1},{8,14},{9,15},{10,... | collective-permute-start | bytes 3145736 | tf_op jit(solution)/shard_map/send_y1b/ppermute | solution.py:71
  36.0 7.3 %collective-permute-start.15 = (bf16[1024,128]{1,0:T(8,128)(2,1)S(1)}, bf16[1024,128]{1,0:T(8,128)(2,1)S(1)}, u32[]{:S(2)}, u32[]{:S(2)}) collective-permute-start(bf16[1024,128]{1,0:T(8,128)(2,1)S(1)} %get-tuple-element.61), channel_id=1, source_target_pairs={{0,97},{1,96},{2,99},{3,98},{4,101},{5,100},{6,103},{7,102},{8,105... | collective-permute-start | bytes 786440 | tf_op jit(solution)/shard_map/send_Bzbc/ppermute | solution.py:71
  37.1 30.0 %collective-permute-start.5 = (bf16[4,2,512,128]{3,2,1,0:T(8,128)(2,1)S(1)}, bf16[4,2,512,128]{3,2,1,0:T(8,128)(2,1)S(1)}, u32[]{:S(2)}, u32[]{:S(2)}) collective-permute-start(bf16[4,2,512,128]{3,2,1,0:T(8,128)(2,1)S(1)} %pad_maximum_fusion.refs_0_), channel_id=1, source_target_pairs={{0,2},{1,3},{2,0},{3,1},{4,6},{5,7},{6,4},{7,5},{8,10},{9,11},{10,... | collective-permute-start | bytes 3145736 | tf_op jit(solution)/shard_map/send_y1a/ppermute | solution.py:71
  37.9 7.9 %collective-permute-start.13 = (bf16[1024,128]{1,0:T(8,128)(2,1)S(1)}, bf16[1024,128]{1,0:T(8,128)(2,1)S(1)}, u32[]{:S(2)}, u32[]{:S(2)}) collective-permute-start(bf16[1024,128]{1,0:T(8,128)(2,1)S(1)} %get-tuple-element.57), channel_id=1, source_target_pairs={{0,65},{1,64},{2,67},{3,66},{4,69},{5,68},{6,71},{7,70},{8,73},{9,... | collective-permute-start | bytes 786440 | tf_op jit(solution)/shard_map/send_Bzb/ppermute | solution.py:71
  38.0 15.9 %collective-permute-start.10 = (bf16[2,2,2,256,128]{4,3,2,1,0:T(8,128)(2,1)S(1)}, bf16[2,2,2,256,128]{4,3,2,1,0:T(8,128)(2,1)S(1)}, u32[]{:S(2)}, u32[]{:S(2)}) collective-permute-start(bf16[2,2,2,256,128]{4,3,2,1,0:T(8,128)(2,1)S(1)} %pad_maximum_fusion.5.refs_4_), channel_id=1, source_target_pairs={{0,24},{1,25},{2,26},{3,27},{4,28},{5,29},{6,30},{7,31},{8,16},{9,... | collective-permute-start | bytes 1572872 | tf_op jit(solution)/shard_map/send_xPb/ppermute | solution.py:71
  43.3 13.4 %collective-permute-start.9 = (bf16[2,2,2,256,128]{4,3,2,1,0:T(8,128)(2,1)S(1)}, bf16[2,2,2,256,128]{4,3,2,1,0:T(8,128)(2,1)S(1)}, u32[]{:S(2)}, u32[]{:S(2)}) collective-permute-start(bf16[2,2,2,256,128]{4,3,2,1,0:T(8,128)(2,1)S(1)} %pad_maximum_fusion.5.refs_4_), channel_id=1, source_target_pairs={{0,8},{1,9},{2,10},{3,11},{4,12},{5,13},{6,14},{7,15},{8,0},{9,1},... | collective-permute-start | bytes 1572872 | tf_op jit(solution)/shard_map/send_xPa/ppermute | solution.py:71
  45.8 6.1 %collective-permute-start.16 = (bf16[1024,128]{1,0:T(8,128)(2,1)S(1)}, bf16[1024,128]{1,0:T(8,128)(2,1)S(1)}, u32[]{:S(2)}, u32[]{:S(2)}) collective-permute-start(bf16[1024,128]{1,0:T(8,128)(2,1)S(1)} %get-tuple-element.62), channel_id=1, source_target_pairs={{0,33},{1,32},{2,35},{3,34},{4,37},{5,36},{6,39},{7,38},{8,41},{9,... | collective-permute-start | bytes 786440 | tf_op jit(solution)/shard_map/send_Bzac/ppermute | solution.py:71
  51.9 8.2 %collective-permute-start.14 = (bf16[1024,128]{1,0:T(8,128)(2,1)S(1)}, bf16[1024,128]{1,0:T(8,128)(2,1)S(1)}, u32[]{:S(2)}, u32[]{:S(2)}) collective-permute-start(bf16[1024,128]{1,0:T(8,128)(2,1)S(1)} %get-tuple-element.58), channel_id=1, source_target_pairs={{0,64},{1,65},{2,66},{3,67},{4,68},{5,69},{6,70},{7,71},{8,72},{9,... | collective-permute-start | bytes 786440 | tf_op jit(solution)/shard_map/send_Az2/ppermute | solution.py:71
  53.9 13.1 %collective-permute-start.17 = (bf16[1024,128]{1,0:T(8,128)(2,1)S(1)}, bf16[1024,128]{1,0:T(8,128)(2,1)S(1)}, u32[]{:S(2)}, u32[]{:S(2)}) collective-permute-start(bf16[1024,128]{1,0:T(8,128)(2,1)S(1)} %get-tuple-element.63), channel_id=1, source_target_pairs={{0,96},{1,97},{2,98},{3,99},{4,100},{5,101},{6,102},{7,103},{8,104... | collective-permute-start | bytes 786440 | tf_op jit(solution)/shard_map/send_Az2c/ppermute | solution.py:71
  56.6 13.5 %collective-permute-start.11 = (bf16[2,2,2,256,128]{4,3,2,1,0:T(8,128)(2,1)S(1)}, bf16[2,2,2,256,128]{4,3,2,1,0:T(8,128)(2,1)S(1)}, u32[]{:S(2)}, u32[]{:S(2)}) collective-permute-start(bf16[2,2,2,256,128]{4,3,2,1,0:T(8,128)(2,1)S(1)} %collective-permute-done.10.refs_6_), channel_id=1, source_target_pairs={{0,8},{1,9},{2,10},{3,11},{4,12},{5,13},{6,14},{7,15},{8,0},{9,1},... | collective-permute-start | bytes 1572872 | tf_op jit(solution)/shard_map/send_xPf/ppermute | solution.py:71
  59.3 19.8 %collective-permute-start.22 = (bf16[4,2,2,256,128]{4,3,2,1,0:T(8,128)(2,1)S(1)}, bf16[4,2,2,256,128]{4,3,2,1,0:T(8,128)(2,1)S(1)}, u32[]{:S(2)}, u32[]{:S(2)}) collective-permute-start(bf16[4,2,2,256,128]{4,3,2,1,0:T(8,128)(2,1)S(1)} %pad_maximum_fusion.2.refs_4_), channel_id=1, source_target_pairs={{0,24},{1,25},{2,26},{3,27},{4,28},{5,29},{6,30},{7,31},{8,16},{9,... | collective-permute-start | bytes 3145736 | tf_op jit(solution)/shard_map/send_xQb/ppermute | solution.py:71
  60.0 20.1 %collective-permute-start.7 = (bf16[4,2,512,128]{3,2,1,0:T(8,128)(2,1)S(1)}, bf16[4,2,512,128]{3,2,1,0:T(8,128)(2,1)S(1)}, u32[]{:S(2)}, u32[]{:S(2)}) collective-permute-start(bf16[4,2,512,128]{3,2,1,0:T(8,128)(2,1)S(1)} %collective-permute-done.6.refs_2_), channel_id=1, source_target_pairs={{0,2},{1,3},{2,0},{3,1},{4,6},{5,7},{6,4},{7,5},{8,10},{9,11},{10,... | collective-permute-start | bytes 3145736 | tf_op jit(solution)/shard_map/send_y1f/ppermute | solution.py:71
  67.1 22.8 %collective-permute-start.19 = (bf16[4,2,512,128]{3,2,1,0:T(8,128)(2,1)S(1)}, bf16[4,2,512,128]{3,2,1,0:T(8,128)(2,1)S(1)}, u32[]{:S(2)}, u32[]{:S(2)}) collective-permute-start(bf16[4,2,512,128]{3,2,1,0:T(8,128)(2,1)S(1)} %pad_maximum_fusion.1.refs_0_), channel_id=1, source_target_pairs={{0,6},{1,7},{2,4},{3,5},{4,2},{5,3},{6,0},{7,1},{8,14},{9,15},{10,... | collective-permute-start | bytes 3145736 | tf_op jit(solution)/shard_map/send_y2b/ppermute | solution.py:71
  70.1 24.0 %collective-permute-start.21 = (bf16[4,2,2,256,128]{4,3,2,1,0:T(8,128)(2,1)S(1)}, bf16[4,2,2,256,128]{4,3,2,1,0:T(8,128)(2,1)S(1)}, u32[]{:S(2)}, u32[]{:S(2)}) collective-permute-start(bf16[4,2,2,256,128]{4,3,2,1,0:T(8,128)(2,1)S(1)} %pad_maximum_fusion.2.refs_4_), channel_id=1, source_target_pairs={{0,8},{1,9},{2,10},{3,11},{4,12},{5,13},{6,14},{7,15},{8,0},{9,1},... | collective-permute-start | bytes 3145736 | tf_op jit(solution)/shard_map/send_xQa/ppermute | solution.py:71
  72.6 20.4 %collective-permute-start.26 = (bf16[1024,128]{1,0:T(8,128)(2,1)S(1)}, bf16[1024,128]{1,0:T(8,128)(2,1)S(1)}, u32[]{:S(2)}, u32[]{:S(2)}) collective-permute-start(bf16[1024,128]{1,0:T(8,128)(2,1)S(1)} %get-tuple-element.73), channel_id=1, source_target_pairs={{0,64},{1,65},{2,66},{3,67},{4,68},{5,69},{6,70},{7,71},{8,72},{9,... | collective-permute-start | bytes 786440 | tf_op jit(solution)/shard_map/send_Bz2/ppermute | solution.py:71
  79.1 25.8 %collective-permute-start.23 = (bf16[4,2,2,256,128]{4,3,2,1,0:T(8,128)(2,1)S(1)}, bf16[4,2,2,256,128]{4,3,2,1,0:T(8,128)(2,1)S(1)}, u32[]{:S(2)}, u32[]{:S(2)}) collective-permute-start(bf16[4,2,2,256,128]{4,3,2,1,0:T(8,128)(2,1)S(1)} %collective-permute-done.22.refs_6_), channel_id=1, source_target_pairs={{0,8},{1,9},{2,10},{3,11},{4,12},{5,13},{6,14},{7,15},{8,0},{9,1},... | collective-permute-start | bytes 3145736 | tf_op jit(solution)/shard_map/send_xQf/ppermute | solution.py:71
  80.1 13.9 %collective-permute-start.27 = (bf16[1024,128]{1,0:T(8,128)(2,1)S(1)}, bf16[1024,128]{1,0:T(8,128)(2,1)S(1)}, u32[]{:S(2)}, u32[]{:S(2)}) collective-permute-start(bf16[1024,128]{1,0:T(8,128)(2,1)S(1)} %get-tuple-element.75), channel_id=1, source_target_pairs={{0,96},{1,97},{2,98},{3,99},{4,100},{5,101},{6,102},{7,103},{8,104... | collective-permute-start | bytes 786440 | tf_op jit(solution)/shard_map/send_Bz2c/ppermute | solution.py:71
  89.9 19.9 %collective-permute-start.18 = (bf16[4,2,512,128]{3,2,1,0:T(8,128)(2,1)S(1)}, bf16[4,2,512,128]{3,2,1,0:T(8,128)(2,1)S(1)}, u32[]{:S(2)}, u32[]{:S(2)}) collective-permute-start(bf16[4,2,512,128]{3,2,1,0:T(8,128)(2,1)S(1)} %pad_maximum_fusion.1.refs_0_), channel_id=1, source_target_pairs={{0,2},{1,3},{2,0},{3,1},{4,6},{5,7},{6,4},{7,5},{8,10},{9,11},{10,... | collective-permute-start | bytes 3145736 | tf_op jit(solution)/shard_map/send_y2a/ppermute | solution.py:71
  93.0 23.4 %collective-permute-start.20 = (bf16[4,2,512,128]{3,2,1,0:T(8,128)(2,1)S(1)}, bf16[4,2,512,128]{3,2,1,0:T(8,128)(2,1)S(1)}, u32[]{:S(2)}, u32[]{:S(2)}) collective-permute-start(bf16[4,2,512,128]{3,2,1,0:T(8,128)(2,1)S(1)} %collective-permute-done.19.refs_2_), channel_id=1, source_target_pairs={{0,2},{1,3},{2,0},{3,1},{4,6},{5,7},{6,4},{7,5},{8,10},{9,11},{10,... | collective-permute-start | bytes 3145736 | tf_op jit(solution)/shard_map/send_y2f/ppermute | solution.py:71
  94.1 9.3 %collective-permute-start.29 = (bf16[2,2,2,256,128]{4,3,2,1,0:T(8,128)(2,1)S(1)}, bf16[2,2,2,256,128]{4,3,2,1,0:T(8,128)(2,1)S(1)}, u32[]{:S(2)}, u32[]{:S(2)}) collective-permute-start(bf16[2,2,2,256,128]{4,3,2,1,0:T(8,128)(2,1)S(1)} %pad_maximum_fusion.6.refs_4_), channel_id=1, source_target_pairs={{0,24},{1,25},{2,26},{3,27},{4,28},{5,29},{6,30},{7,31},{8,16},{9,... | collective-permute-start | bytes 1572872 | tf_op jit(solution)/shard_map/send_xSb/ppermute | solution.py:71
  103.4 19.9 %collective-permute-start.30 = (bf16[2,2,2,256,128]{4,3,2,1,0:T(8,128)(2,1)S(1)}, bf16[2,2,2,256,128]{4,3,2,1,0:T(8,128)(2,1)S(1)}, u32[]{:S(2)}, u32[]{:S(2)}) collective-permute-start(bf16[2,2,2,256,128]{4,3,2,1,0:T(8,128)(2,1)S(1)} %collective-permute-done.29.refs_6_), channel_id=1, source_target_pairs={{0,8},{1,9},{2,10},{3,11},{4,12},{5,13},{6,14},{7,15},{8,0},{9,1},... | collective-permute-start | bytes 1572872 | tf_op jit(solution)/shard_map/send_xSf/ppermute | solution.py:71
  104.9 18.4 %collective-permute-start.28 = (bf16[2,2,2,256,128]{4,3,2,1,0:T(8,128)(2,1)S(1)}, bf16[2,2,2,256,128]{4,3,2,1,0:T(8,128)(2,1)S(1)}, u32[]{:S(2)}, u32[]{:S(2)}) collective-permute-start(bf16[2,2,2,256,128]{4,3,2,1,0:T(8,128)(2,1)S(1)} %pad_maximum_fusion.6.refs_4_), channel_id=1, source_target_pairs={{0,8},{1,9},{2,10},{3,11},{4,12},{5,13},{6,14},{7,15},{8,0},{9,1},... | collective-permute-start | bytes 1572872 | tf_op jit(solution)/shard_map/send_xSa/ppermute | solution.py:71
  119.0 9.0 %collective-permute-start.25 = (bf16[1,512,256]{2,1,0:T(8,128)(2,1)S(1)}, bf16[1,512,256]{2,1,0:T(8,128)(2,1)S(1)}, u32[]{:S(2)}, u32[]{:S(2)}) collective-permute-start(bf16[1,512,256]{2,1,0:T(8,128)(2,1)S(1)} %correlate.7), channel_id=1, source_target_pairs={{0,1},{1,0},{2,3},{3,2},{4,5},{5,4},{6,7},{7,6},{8,9},{9,8},{10,11... | collective-permute-start | bytes 786440 | tf_op jit(solution)/shard_map/ppermute | solution.py:71
  121.8 8.8 %collective-permute-start.24 = (bf16[1,512,256]{2,1,0:T(8,128)(2,1)S(1)}, bf16[1,512,256]{2,1,0:T(8,128)(2,1)S(1)}, u32[]{:S(2)}, u32[]{:S(2)}) collective-permute-start(bf16[1,512,256]{2,1,0:T(8,128)(2,1)S(1)} %correlate.8), channel_id=1, source_target_pairs={{0,1},{1,0},{2,3},{3,2},{4,5},{5,4},{6,7},{7,6},{8,9},{9,8},{10,11... | collective-permute-start | bytes 786440 | tf_op jit(solution)/shard_map/ppermute | solution.py:71
  (2 other events, 4.1 us)
